TPU v7x, 32 devices: a whole 2x2x4 slice. The times are simulated.
32 devices in a mesh: seq: 8 (over z, x), kv: 4 (over y, core).
Axes of the slice: x: 2, y: 2, z: 4, core: 2. Of those that a mesh axis runs over, the one named last changes fastest.
Arguments:
- tokens: bfloat16 [1, 4096, 2048], P(None, 'seq'), may hold values from -6 to 6
- attention_norm_gain: bfloat16 [2048], P('seq'), may hold values from 0.5 to 1.5
- query_weight: bfloat16 [2048, 2048], P('seq', 'kv'), may hold values from -0.125 to 0.125
- key_value_weight: bfloat16 [2, 2048, 512], P(None, 'seq', 'kv'), may hold values from -0.125 to 0.125
- output_weight: bfloat16 [2048, 2048], P(('kv', 'seq')), may hold values from -0.5 to 0.5
- adapter_down_matrices: bfloat16 [3, 2048, 8], P(None, 'seq'), may hold values from -0.125 to 0.125
- adapter_query_up: bfloat16 [8, 2048], P(None, ('kv', 'seq')), may hold values from -2 to 2
- adapter_key_value_up: bfloat16 [2, 8, 512], P(None, None, ('kv', 'seq')), may hold values from -2 to 2
- adapter_output_down: bfloat16 [2048, 8], P(('kv', 'seq')), may hold values from -0.5 to 0.5
- adapter_output_up: bfloat16 [8, 2048], P(None, 'seq'), may hold values from -2 to 2
- query_feature_matrix: bfloat16 [32, 64, 64], P('kv', 'seq'), may hold values from -1 to 1
- key_feature_matrix: bfloat16 [8, 64, 64], P('kv', 'seq'), may hold values from -1 to 1
- feedforward_norm_gain: bfloat16 [2048], P('seq'), may hold values from 0.5 to 1.5
- gate_weight: bfloat16 [2048, 8192], P('seq', 'kv'), may hold values from -0.125 to 0.125
- up_weight: bfloat16 [2048, 8192], P('seq', 'kv'), may hold values from -0.125 to 0.125
- down_weight: bfloat16 [8192, 2048], P(('kv', 'seq')), may hold values from -0.0625 to 0.0625
- cotangent: bfloat16 [1, 4096, 2048], P(None, 'seq'), may hold values from -6 to 6
Outputs:
- activations: bfloat16 [1, 4096, 2048], P(None, 'seq')
- grad_tokens: float32 [1, 4096, 2048], P(None, 'seq')
- grad_g_attn: float32 [2048], P('seq')
- grad_w_query: float32 [2048, 2048], P('seq', 'kv')
- grad_w_kv: float32 [2, 2048, 512], P(None, 'seq', 'kv')
- grad_w_out: float32 [2048, 2048], P(('kv', 'seq'))
- grad_lora_down: float32 [3, 2048, 8], P(None, 'seq')
- grad_lora_up_query: float32 [8, 2048], P(None, ('kv', 'seq'))
- grad_lora_up_kv: float32 [2, 8, 512], P(None, None, ('kv', 'seq'))
- grad_lora_down_out: float32 [2048, 8], P(('kv', 'seq'))
- grad_lora_up_out: float32 [8, 2048], P(None, 'seq')
- grad_fmap_query: float32 [32, 64, 64], P('kv', 'seq')
- grad_fmap_key: float32 [8, 64, 64], P('kv', 'seq')
- grad_g_mlp: float32 [2048], P('seq')
- grad_w_gate: float32 [2048, 8192], P('seq', 'kv')
- grad_w_up: float32 [2048, 8192], P('seq', 'kv')
- grad_w_down: float32 [8192, 2048], P(('kv', 'seq'))
All inputs are finite; a program needn't handle non-finite values.
Results may differ from a plain program's by a relative error of at most 0.024.
Values may be sent and summed in bfloat16 or wider, within the bound.
No kernel may reach another device: no remote copies, remote signals or barrier semaphores. Data moves between devices by JAX's collectives and lax.ppermute only.
A program may use at most 256 MiB of HBM per device.

v0:
```python
import jax
import jax.numpy as jnp
from jax import lax
from jax.sharding import PartitionSpec as P

WIN = 64


epsilon = 1e-05


def from_behind(array, axis, by):
    length = lax.axis_size(axis)
    pairs = [(i, i + by) for i in range(length) if 0 <= i + by < length]
    return lax.ppermute(array, axis, pairs)


def prefix(part, axis, combine, identity):
    place = lax.axis_index(axis)
    gathered = jax.tree.map(lambda a: lax.all_gather(a, axis), part)
    state = jax.tree.map(lambda a, e: jnp.zeros_like(a) + jnp.asarray(e, a.dtype), part, identity)

    def one(hop, state):
        return combine(
            state, jax.tree.map(lambda a: lax.dynamic_index_in_dim(a, hop, 0, False), gathered)
        )

    return lax.fori_loop(0, place, one, state)


def prefix_2(array, axis, join, neutral):
    count = lax.axis_size(axis)
    place = lax.axis_index(axis)
    ahead = count - 1 - place
    gathered = jax.tree.map(
        lambda a, kind: lax.all_gather(a.astype(kind), axis),
        array,
        jax.tree.map(lambda a: jnp.bfloat16 if a.dtype == jnp.float32 else a.dtype, array),
    )
    state = jax.tree.map(lambda a, e: jnp.zeros_like(a) + jnp.asarray(e, a.dtype), array, neutral)

    def one(hop, state):
        source = count - 1 - hop
        return join(
            state,
            jax.tree.map(
                lambda a, own: lax.dynamic_index_in_dim(a, source, 0, False).astype(own.dtype),
                gathered,
                array,
            ),
        )

    return lax.fori_loop(0, ahead, one, state)


def spread_features(mixing):
    return jnp.concatenate([jax.nn.softmax(mixing, -1), jax.nn.softmax(-mixing, -1)], -1)


def feature_map(input_tokens, fmap):
    mixing = jnp.einsum("...hd,hde->...he", input_tokens, fmap, preferred_element_type=jnp.float32)
    return (mixing, spread_features(mixing).astype(jnp.bfloat16))


def feature_back(input_tokens, fmap, mixing, grad_feat):
    grad_low = lax.optimization_barrier(grad_feat.astype(jnp.bfloat16)).astype(jnp.float32)
    unused, pull = jax.vjp(spread_features, mixing)
    grad_mix = pull(grad_low)[0].astype(jnp.bfloat16)
    head_count, head_size = (fmap.shape[0], fmap.shape[1])
    grad_inputs = jnp.einsum("...he,hde->...hd", grad_mix, fmap, preferred_element_type=jnp.float32)
    flat_inputs = input_tokens.reshape(-1, head_count, head_size)
    flat_grad = grad_mix.reshape(-1, head_count, head_size)
    grad_fmap = jnp.einsum(
        "nhd,nhe->hde", flat_inputs, flat_grad, preferred_element_type=jnp.float32
    )
    return (grad_inputs, grad_fmap)


def norm_back(values, scale, gain, grad):
    scaled_grad = grad * gain.astype(jnp.float32)
    gain_grad = jnp.sum(grad * values * scale, 0)
    grad_values = scale * scaled_grad - values * scale * scale * scale * jnp.mean(
        scaled_grad * values, -1, keepdims=True
    )
    return (gain_grad, grad_values)


def add_pair(earlier, later):
    return (earlier[0] + later[0], earlier[1] + later[1])


def window_masks(block_len, width, is_valid):
    row_ids = jnp.arange(block_len)[:, None]
    col_ids = jnp.arange(block_len + width)[None, :]
    in_window = (col_ids > row_ids) & (col_ids <= row_ids + width) & is_valid[None, :]
    is_early = col_ids[:, :block_len] <= row_ids
    return (in_window, is_early)


def attention_weights(query_s, feat_s, key_s, kfeat_s, in_window, is_early):
    score_scale = query_s.shape[-1] ** (-0.5)
    scores = (
        jnp.einsum("ikgd,jkd->kgij", query_s, key_s, preferred_element_type=jnp.float32)
        * score_scale
    )
    window = jnp.where(in_window, jnp.exp(scores), 0.0)
    linear = jnp.einsum("ikgf,jkf->kgij", feat_s, kfeat_s, preferred_element_type=jnp.float32)
    earlier = jnp.where(is_early, linear, 0.0)
    return (window, earlier)


def combine_values(window, earlier, value_s, feat_s, state_s):
    block_len = earlier.shape[-1]
    numerator = jnp.einsum(
        "kgij,jkd->ikgd", window.astype(jnp.bfloat16), value_s, preferred_element_type=jnp.float32
    )
    numerator = numerator + jnp.einsum(
        "kgij,jkd->ikgd",
        earlier.astype(jnp.bfloat16),
        value_s[:block_len],
        preferred_element_type=jnp.float32,
    )
    return numerator + jnp.einsum(
        "ikgf,kfd->ikgd", feat_s, state_s.astype(jnp.bfloat16), preferred_element_type=jnp.float32
    )


def row_totals(window, earlier, feat_s, norm_s):
    totals = jnp.transpose(jnp.sum(window, -1) + jnp.sum(earlier, -1), (2, 0, 1))
    return totals + jnp.sum(feat_s.astype(jnp.float32) * norm_s[None, :, None, :], -1)


def attention_back(
    query_s, feat_s, key_s, value_s, kfeat_s, state_s, norm_s, denom_s, grad_s, in_window, is_early
):
    block_len = kfeat_s.shape[0]
    score_scale = query_s.shape[-1] ** (-0.5)
    window, earlier = attention_weights(query_s, feat_s, key_s, kfeat_s, in_window, is_early)
    numerator = combine_values(window, earlier, value_s, feat_s, state_s)
    grad_num = (grad_s / denom_s[..., None]).astype(jnp.bfloat16)
    grad_den = -jnp.sum(grad_s * numerator, -1) / (denom_s * denom_s)
    from_values = jnp.einsum(
        "ikgd,jkd->kgij", grad_num, value_s, preferred_element_type=jnp.float32
    )
    den_cols = jnp.transpose(grad_den, (1, 2, 0))[..., None]
    grad_window = ((from_values + den_cols) * window).astype(jnp.bfloat16)
    grad_early = jnp.where(is_early, from_values[..., :block_len] + den_cols, 0.0).astype(
        jnp.bfloat16
    )
    grad_query = (
        jnp.einsum("kgij,jkd->ikgd", grad_window, key_s, preferred_element_type=jnp.float32)
        * score_scale
    )
    grad_keys = (
        jnp.einsum("kgij,ikgd->jkd", grad_window, query_s, preferred_element_type=jnp.float32)
        * score_scale
    )
    grad_qfeat = jnp.einsum(
        "kgij,jkf->ikgf", grad_early, kfeat_s, preferred_element_type=jnp.float32
    )
    grad_qfeat = grad_qfeat + jnp.einsum(
        "ikgd,kfd->ikgf", grad_num, state_s.astype(jnp.bfloat16), preferred_element_type=jnp.float32
    )
    grad_qfeat = grad_qfeat + grad_den[..., None] * norm_s[None, :, None, :]
    grad_kfeat = jnp.einsum(
        "kgij,ikgf->jkf", grad_early, feat_s, preferred_element_type=jnp.float32
    )
    from_early = jnp.einsum(
        "kgij,ikgd->jkd", earlier.astype(jnp.bfloat16), grad_num, preferred_element_type=jnp.float32
    )
    grad_values = jnp.einsum(
        "kgij,ikgd->jkd", window.astype(jnp.bfloat16), grad_num, preferred_element_type=jnp.float32
    )
    grad_values = grad_values + jnp.pad(
        from_early, ((0, grad_values.shape[0] - block_len), (0, 0), (0, 0))
    )
    grad_state = jnp.einsum("ikgf,ikgd->kfd", feat_s, grad_num, preferred_element_type=jnp.float32)
    grad_norm = jnp.sum(feat_s.astype(jnp.float32) * grad_den[..., None], (0, 2))
    return (grad_query, grad_qfeat, grad_keys, grad_values, grad_kfeat, grad_state, grad_norm)


def per_device(
    tokens,
    attention_norm_gain,
    query_weight,
    key_value_weight,
    output_weight,
    adapter_down_matrices,
    adapter_query_up,
    adapter_key_value_up,
    adapter_output_down,
    adapter_output_up,
    query_feature_matrix,
    key_feature_matrix,
    feedforward_norm_gain,
    gate_weight,
    up_weight,
    down_weight,
    cotangent,
):
    attn_full = (
        lax.all_gather(attention_norm_gain, "seq", axis=0, tiled=True),
        lax.all_gather(query_weight, "seq", axis=0, tiled=True),
        lax.all_gather(key_value_weight, "seq", axis=1, tiled=True),
        lax.all_gather(output_weight, "seq", axis=0, tiled=True),
        lax.all_gather(adapter_down_matrices, "seq", axis=1, tiled=True),
        lax.all_gather(adapter_query_up, "seq", axis=1, tiled=True),
        lax.all_gather(adapter_key_value_up, "seq", axis=2, tiled=True),
        lax.all_gather(adapter_output_down, "seq", axis=0, tiled=True),
        lax.all_gather(adapter_output_up, "seq", axis=1, tiled=True),
        lax.all_gather(query_feature_matrix, "seq", axis=1, tiled=True),
        lax.all_gather(key_feature_matrix, "seq", axis=1, tiled=True),
    )
    mlp_full = (
        lax.all_gather(feedforward_norm_gain, "seq", axis=0, tiled=True),
        lax.all_gather(gate_weight, "seq", axis=0, tiled=True),
        lax.all_gather(up_weight, "seq", axis=0, tiled=True),
        lax.all_gather(down_weight, "seq", axis=0, tiled=True),
    )
    (
        gain_one,
        query_w,
        kv_w,
        out_w,
        adapter_down_weight,
        query_up_weight,
        key_value_up_weight,
        output_down_weight,
        output_up_weight,
        fq_w,
        fk_w,
    ) = attn_full
    gain_two, gate_w, up_w, down_proj = mlp_full
    sequences, block_len, width = tokens.shape
    total_rows = sequences * block_len
    heads_local = fq_w.shape[0]
    kv_local = fk_w.shape[0]
    head_size = fq_w.shape[2]
    group_size = heads_local // kv_local
    residual_stream = tokens.reshape(total_rows, width).astype(jnp.float32)
    scale_one = lax.rsqrt(jnp.mean(residual_stream * residual_stream, -1, keepdims=True) + epsilon)
    normalized_input = (residual_stream * scale_one * gain_one.astype(jnp.float32)).astype(
        jnp.bfloat16
    )
    adapter_token_rows = jnp.einsum(
        "td,cdr->ctr", normalized_input, adapter_down_weight, preferred_element_type=jnp.float32
    ).astype(jnp.bfloat16)
    query_rows = (
        jnp.dot(normalized_input, query_w, preferred_element_type=jnp.float32)
        + jnp.dot(adapter_token_rows[0], query_up_weight, preferred_element_type=jnp.float32)
    ).astype(jnp.bfloat16)
    key_value_rows = jnp.einsum(
        "td,cde->cte", normalized_input, kv_w, preferred_element_type=jnp.float32
    )
    key_value_rows = (
        key_value_rows
        + jnp.einsum(
            "usf,ufb->usb",
            adapter_token_rows[1:],
            key_value_up_weight,
            preferred_element_type=jnp.float32,
        )
    ).astype(jnp.bfloat16)
    kv_seq = key_value_rows.reshape(2, sequences, block_len, kv_local * head_size)
    arrived = from_behind(kv_seq[:, :, block_len - WIN :], "seq", 1)
    kv_ext = jnp.concatenate([arrived, kv_seq], 2).reshape(
        2, sequences, block_len + WIN, kv_local, head_size
    )
    key_ext = kv_ext[0]
    value_ext = kv_ext[1]
    offset = lax.axis_index("seq") * block_len
    is_valid = offset - WIN + jnp.arange(block_len + WIN) >= 0
    in_window, is_early = window_masks(block_len, WIN, is_valid)
    key_mask = is_valid[:block_len][None, :, None, None]
    query_heads = query_rows.reshape(sequences, block_len, heads_local, head_size)
    query_mix, query_feat = feature_map(query_heads, fq_w)
    key_mix, key_feat = feature_map(key_ext[:, :block_len], fk_w)
    key_feat = jnp.where(key_mask, key_feat, jnp.zeros_like(key_feat))
    value_head = value_ext[:, :block_len]
    totals = jnp.einsum("sjkf,sjkd->skfd", key_feat, value_head, preferred_element_type=jnp.float32)
    feat_sums = jnp.sum(key_feat.astype(jnp.float32), 1)
    states, norms = prefix(
        (totals, feat_sums), "seq", add_pair, (jnp.zeros_like(totals), jnp.zeros_like(feat_sums))
    )
    query_groups = query_heads.reshape(sequences, block_len, kv_local, group_size, head_size)
    feat_groups = query_feat.reshape(sequences, block_len, kv_local, group_size, 2 * head_size)

    def forward_one(items):
        query_s, feat_s, key_s, value_s, kfeat_s, state_s, norm_s = items
        window, earlier = attention_weights(query_s, feat_s, key_s, kfeat_s, in_window, is_early)
        numerator = combine_values(window, earlier, value_s, feat_s, state_s)
        denominator = row_totals(window, earlier, feat_s, norm_s)
        return ((numerator / denominator[..., None]).astype(jnp.bfloat16), denominator)

    attended_output, denominators = lax.map(
        forward_one, (query_groups, feat_groups, key_ext, value_ext, key_feat, states, norms)
    )
    attended_token_rows = attended_output.reshape(total_rows, heads_local * head_size)
    projected_rows, adapter_output = lax.psum(
        (
            jnp.dot(attended_token_rows, out_w, preferred_element_type=jnp.float32),
            jnp.dot(attended_token_rows, output_down_weight, preferred_element_type=jnp.float32),
        ),
        "kv",
    )
    adapter_output = adapter_output.astype(jnp.bfloat16)
    middle_hidden = (
        residual_stream
        + projected_rows
        + jnp.dot(adapter_output, output_up_weight, preferred_element_type=jnp.float32)
    )
    scale_two = lax.rsqrt(jnp.mean(middle_hidden * middle_hidden, -1, keepdims=True) + epsilon)
    normed_two = (middle_hidden * scale_two * gain_two.astype(jnp.float32)).astype(jnp.bfloat16)
    gate_pre = jnp.dot(normed_two, gate_w, preferred_element_type=jnp.float32)
    up_pre = jnp.dot(normed_two, up_w, preferred_element_type=jnp.float32)
    sigma = jax.nn.sigmoid(gate_pre)
    activated = gate_pre * sigma
    hidden = (activated * up_pre).astype(jnp.bfloat16)
    down_terms = jnp.dot(hidden, down_proj, preferred_element_type=jnp.float32)
    ffn_out = lax.psum(down_terms.astype(jnp.bfloat16), "kv").astype(jnp.float32)
    output = (middle_hidden + ffn_out).astype(jnp.bfloat16).reshape(sequences, block_len, width)
    attn_full = (
        lax.all_gather(attention_norm_gain, "seq", axis=0, tiled=True),
        lax.all_gather(query_weight, "seq", axis=0, tiled=True),
        lax.all_gather(key_value_weight, "seq", axis=1, tiled=True),
        lax.all_gather(output_weight, "seq", axis=0, tiled=True),
        lax.all_gather(adapter_down_matrices, "seq", axis=1, tiled=True),
        lax.all_gather(adapter_query_up, "seq", axis=1, tiled=True),
        lax.all_gather(adapter_key_value_up, "seq", axis=2, tiled=True),
        lax.all_gather(adapter_output_down, "seq", axis=0, tiled=True),
        lax.all_gather(adapter_output_up, "seq", axis=1, tiled=True),
        lax.all_gather(query_feature_matrix, "seq", axis=1, tiled=True),
        lax.all_gather(key_feature_matrix, "seq", axis=1, tiled=True),
    )
    mlp_full = (
        lax.all_gather(feedforward_norm_gain, "seq", axis=0, tiled=True),
        lax.all_gather(gate_weight, "seq", axis=0, tiled=True),
        lax.all_gather(up_weight, "seq", axis=0, tiled=True),
        lax.all_gather(down_weight, "seq", axis=0, tiled=True),
    )
    (
        gain_one,
        query_w,
        kv_w,
        out_w,
        adapter_down_weight,
        query_up_weight,
        key_value_up_weight,
        output_down_weight,
        output_up_weight,
        fq_w,
        fk_w,
    ) = attn_full
    gain_two, gate_w, up_w, down_proj = mlp_full
    grad_out = cotangent.reshape(total_rows, width)
    grad_hidden = jnp.dot(grad_out, down_proj.T, preferred_element_type=jnp.float32)
    grad_gate = (grad_hidden * up_pre * sigma * (1.0 + gate_pre * (1.0 - sigma))).astype(
        jnp.bfloat16
    )
    grad_up = (grad_hidden * activated).astype(jnp.bfloat16)
    grad_down_w = jnp.dot(hidden.T, grad_out, preferred_element_type=jnp.float32)
    grad_gate_w = jnp.dot(normed_two.T, grad_gate, preferred_element_type=jnp.float32)
    grad_up_w = jnp.dot(normed_two.T, grad_up, preferred_element_type=jnp.float32)
    grad_normed_two = lax.psum(
        jnp.dot(grad_gate, gate_w.T, preferred_element_type=jnp.float32)
        + jnp.dot(grad_up, up_w.T, preferred_element_type=jnp.float32),
        "kv",
    )
    gain_grad_two, grad_middle_norm = norm_back(middle_hidden, scale_two, gain_two, grad_normed_two)
    grad_middle = grad_out.astype(jnp.float32) + grad_middle_norm
    mlp_grads = (
        lax.psum_scatter(
            gain_grad_two.astype(jnp.bfloat16), "seq", scatter_dimension=0, tiled=True
        ).astype(jnp.float32),
        lax.psum_scatter(
            grad_gate_w.astype(jnp.bfloat16), "seq", scatter_dimension=0, tiled=True
        ).astype(jnp.float32),
        lax.psum_scatter(
            grad_up_w.astype(jnp.bfloat16), "seq", scatter_dimension=0, tiled=True
        ).astype(jnp.float32),
        lax.psum_scatter(
            grad_down_w.astype(jnp.bfloat16), "seq", scatter_dimension=0, tiled=True
        ).astype(jnp.float32),
    )
    branch_gradient = grad_middle.astype(jnp.bfloat16)
    adapter_output_gradient = jnp.dot(
        branch_gradient, output_up_weight.T, preferred_element_type=jnp.float32
    ).astype(jnp.bfloat16)
    output_up_gradient = jnp.dot(
        adapter_output.T, branch_gradient, preferred_element_type=jnp.float32
    )
    grad_out_w = jnp.dot(attended_token_rows.T, branch_gradient, preferred_element_type=jnp.float32)
    output_down_gradient = jnp.dot(
        attended_token_rows.T, adapter_output_gradient, preferred_element_type=jnp.float32
    )
    grad_attended = jnp.dot(branch_gradient, out_w.T, preferred_element_type=jnp.float32) + jnp.dot(
        adapter_output_gradient, output_down_weight.T, preferred_element_type=jnp.float32
    )
    grad_groups = grad_attended.reshape(sequences, block_len, kv_local, group_size, head_size)

    def backward_one(items):
        query_s, feat_s, key_s, value_s, kfeat_s, state_s, norm_s, denom_s, grad_s = items
        return attention_back(
            query_s,
            feat_s,
            key_s,
            value_s,
            kfeat_s,
            state_s,
            norm_s,
            denom_s,
            grad_s,
            in_window,
            is_early,
        )

    grad_query_s, grad_qfeat, grad_key_ext, grad_value_ext, grad_kfeat, grad_states, grad_norms = (
        lax.map(
            backward_one,
            (
                query_groups,
                feat_groups,
                key_ext,
                value_ext,
                key_feat,
                states,
                norms,
                denominators,
                grad_groups,
            ),
        )
    )
    later_states, later_norms = prefix_2(
        (grad_states, grad_norms),
        "seq",
        add_pair,
        (jnp.zeros_like(grad_states), jnp.zeros_like(grad_norms)),
    )
    later_low = later_states.astype(jnp.bfloat16)
    grad_kfeat = (
        grad_kfeat
        + jnp.einsum("skfd,sjkd->sjkf", later_low, value_head, preferred_element_type=jnp.float32)
        + later_norms[:, None]
    )
    grad_kfeat = jnp.where(key_mask, grad_kfeat, 0.0)
    extra_values = jnp.einsum(
        "sjkf,skfd->sjkd", key_feat, later_low, preferred_element_type=jnp.float32
    )
    grad_value_ext = jnp.concatenate(
        [grad_value_ext[:, :block_len] + extra_values, grad_value_ext[:, block_len:]], 1
    )
    key_from_feat, grad_fk = feature_back(key_ext[:, :block_len], fk_w, key_mix, grad_kfeat)
    grad_key_ext = jnp.concatenate(
        [grad_key_ext[:, :block_len] + key_from_feat, grad_key_ext[:, block_len:]], 1
    )
    query_from_feat, grad_fq = feature_back(
        query_heads,
        fq_w,
        query_mix,
        grad_qfeat.reshape(sequences, block_len, heads_local, 2 * head_size),
    )
    grad_queries = (
        grad_query_s.reshape(sequences, block_len, heads_local, head_size) + query_from_feat
    )
    grad_kv_ext = jnp.stack([grad_key_ext, grad_value_ext]).reshape(
        2, sequences, block_len + WIN, kv_local * head_size
    )
    returned = from_behind(grad_kv_ext[:, :, :WIN].astype(jnp.bfloat16), "seq", -1).astype(
        jnp.float32
    )
    grad_kv = grad_kv_ext[:, :, WIN:]
    grad_kv = jnp.concatenate(
        [grad_kv[:, :, : block_len - WIN], grad_kv[:, :, block_len - WIN :] + returned], 2
    )
    key_value_lowrank_gradient = grad_kv.reshape(2, total_rows, kv_local * head_size).astype(
        jnp.bfloat16
    )
    query_lowrank_gradient = grad_queries.reshape(total_rows, heads_local * head_size).astype(
        jnp.bfloat16
    )
    grad_query_w = jnp.dot(
        normalized_input.T, query_lowrank_gradient, preferred_element_type=jnp.float32
    )
    grad_kv_w = jnp.einsum(
        "td,cte->cde",
        normalized_input,
        key_value_lowrank_gradient,
        preferred_element_type=jnp.float32,
    )
    query_up_gradient = jnp.dot(
        adapter_token_rows[0].T, query_lowrank_gradient, preferred_element_type=jnp.float32
    )
    grad_up_kv = jnp.einsum(
        "diu,dif->duf",
        adapter_token_rows[1:],
        key_value_lowrank_gradient,
        preferred_element_type=jnp.float32,
    )
    adapter_portion = jnp.concatenate(
        [
            jnp.dot(query_lowrank_gradient, query_up_weight.T, preferred_element_type=jnp.float32)[
                None
            ],
            jnp.einsum(
                "cte,cre->ctr",
                key_value_lowrank_gradient,
                key_value_up_weight,
                preferred_element_type=jnp.float32,
            ),
        ],
        0,
    )
    normalized_portion = jnp.dot(
        query_lowrank_gradient, query_w.T, preferred_element_type=jnp.float32
    ) + jnp.einsum(
        "cte,cde->td", key_value_lowrank_gradient, kv_w, preferred_element_type=jnp.float32
    )
    normalized_gradient, adapter_gradient = (
        lax.psum(normalized_portion.astype(jnp.bfloat16), "kv").astype(jnp.float32),
        lax.psum(adapter_portion.astype(jnp.bfloat16), "kv").astype(jnp.float32),
    )
    adapter_lowrank_gradient = adapter_gradient.astype(jnp.bfloat16)
    adapter_down_gradient = jnp.einsum(
        "og,boy->bgy",
        normalized_input,
        adapter_lowrank_gradient,
        preferred_element_type=jnp.float32,
    )
    normalized_gradient = normalized_gradient + jnp.einsum(
        "uki,usi->ks",
        adapter_lowrank_gradient,
        adapter_down_weight,
        preferred_element_type=jnp.float32,
    )
    gain_grad_one, grad_resid = norm_back(residual_stream, scale_one, gain_one, normalized_gradient)
    grad_tokens = (grad_middle + grad_resid).reshape(sequences, block_len, width)
    attn_grads = (
        lax.psum_scatter(
            gain_grad_one.astype(jnp.bfloat16), "seq", scatter_dimension=0, tiled=True
        ).astype(jnp.float32),
        lax.psum_scatter(
            grad_query_w.astype(jnp.bfloat16), "seq", scatter_dimension=0, tiled=True
        ).astype(jnp.float32),
        lax.psum_scatter(
            grad_kv_w.astype(jnp.bfloat16), "seq", scatter_dimension=1, tiled=True
        ).astype(jnp.float32),
        lax.psum_scatter(
            grad_out_w.astype(jnp.bfloat16), "seq", scatter_dimension=0, tiled=True
        ).astype(jnp.float32),
        lax.psum_scatter(
            adapter_down_gradient.astype(jnp.bfloat16), "seq", scatter_dimension=1, tiled=True
        ).astype(jnp.float32),
        lax.psum_scatter(
            query_up_gradient.astype(jnp.bfloat16), "seq", scatter_dimension=1, tiled=True
        ).astype(jnp.float32),
        lax.psum_scatter(
            grad_up_kv.astype(jnp.bfloat16), "seq", scatter_dimension=2, tiled=True
        ).astype(jnp.float32),
        lax.psum_scatter(
            output_down_gradient.astype(jnp.bfloat16), "seq", scatter_dimension=0, tiled=True
        ).astype(jnp.float32),
        lax.psum_scatter(
            output_up_gradient.astype(jnp.bfloat16), "seq", scatter_dimension=1, tiled=True
        ).astype(jnp.float32),
        lax.psum_scatter(
            grad_fq.astype(jnp.bfloat16), "seq", scatter_dimension=1, tiled=True
        ).astype(jnp.float32),
        lax.psum_scatter(
            grad_fk.astype(jnp.bfloat16), "seq", scatter_dimension=1, tiled=True
        ).astype(jnp.float32),
    )
    return (output, grad_tokens) + tuple(attn_grads) + tuple(mlp_grads)


def solution(mesh):
    return jax.shard_map(
        per_device,
        mesh=mesh,
        in_specs=(
            P(None, "seq", None),
            P("seq"),
            P("seq", "kv"),
            P(None, "seq", "kv"),
            P(("kv", "seq"), None),
            P(None, "seq", None),
            P(None, ("kv", "seq")),
            P(None, None, ("kv", "seq")),
            P(("kv", "seq"), None),
            P(None, "seq"),
            P("kv", "seq", None),
            P("kv", "seq", None),
            P("seq"),
            P("seq", "kv"),
            P("seq", "kv"),
            P(("kv", "seq"), None),
            P(None, "seq", None),
        ),
        out_specs=(
            P(None, "seq", None),
            P(None, "seq", None),
            P("seq"),
            P("seq", "kv"),
            P(None, "seq", "kv"),
            P(("kv", "seq"), None),
            P(None, "seq", None),
            P(None, ("kv", "seq")),
            P(None, None, ("kv", "seq")),
            P(("kv", "seq"), None),
            P(None, "seq"),
            P("kv", "seq", None),
            P("kv", "seq", None),
            P("seq"),
            P("seq", "kv"),
            P("seq", "kv"),
            P(("kv", "seq"), None),
        ),
        check_vma=False,
    )
```

profile of v0, /device:TPU:9, one launch (start us, length us, event | category | flops | bytes accessed | tf_op | source)
XLA Modules:
  0.0 2099.5 jit_solution(5120855828614904464)
XLA Ops:
  27.3 24.5 %all_gather.85 = bf16[2,8,128]{1,0,2:T(2,128)(2,1)S(1)} all-gather(bf16[2,8,16]{1,0,2:T(2,128)(2,1)S(1)} %copy.96), channel_id=1, replica_groups=mesh['seq'=8,'kv'=4] {'seq'}, dimensions={2}, use_global_device_ids=true | all-gather | bytes 4608 | tf_op jit(solution)/shard_map/all_gather | solution.py:208
  75.0 24.6 %all_gather.84 = bf16[3,2048,8]{1,2,0:T(8,128)(2,1)S(1)} all-gather(bf16[3,256,8]{1,2,0:T(8,128)(2,1)} %param.26), channel_id=1, replica_groups=mesh['seq'=8,'kv'=4] {'seq'}, dimensions={1}, use_global_device_ids=true | all-gather | bytes 110592 | tf_op jit(solution)/shard_map/all_gather | solution.py:206
  129.4 24.6 %all_gather.89 = bf16[8,64,64]{2,1,0:T(8,128)(2,1)} all-gather(bf16[8,8,64]{2,1,0:T(8,128)(2,1)S(1)} %copy-done.109), channel_id=1, replica_groups=mesh['seq'=8,'kv'=4] {'seq'}, dimensions={1}, use_global_device_ids=true | all-gather | bytes 73728 | tf_op jit(solution)/shard_map/all_gather | solution.py:211
  155.8 24.9 %all-gather = f32[16,128,64]{1,2,0:T(8,128)S(1)} all-gather(f32[2,128,64]{1,2,0:T(8,128)S(1)} %fusion.114), channel_id=2, replica_groups=mesh['seq'=8,'kv'=4] {'seq'}, dimensions={0}, use_global_device_ids=true | all-gather | bytes 589824 | tf_op jit(solution)/shard_map/all_gather | solution.py:20
  265.1 24.4 %all_gather.96 = bf16[8,2048]{1,0:T(8,128)(2,1)S(1)} all-gather(bf16[8,256]{1,0:T(8,128)(2,1)S(1)} %copy-done.117), channel_id=1, replica_groups=mesh['seq'=8,'kv'=4] {'seq'}, dimensions={1}, use_global_device_ids=true | all-gather | bytes 36864 | tf_op jit(solution)/shard_map/all_gather | solution.py:210
  290.8 60.4 %psum.43 = bf16[512,8]{0,1:T(8,128)(2,1)S(1)} all-reduce(f32[512,8]{0,1:T(8,128)S(1)} %fusion.153), channel_id=1, replica_groups=mesh['seq'=8,'kv'=4] {'kv'}, use_global_device_ids=true, to_apply=%region_16.17 | all-reduce | flops 4096 | bytes 24576 | tf_op jit(solution)/shard_map/psum | solution.py:299
  358.1 118.1 %all-gather.23.cloned.1.call-done = bf16[2048,2048]{1,0:T(8,128)(2,1)} async-done(((bf16[256,2048]{1,0:T(8,128)(2,1)}), bf16[2048,2048]{1,0:T(8,128)(2,1)}) %all-gather.23.cloned.1.call-update) | async-done | bytes 8388624 | tf_op jit(solution)/shard_map/all_gather | solution.py:216
  486.7 114.8 %all-gather.25.cloned.1.call-done = bf16[2048,2048]{1,0:T(8,128)(2,1)} async-done(((bf16[256,2048]{1,0:T(8,128)(2,1)}), bf16[2048,2048]{1,0:T(8,128)(2,1)}) %all-gather.25.cloned.1.call-update) | async-done | bytes 8388624 | tf_op jit(solution)/shard_map/all_gather | solution.py:217
  612.0 115.0 %all-gather.27.cloned.1.call-done = bf16[2048,2048]{1,0:T(8,128)(2,1)} async-done(((bf16[256,2048]{1,0:T(8,128)(2,1)}), bf16[2048,2048]{1,0:T(8,128)(2,1)}) %all-gather.27.cloned.1.call-update) | async-done | bytes 8388624 | tf_op jit(solution)/shard_map/all_gather | solution.py:218
  756.9 84.6 %all-reduce.12.cloned.1.call-done = f32[512,2048]{1,0:T(8,128)} async-done(((f32[512,2048]{1,0:T(8,128)}), f32[512,2048]{1,0:T(8,128)}) %all-reduce.12.cloned.1.call-update) | async-done | bytes 4194320 | tf_op jit(solution)/shard_map/psum | solution.py:364
  858.2 23.8 %all-gather.2 = bf16[16,128,64]{1,2,0:T(8,128)(2,1)} all-gather(bf16[2,128,64]{1,2,0:T(8,128)(2,1)S(1)} %fusion.84), channel_id=4, replica_groups=mesh['seq'=8,'kv'=4] {'seq'}, dimensions={0}, use_global_device_ids=true | all-gather | bytes 294912 | tf_op jit(solution)/shard_map/all_gather | solution.py:36
  1059.9 41.8 %reduce-scatter.42.cloned.1.call-done = bf16[64,8]{1,0:T(8,128)(2,1)} async-done(((bf16[512,8]{1,0:T(8,128)(2,1)}), bf16[64,8]{1,0:T(8,128)(2,1)}) %reduce-scatter.42.cloned.1.call-update) | async-done | bytes 1040
  1103.1 54.7 %reduce-scatter.40.cloned.1.call-done = bf16[16,16]{1,0:T(8,128)(2,1)} async-done(((bf16[128,16]{1,0:T(8,128)(2,1)}), bf16[16,16]{1,0:T(8,128)(2,1)}) %reduce-scatter.40.cloned.1.call-update) | async-done | bytes 528
  1159.2 54.2 %reduce-scatter.30.cloned.1.call-done = bf16[8,256]{1,0:T(8,128)(2,1)} async-done(((bf16[8,2048]{1,0:T(8,128)(2,1)}), bf16[8,256]{1,0:T(8,128)(2,1)}) %reduce-scatter.30.cloned.1.call-update) | async-done | bytes 4112 | tf_op jit(solution)/shard_map/reduce_scatter | solution.py:562
  1214.6 62.7 %reduce-scatter.44.cloned.1.call-done = bf16[8,512]{1,0:T(8,128)(2,1)} async-done(((bf16[64,512]{1,0:T(8,128)(2,1)}), bf16[8,512]{1,0:T(8,128)(2,1)}) %reduce-scatter.44.cloned.1.call-update) | async-done | bytes 8208
  1278.7 58.7 %reduce-scatter.28.cloned.1.call-done = bf16[3,256,8]{1,2,0:T(8,128)(2,1)} async-done(((bf16[3,2048,8]{1,2,0:T(8,128)(2,1)}), bf16[3,256,8]{1,2,0:T(8,128)(2,1)}) %reduce-scatter.28.cloned.1.call-update) | async-done | bytes 12304 | tf_op jit(solution)/shard_map/reduce_scatter | solution.py:550
  1338.7 64.9 %reduce-scatter.24.cloned.1.call-done = bf16[2,256,128]{1,2,0:T(8,128)(2,1)} async-done(((bf16[2,2048,128]{1,2,0:T(8,128)(2,1)}), bf16[2,256,128]{1,2,0:T(8,128)(2,1)}) %reduce-scatter.24.cloned.1.call-update) | async-done | bytes 131088 | tf_op jit(solution)/shard_map/reduce_scatter | solution.py:544
  1405.3 88.6 %all-reduce.14.cloned.1.call-done = (bf16[512,2048]{1,0:T(8,128)(2,1)}, bf16[512,2048]{1,0:T(8,128)(2,1)}) async-done(((bf16[512,2048]{1,0:T(8,128)(2,1)}, bf16[512,2048]{1,0:T(8,128)(2,1)}), (bf16[512,2048]{1,0:T(8,128)(2,1)}, bf16[512,2048]{1,0:T(8,128)(2,1)})) %all-reduce.14.cloned.1.call-update) | async-done | bytes 4194320 | tf_op jit(solution)/shard_map/psum | solution.py:320
  1499.1 28.7 %all-reduce.4 = (bf16[2048]{0:T(1024)(128)(2,1)S(1)}, bf16[2,64,64]{2,1,0:T(8,128)(2,1)S(1)}, bf16[2048]{0:T(1024)(128)(2,1)S(1)}) all-reduce(bf16[2048]{0:T(1024)(128)(2,1)S(1)} %get-tuple-element.318, bf16[2,64,64]{2,1,0:T(8,128)(2,1)S(1)} %convolution_convert_fusion.10, ...), channel_id=6, replica_groups=mesh['seq'=8,'kv'=4] {'seq'}, use_global_device_ids=true, to_apply=%region_33.34.clone | all-reduce | flops 12288 | bytes 49152
  1539.0 24.6 %reduce-scatter.22.cloned.1.call-done = bf16[256,512]{1,0:T(8,128)(2,1)} async-done(((bf16[2048,512]{1,0:T(8,128)(2,1)}), bf16[256,512]{1,0:T(8,128)(2,1)}) %reduce-scatter.22.cloned.1.call-update) | async-done | bytes 262160 | tf_op jit(solution)/shard_map/reduce_scatter | solution.py:541
  1565.4 68.3 %reduce-scatter.26.cloned.1.call-done = bf16[64,2048]{1,0:T(8,128)(2,1)} async-done(((bf16[512,2048]{1,0:T(8,128)(2,1)}), bf16[64,2048]{1,0:T(8,128)(2,1)}) %reduce-scatter.26.cloned.1.call-update) | async-done | bytes 262160 | tf_op jit(solution)/shard_map/reduce_scatter | solution.py:547
  1635.4 150.4 %reduce-scatter.32.cloned.1.call-done = bf16[256,2048]{1,0:T(8,128)(2,1)} async-done(((bf16[2048,2048]{1,0:T(8,128)(2,1)}), bf16[256,2048]{1,0:T(8,128)(2,1)}) %reduce-scatter.32.cloned.1.call-update) | async-done | bytes 1048592 | tf_op jit(solution)/shard_map/reduce_scatter | solution.py:375
  1788.7 149.1 %reduce-scatter.34.cloned.1.call-done = bf16[256,2048]{1,0:T(8,128)(2,1)} async-done(((bf16[2048,2048]{1,0:T(8,128)(2,1)}), bf16[256,2048]{1,0:T(8,128)(2,1)}) %reduce-scatter.34.cloned.1.call-update) | async-done | bytes 1048592 | tf_op jit(solution)/shard_map/reduce_scatter | solution.py:378
  1940.5 148.9 %reduce-scatter.36.cloned.1.call-done = bf16[256,2048]{1,0:T(8,128)(2,1)} async-done(((bf16[2048,2048]{1,0:T(8,128)(2,1)}), bf16[256,2048]{1,0:T(8,128)(2,1)}) %reduce-scatter.36.cloned.1.call-update) | async-done | bytes 1048592 | tf_op jit(solution)/shard_map/reduce_scatter | solution.py:381
  (498 shorter events, 457.5 us)
Async XLA Ops:
  7.2 96.3 %all-gather.17.cloned.1.call-start = ((), (), s32[]{:S(2)}) async-start(), calls=%async_computation.12 | async-start | bytes 1179648 | tf_op jit(solution)/shard_map/all_gather | solution.py:204
  7.9 188.5 %all-gather.19.cloned.1.call-start = ((), (), s32[]{:S(2)}) async-start(), calls=%async_computation.13 | async-start | bytes 2359296 | tf_op jit(solution)/shard_map/all_gather | solution.py:203
  8.7 213.2 %all-gather.21.cloned.1.call-start = ((), (), s32[]{:S(2)}) async-start(), calls=%async_computation.14 | async-start | bytes 2359296 | tf_op jit(solution)/shard_map/all_gather | solution.py:205
  9.4 341.8 %all-reduce.10.cloned.1.call-start = ((), (), s32[]{:S(2)}) async-start(), calls=%async_computation.15 | async-start | bytes 8388608 | tf_op jit(solution)/shard_map/psum | solution.py:299
  105.5 48.5 %collective-permute-start = (bf16[2,1,64,128]{3,2,0,1:T(8,128)(2,1)S(1)}, bf16[2,1,64,128]{3,2,0,1:T(8,128)(2,1)S(1)}, u32[]{:S(2)}, u32[]{:S(2)}) collective-permute-start(bf16[2,1,64,128]{3,2,0,1:T(8,128)(2,1)S(1)} %slice.92), channel_id=1, source_target_pairs={{0,4},{4,8},{8,12},{12,16},{16,20},{20,24},{24,28},{1,5},{5,9},{9,... | collective-permute-start | bytes 98312 | tf_op jit(solution)/shard_map/ppermute | solution.py:15
  215.6 637.5 %copy-start.68 = (f32[512,2,4]{0,2,1:T(4,128)}, f32[512,2,4]{0,2,1:T(4,128)S(1)}, u32[]{:S(2)}) copy-start(f32[512,2,4]{0,2,1:T(4,128)S(1)} %bitcast_add_fusion.6) | copy-start | bytes 49156
  227.0 249.2 %all-gather.23.cloned.1.call-start = ((), (), s32[]{:S(2)}) async-start(), calls=%async_computation.16 | async-start | bytes 9437184 | tf_op jit(solution)/shard_map/all_gather | solution.py:216
  227.6 374.0 %all-gather.25.cloned.1.call-start = ((), (), s32[]{:S(2)}) async-start(), calls=%async_computation.17 | async-start | bytes 9437184 | tf_op jit(solution)/shard_map/all_gather | solution.py:217
  228.2 498.9 %all-gather.27.cloned.1.call-start = ((), (), s32[]{:S(2)}) async-start(), calls=%async_computation.18 | async-start | bytes 9437184 | tf_op jit(solution)/shard_map/all_gather | solution.py:218
  228.9 612.6 %all-reduce.12.cloned.1.call-start = ((), (), s32[]{:S(2)}) async-start(), calls=%async_computation.19 | async-start | bytes 8388608 | tf_op jit(solution)/shard_map/psum | solution.py:364
  755.6 302.9 %reduce-scatter.38.cloned.1.call-start = ((), (), s32[]{:S(2)}) async-start(), calls=%async_computation.28 | async-start | bytes 147456
  949.3 19.5 collective-permute-start.1
  966.9 134.8 %reduce-scatter.42.cloned.1.call-start = ((), (), s32[]{:S(2)}) async-start(), calls=%async_computation.30 | async-start | bytes 147456
  968.8 189.0 %reduce-scatter.40.cloned.1.call-start = ((), (), s32[]{:S(2)}) async-start(), calls=%async_computation.29 | async-start | bytes 36864
  971.9 241.5 %reduce-scatter.30.cloned.1.call-start = ((), (), s32[]{:S(2)}) async-start(), calls=%async_computation.24 | async-start | bytes 36864 | tf_op jit(solution)/shard_map/reduce_scatter | solution.py:562
  975.5 301.8 %reduce-scatter.44.cloned.1.call-start = ((), (), s32[]{:S(2)}) async-start(), calls=%async_computation.31 | async-start | bytes 73728
  976.3 361.1 %reduce-scatter.28.cloned.1.call-start = ((), (), s32[]{:S(2)}) async-start(), calls=%async_computation.23 | async-start | bytes 110592 | tf_op jit(solution)/shard_map/reduce_scatter | solution.py:550
  1000.4 403.2 %reduce-scatter.24.cloned.1.call-start = ((), (), s32[]{:S(2)}) async-start(), calls=%async_computation.21 | async-start | bytes 1179648 | tf_op jit(solution)/shard_map/reduce_scatter | solution.py:544
  1004.1 489.9 %all-reduce.14.cloned.1.call-start = ((), (), s32[]{:S(2)}) async-start(), calls=%async_computation.32 | async-start | bytes 8388608 | tf_op jit(solution)/shard_map/psum | solution.py:320
  1017.6 546.0 %reduce-scatter.22.cloned.1.call-start = ((), (), s32[]{:S(2)}) async-start(), calls=%async_computation.20 | async-start | bytes 2359296 | tf_op jit(solution)/shard_map/reduce_scatter | solution.py:541
  1020.7 613.0 %reduce-scatter.26.cloned.1.call-start = ((), (), s32[]{:S(2)}) async-start(), calls=%async_computation.22 | async-start | bytes 2359296 | tf_op jit(solution)/shard_map/reduce_scatter | solution.py:547
  1024.9 761.0 %reduce-scatter.32.cloned.1.call-start = ((), (), s32[]{:S(2)}) async-start(), calls=%async_computation.25 | async-start | bytes 9437184 | tf_op jit(solution)/shard_map/reduce_scatter | solution.py:375
  1035.1 902.7 %reduce-scatter.34.cloned.1.call-start = ((), (), s32[]{:S(2)}) async-start(), calls=%async_computation.26 | async-start | bytes 9437184 | tf_op jit(solution)/shard_map/reduce_scatter | solution.py:378
  1045.3 1044.1 %reduce-scatter.36.cloned.1.call-start = ((), (), s32[]{:S(2)}) async-start(), calls=%async_computation.27 | async-start | bytes 9437184 | tf_op jit(solution)/shard_map/reduce_scatter | solution.py:381
  (126 other events, 6155.1 us)
Sparse Core Ops, SparseCore 0:
  10.2 40.0 all-gather.16
  52.4 49.5 all-gather.18
  104.1 49.0 all-gather.20
  227.1 123.8 all-reduce.9
  353.2 122.9 all-gather.22
  478.4 123.1 all-gather.24
  603.9 123.1 all-gather.26
  755.7 85.7 all-reduce.11
  967.0 71.5 reduce-scatter.37
  1041.8 59.8 reduce-scatter.41
  1105.4 52.3 reduce-scatter.39
  1160.7 52.5 reduce-scatter.29
  1216.7 60.5 reduce-scatter.43
  1280.4 56.9 reduce-scatter.27
  1340.7 62.9 reduce-scatter.23
  1407.2 86.6 all-reduce.13
  1497.3 66.2 reduce-scatter.21
  1567.0 66.6 reduce-scatter.25
  1637.3 148.5 reduce-scatter.31
  1789.8 147.9 reduce-scatter.33
  1941.4 147.9 reduce-scatter.35
where the time goes:
time: 2110 us; the launch traced here: 2100 us
  waiting for transfers between devices  1400 us (66%)
  blocking collectives  382 us (18%)
  matrix products  180 us (9%)
  other arithmetic  67.5 us (3%)
  local copies, waits for them, and re-layouts  39.4 us (2%)
    unnamed x25, waiting for transfers between devices  163 us
    reduce_scatter x1, waiting for transfers between devices, per_device(): lax.psum_scatter(grad_gate_w.astype(jnp.bfloat16), 'seq', scatter_dimensi...  150 us
    reduce_scatter x1, waiting for transfers between devices, per_device(): lax.psum_scatter(grad_up_w.astype(jnp.bfloat16), 'seq', scatter_dimension...  149 us
    reduce_scatter x1, waiting for transfers between devices, per_device(): lax.psum_scatter(grad_down_w.astype(jnp.bfloat16), 'seq', scatter_dimensi...  149 us
    all_gather x1, waiting for transfers between devices, per_device(): lax.all_gather(gate_weight, 'seq', axis=0, tiled=True)  118 us
    all_gather x1, waiting for transfers between devices, per_device(): lax.all_gather(down_weight, 'seq', axis=0, tiled=True)  115 us
    all_gather x1, waiting for transfers between devices, per_device(): lax.all_gather(up_weight, 'seq', axis=0, tiled=True)  115 us
    psum x1, waiting for transfers between devices, per_device(): lax.psum(down_terms.astype(jnp.bfloat16), 'kv').astype(jnp.float32)  88.6 us
  transfers between devices with their start and end apart: 23, of which 16 were waited for; matrix products, arithmetic and copies ran while one was open for 8% of the time, Pallas kernels for 0%

commit v1 on v0

v1 whole, which is shorter than its diff:
```python
import jax
import jax.numpy as jnp
from jax import lax
from jax.sharding import PartitionSpec as P

WIN = 64
RING = 4
epsilon = 1e-05
bf16 = jnp.bfloat16
f32 = jnp.float32


def trade(array, axis, mask):
    count = lax.axis_size(axis)
    return lax.ppermute(array, axis, [(i, i ^ mask) for i in range(count)])


def moved(array, axis, by):
    count = lax.axis_size(axis)
    pairs = [(i, i + by) for i in range(count) if 0 <= i + by < count]
    return lax.ppermute(array, axis, pairs)


def earlier_sum(part, axis, sign):
    count = lax.axis_size(axis)
    result = None
    window, reach = part, 1
    while reach < count:
        terms = [moved(window, axis, sign * reach * k) for k in (1, 2, 3) if reach * k < count]
        total = terms[0]
        for term in terms[1:]:
            total = total + term
        result = total if result is None else result + total
        window = window + total
        reach *= 4
    return result


def dot(a, b):
    return jnp.dot(a, b, preferred_element_type=f32)


def dot_nt(a, b):
    return lax.dot_general(a, b, (((1,), (1,)), ((), ())), preferred_element_type=f32)


def dot_tn(a, b):
    return lax.dot_general(a, b, (((0,), (0,)), ((), ())), preferred_element_type=f32)


def add_low(a, b):
    return (a.astype(f32) + b.astype(f32)).astype(bf16)


def placed(pieces, order):
    rows = pieces[0].shape[0]
    result = jnp.zeros((rows * len(pieces),) + pieces[0].shape[1:], pieces[0].dtype)
    for piece, at in zip(pieces, order):
        result = lax.dynamic_update_slice_in_dim(result, piece, at * rows, 0)
    return result


def block(array, at, rows, axis=0):
    return lax.dynamic_slice_in_dim(array, at * rows, rows, axis)


def seq_gather(own, pair):
    got = {0: own}
    got[2 * pair] = trade(own, "seq", 2 * pair)
    got[pair] = trade(own, "seq", pair)
    got[3 * pair] = trade(got[2 * pair], "seq", pair)
    bit = 1
    while bit < pair:
        for mask in list(got):
            got[mask | bit] = trade(got[mask], "seq", bit)
        bit *= 2
    return [got[i] for i in range(len(got))]


def token_gather(own, pair):
    got = [own, None, None, None]
    got[2] = trade(own, "seq", 2 * pair)
    got[1] = trade(own, "seq", pair)
    got[3] = trade(got[2], "seq", pair)
    result = []
    for piece in got:
        side = trade(piece, "kv", 2)
        result.append([piece, trade(piece, "kv", 1), side, trade(side, "kv", 1)])
    return result


def token_sum(parts, pair):
    sums = {}
    for d in (3, 2, 1, 0):
        near = add_low(parts[d][0], trade(parts[d][1], "kv", 1))
        side = add_low(parts[d][2], trade(parts[d][3], "kv", 1))
        sums[d] = add_low(near, trade(side, "kv", 2))
    far = add_low(sums[2], trade(sums[3], "seq", pair))
    near = add_low(sums[0], trade(sums[1], "seq", pair))
    return add_low(near, trade(far, "seq", 2 * pair))


def kv_sum(parts):
    near = add_low(parts[0], trade(parts[1], "kv", 1))
    side = add_low(parts[2], trade(parts[3], "kv", 1))
    return near.astype(f32) + trade(side, "kv", 2).astype(f32)


def kv_gather(own):
    side = trade(own, "kv", 2)
    return [own, trade(own, "kv", 1), side, trade(side, "kv", 1)]


def kv_total(own):
    for mask in (1, 2):
        low = lax.optimization_barrier(own.astype(bf16))
        own = low.astype(f32) + trade(low, "kv", mask).astype(f32)
    return own


def seq_scatter(parts, pair):
    parts = list(parts)
    size = len(parts)
    bit = 1
    while bit < pair:
        for i in range(0, size, 2 * bit):
            parts[i] = add_low(parts[i], trade(parts[i + bit], "seq", bit))
        bit *= 2
    far = add_low(parts[2 * pair], trade(parts[3 * pair], "seq", pair))
    near = add_low(parts[0], trade(parts[pair], "seq", pair))
    return near.astype(f32) + trade(far, "seq", 2 * pair).astype(f32)


def seq_halves(parts):
    bit = parts.shape[0] // 2
    while bit:
        parts = add_low(parts[:bit], trade(parts[bit:], "seq", bit))
        bit //= 2
    return parts[0]


def spread_features(mixing):
    return jnp.concatenate([jax.nn.softmax(mixing, -1), jax.nn.softmax(-mixing, -1)], -1)


def feature_map(rows, matrix):
    mixing = jnp.einsum("thd,hde->the", rows, matrix, preferred_element_type=f32)
    return mixing, spread_features(mixing).astype(bf16)


def feature_back(rows, matrix, mixing, grad):
    grad = grad.astype(bf16).astype(f32)
    unused, pull = jax.vjp(spread_features, mixing)
    grad_mix = pull(grad)[0].astype(bf16)
    grad_rows = jnp.einsum("the,hde->thd", grad_mix, matrix, preferred_element_type=f32)
    grad_matrix = jnp.einsum("thd,the->hde", rows, grad_mix, preferred_element_type=f32)
    return grad_rows, grad_matrix


def norm_back(values, scale, gain, grad):
    scaled = grad * gain
    gain_grad = jnp.sum(grad * values * scale, 0)
    mean = jnp.mean(scaled * values, -1, keepdims=True)
    return gain_grad, scale * scaled - values * scale * scale * scale * mean


def inverse_rms(values):
    return lax.rsqrt(jnp.mean(values * values, -1, keepdims=True) + epsilon)


def window_masks(length, offset):
    row_ids = jnp.arange(length)[:, None]
    col_ids = jnp.arange(length + WIN)[None, :]
    is_valid = offset - WIN + jnp.arange(length + WIN) >= 0
    in_window = (col_ids > row_ids) & (col_ids <= row_ids + WIN) & is_valid[None, :]
    is_early = col_ids[:, :length] <= row_ids
    return in_window, is_early, is_valid[:length]


def attend(query, feat, key, value, kfeat, state, norm, masks):
    in_window, is_early = masks
    length = query.shape[0]
    scores = jnp.einsum("ikgd,jkd->kgij", query, key, preferred_element_type=f32) * query.shape[-1] ** (-0.5)
    window = jnp.where(in_window, jnp.exp(scores), 0.0)
    linear = jnp.einsum("ikgf,jkf->kgij", feat, kfeat, preferred_element_type=f32)
    early = jnp.where(is_early, linear, 0.0)
    window_low, early_low = window.astype(bf16), early.astype(bf16)
    top = jnp.einsum("kgij,jkd->ikgd", window_low, value, preferred_element_type=f32)
    top = top + jnp.einsum("kgij,jkd->ikgd", early_low, value[:length], preferred_element_type=f32)
    top = top + jnp.einsum("ikgf,kfd->ikgd", feat, state.astype(bf16), preferred_element_type=f32)
    under = jnp.transpose(jnp.sum(window, -1) + jnp.sum(early, -1), (2, 0, 1))
    under = under + jnp.sum(feat.astype(f32) * norm[None, :, None, :], -1)
    return window_low, early_low, top, under


def attend_state_back(feat, top, under, grad):
    grad_top = (grad / under[..., None]).astype(bf16)
    grad_under = -jnp.sum(grad * top, -1) / (under * under)
    grad_state = jnp.einsum("ikgf,ikgd->kfd", feat, grad_top, preferred_element_type=f32)
    grad_norm = jnp.sum(feat.astype(f32) * grad_under[..., None], (0, 2))
    return grad_top, grad_under, grad_state, grad_norm


def attend_back(query, feat, key, value, kfeat, state, norm, window, early, grad_top, grad_under, is_early):
    length = query.shape[0]
    scale = query.shape[-1] ** (-0.5)
    e = jnp.einsum("ikgd,jkd->kgij", grad_top, value, preferred_element_type=f32)
    e = e + jnp.transpose(grad_under, (1, 2, 0))[..., None]
    grad_window = (e * window.astype(f32)).astype(bf16)
    grad_early = jnp.where(is_early, e[..., :length], 0.0).astype(bf16)
    grad_query = jnp.einsum("kgij,jkd->ikgd", grad_window, key, preferred_element_type=f32) * scale
    grad_key = jnp.einsum("kgij,ikgd->jkd", grad_window, query, preferred_element_type=f32) * scale
    grad_feat = jnp.einsum("kgij,jkf->ikgf", grad_early, kfeat, preferred_element_type=f32)
    grad_feat = grad_feat + jnp.einsum("ikgd,kfd->ikgf", grad_top, state.astype(bf16), preferred_element_type=f32)
    grad_feat = grad_feat + grad_under[..., None] * norm[None, :, None, :]
    grad_kfeat = jnp.einsum("kgij,ikgf->jkf", grad_early, feat, preferred_element_type=f32)
    grad_value = jnp.einsum("kgij,ikgd->jkd", window, grad_top, preferred_element_type=f32)
    from_early = jnp.einsum("kgij,ikgd->jkd", early, grad_top, preferred_element_type=f32)
    grad_value = grad_value + jnp.pad(from_early, ((0, WIN), (0, 0), (0, 0)))
    return grad_query, grad_feat, grad_key, grad_value, grad_kfeat


def per_device(
    tokens,
    attention_norm_gain,
    query_weight,
    key_value_weight,
    output_weight,
    adapter_down_matrices,
    adapter_query_up,
    adapter_key_value_up,
    adapter_output_down,
    adapter_output_up,
    query_feature_matrix,
    key_feature_matrix,
    feedforward_norm_gain,
    gate_weight,
    up_weight,
    down_weight,
    cotangent,
):
    count = lax.axis_size("seq")
    pair = count // RING
    place = lax.axis_index("seq")
    along, beside = place // pair, place % pair
    lane = lax.axis_index("kv")
    kv_count = lax.axis_size("kv")
    unused, length, width = tokens.shape
    chunk = length // kv_count
    depth = query_weight.shape[0]
    q_cols = query_weight.shape[1]
    kv_cols = key_value_weight.shape[2]
    head_size = query_feature_matrix.shape[2]
    heads = query_feature_matrix.shape[0]
    kv_heads = key_feature_matrix.shape[0]
    group = heads // kv_heads
    rank = adapter_query_up.shape[0]
    all_cols = q_cols + 2 * kv_cols
    lora_cols = 3 * rank

    def wide(a, rows, cols):
        return jnp.pad(a, ((0, rows - a.shape[0]), (0, cols - a.shape[1])))

    small_rows = q_cols // count
    fk_rows = kv_heads * (head_size // count)
    up_rows = 2 * rank
    vec = jnp.concatenate(
        [attention_norm_gain[None], feedforward_norm_gain[None], adapter_output_up], 0
    )
    vec_rows = vec.size // 64
    small = jnp.concatenate(
        [
            wide(
                jnp.concatenate(
                    [query_feature_matrix.reshape(small_rows, head_size), adapter_output_down], 1
                ),
                small_rows,
                104,
            ),
            wide(key_feature_matrix.reshape(fk_rows, head_size), fk_rows, 104),
            wide(
                jnp.concatenate(
                    [
                        adapter_key_value_up.reshape(up_rows, -1),
                        wide(adapter_query_up, up_rows, adapter_query_up.shape[1]),
                    ],
                    1,
                ),
                up_rows,
                104,
            ),
            wide(vec.reshape(vec_rows, 64), vec_rows, 104),
        ],
        0,
    )
    packed = jnp.concatenate(
        [
            query_weight,
            key_value_weight[0],
            key_value_weight[1],
            adapter_down_matrices[0],
            adapter_down_matrices[1],
            adapter_down_matrices[2],
            wide(small, depth, 104),
        ],
        1,
    )
    order = [place ^ i for i in range(count)]
    pieces = seq_gather(packed, pair)
    halo = moved(tokens[0, length - WIN :], "seq", 1)

    full = placed(pieces, order)
    small_full = full.reshape(count, depth, -1)[:, :, all_cols + lora_cols :]
    at = small_rows
    fq_w = jnp.transpose(
        small_full[:, :at, :head_size].reshape(count, heads, -1, head_size), (1, 0, 2, 3)
    ).reshape(heads, head_size, head_size)
    out_down = small_full[:, :at, head_size : head_size + rank].reshape(q_cols, rank)
    fk_w = jnp.transpose(
        small_full[:, at : at + fk_rows, :head_size].reshape(count, kv_heads, -1, head_size),
        (1, 0, 2, 3),
    ).reshape(kv_heads, head_size, head_size)
    at += fk_rows
    kv_each = kv_cols // count
    q_each = q_cols // count
    kv_up = jnp.transpose(
        small_full[:, at : at + up_rows, :kv_each].reshape(count, 2, rank, kv_each), (1, 2, 0, 3)
    ).reshape(2, rank, kv_cols)
    q_up = jnp.transpose(
        small_full[:, at : at + rank, kv_each : kv_each + q_each], (1, 0, 2)
    ).reshape(rank, q_cols)
    at += up_rows
    vecs = jnp.transpose(
        small_full[:, at : at + vec_rows, :64].reshape(count, 2 + rank, depth), (1, 0, 2)
    ).reshape(2 + rank, width)
    gain_one = vecs[0].astype(f32)
    gain_two = vecs[1].astype(f32)
    out_up = vecs[2:]
    spare = full.shape[1] - all_cols
    ups = jnp.concatenate(
        [
            jnp.pad(q_up, ((0, 0), (0, 2 * kv_cols))),
            jnp.pad(kv_up[0], ((0, 0), (q_cols, kv_cols))),
            jnp.pad(kv_up[1], ((0, 0), (q_cols + kv_cols, 0))),
            jnp.zeros((spare - lora_cols, all_cols), bf16),
        ],
        0,
    )

    out_pieces = [output_weight, None, None, None]
    out_pieces[2] = trade(output_weight, "seq", 2 * pair)
    out_pieces[1] = trade(output_weight, "seq", pair)
    out_pieces[3] = trade(out_pieces[2], "seq", pair)
    rows_out = output_weight.shape[0]
    units_each = down_weight.shape[0]
    units = gate_weight.shape[1] // RING

    def unit_block(d):
        at = (along ^ d) * units
        return jnp.concatenate(
            [
                lax.dynamic_slice_in_dim(gate_weight, at, units, 1),
                lax.dynamic_slice_in_dim(up_weight, at, units, 1),
            ],
            1,
        )

    gu_pieces = {d * pair: unit_block(d) for d in range(RING)}
    for d in (2, 1, 3):
        gu_pieces[d * pair] = trade(gu_pieces[d * pair], "seq", d * pair)
    mixed = [jnp.concatenate([down_weight] + out_pieces, 0)]
    bit = 1
    while bit < pair:
        for mask in list(gu_pieces):
            gu_pieces[mask | bit] = trade(gu_pieces[mask], "seq", bit)
        mixed = mixed + [trade(m, "seq", bit) for m in mixed]
        bit *= 2
    gu_w = placed([gu_pieces[i] for i in range(count)], order)
    down_w = placed([m[:units_each] for m in mixed], [beside ^ i for i in range(pair)])
    out_w = placed(
        [mixed[i % pair][units_each + (i // pair) * rows_out :][:rows_out] for i in range(count)],
        order,
    )
    out_ext = jnp.concatenate([out_w, wide(out_down, q_cols, 128)], 1)

    own_dy = block(cotangent[0], lane, chunk)
    dy_pieces = token_gather(own_dy, pair)

    extended = jnp.concatenate([halo, tokens[0]], 0).astype(f32)
    scale_ext = inverse_rms(extended)
    normed_ext = (extended * scale_ext * gain_one).astype(bf16)
    normed = normed_ext[WIN:]
    scale_one = scale_ext[WIN:]
    projected = dot(normed_ext, full)
    lora_ext = projected[:, all_cols:].astype(bf16)
    qkv = (projected[:, :all_cols] + dot(lora_ext, ups)).astype(bf16)
    query = qkv[WIN:, :q_cols].reshape(length, heads, head_size)
    key_ext = qkv[:, q_cols : q_cols + kv_cols].reshape(-1, kv_heads, head_size)
    value_ext = qkv[:, q_cols + kv_cols :].reshape(-1, kv_heads, head_size)
    in_window, is_early, is_valid = window_masks(length, place * length)
    key_mask = is_valid[:, None, None]
    key_mix, key_feat = feature_map(key_ext[:length], fk_w)
    key_feat = jnp.where(key_mask, key_feat, jnp.zeros_like(key_feat))
    value_head = value_ext[:length]
    totals = jnp.einsum("jkf,jkd->kfd", key_feat, value_head, preferred_element_type=f32)
    feat_sums = jnp.sum(key_feat.astype(f32), 0)
    both = earlier_sum(
        jnp.concatenate([totals, jnp.pad(feat_sums[..., None], ((0, 0), (0, 0), (0, 63)))], -1), "seq", 1
    )
    states, norms = both[..., :head_size], both[..., head_size]
    query_mix, query_feat = feature_map(query, fq_w)
    query_groups = query.reshape(length, kv_heads, group, head_size)
    feat_groups = query_feat.reshape(length, kv_heads, group, 2 * head_size)
    window, early, top, under = attend(
        query_groups, feat_groups, key_ext, value_ext, key_feat, states, norms, (in_window, is_early)
    )
    attended = (top / under[..., None]).astype(bf16).reshape(length, q_cols)

    nears = [lane ^ k for k in range(kv_count)]
    chunks = [block(attended, k, chunk) for k in nears]
    branch = kv_sum([dot(c, out_ext).astype(bf16) for c in chunks])
    lora_out = branch[:, width : width + rank].astype(bf16)
    own_tokens = block(tokens[0], lane, chunk).astype(f32)
    middle = own_tokens + branch[:, :width] + dot(lora_out, out_up)
    scale_two = inverse_rms(middle)
    normed_two = (middle * scale_two * gain_two).astype(bf16)

    n_pieces = token_gather(normed_two, pair)
    grad_parts = []
    out_parts = []
    n_blocks, dy_blocks, hidden_blocks, gu_blocks = [], [], [], []
    for d in range(RING):
        n_block = jnp.concatenate(n_pieces[d], 0)
        dy_block = jnp.concatenate(dy_pieces[d], 0)
        grad_hidden = dot_nt(dy_block, down_w)
        pre = dot(n_block, gu_w)
        gate, up = pre[:, :units], pre[:, units:]
        sigma = jax.nn.sigmoid(gate)
        activated = gate * sigma
        hidden = (activated * up).astype(bf16)
        grad_gate = (grad_hidden * up * sigma * (1.0 + gate * (1.0 - sigma))).astype(bf16)
        grad_up = (grad_hidden * activated).astype(bf16)
        grad_gu = jnp.concatenate([grad_gate, grad_up], 1)
        grad_n = dot_nt(grad_gu, gu_w).astype(bf16)
        down = dot(hidden, down_w).astype(bf16)
        grad_parts.append([grad_n[k * chunk : (k + 1) * chunk] for k in range(kv_count)])
        out_parts.append([down[k * chunk : (k + 1) * chunk] for k in range(kv_count)])
        n_blocks.append(n_block)
        dy_blocks.append(dy_block)
        hidden_blocks.append(hidden)
        gu_blocks.append(grad_gu)
    grad_n2 = token_sum(grad_parts, pair).astype(f32)
    gain_grad_two, grad_mid_norm = norm_back(middle, scale_two, gain_two, grad_n2)
    grad_middle = own_dy.astype(f32) + grad_mid_norm
    grad_branch = grad_middle.astype(bf16)

    ffn_out = token_sum(out_parts, pair).astype(f32)
    own_out = (middle + ffn_out).astype(bf16)
    output = placed(kv_gather(own_out), nears)[None]

    grad_gu_w = dot_tn(jnp.concatenate(n_blocks, 0), jnp.concatenate(gu_blocks, 0)).astype(bf16)
    grad_down_w = dot_tn(jnp.concatenate(hidden_blocks, 0), jnp.concatenate(dy_blocks, 0)).astype(bf16)
    gu_parts = [block(grad_gu_w, i, depth) for i in order]
    down_parts = [block(grad_down_w, beside ^ i, units_each) for i in range(pair)]
    bit = pair // 2
    while bit:
        for i in range(count):
            if i % pair < bit:
                gu_parts[i] = add_low(gu_parts[i], trade(gu_parts[i + bit], "seq", bit))
        down_parts = [
            add_low(down_parts[i], trade(down_parts[i + bit], "seq", bit)) for i in range(bit)
        ]
        bit //= 2
    grad_w_down = down_parts[0].astype(f32)
    gate_cols = []
    for d in range(RING):
        own_part = gu_parts[d * pair]
        gate_cols.append(own_part if d == 0 else trade(own_part, "seq", d * pair))
    grad_w_gate = jnp.zeros(gate_weight.shape, f32)
    grad_w_up = jnp.zeros(up_weight.shape, f32)
    for d in range(RING):
        at = (along ^ d) * units
        grad_w_gate = lax.dynamic_update_slice_in_dim(grad_w_gate, gate_cols[d][:, :units].astype(f32), at, 1)
        grad_w_up = lax.dynamic_update_slice_in_dim(grad_w_up, gate_cols[d][:, units:].astype(f32), at, 1)

    branch_pieces = kv_gather(grad_branch)
    lora_pieces = [wide(dot_nt(g, out_up).astype(bf16), chunk, 128) for g in branch_pieces]
    grad_attended = placed(
        [dot_nt(jnp.concatenate([g, l], 1), out_ext) for g, l in zip(branch_pieces, lora_pieces)], nears
    )
    chunks_all = jnp.concatenate(chunks, 0)
    branch_all = jnp.concatenate(branch_pieces, 0)
    grad_out_w = dot_tn(chunks_all, branch_all).astype(bf16)
    grad_out_down = dot_tn(chunks_all, jnp.concatenate(lora_pieces, 0))[:, :rank]
    grad_out_up = dot_tn(lora_out, grad_branch)
    out_stack = jnp.stack([block(grad_out_w, i, rows_out) for i in order])
    grad_w_out = seq_halves(out_stack).astype(f32)

    grad_groups = grad_attended.reshape(length, kv_heads, group, head_size)
    grad_top, grad_under, grad_state, grad_norm = attend_state_back(feat_groups, top, under, grad_groups)
    later = earlier_sum(
        jnp.concatenate([grad_state, jnp.pad(grad_norm[..., None], ((0, 0), (0, 0), (0, 63)))], -1), "seq", -1
    )
    grad_query_s, grad_qfeat, grad_key_ext, grad_value_ext, grad_kfeat = attend_back(
        query_groups, feat_groups, key_ext, value_ext, key_feat, states, norms, window, early, grad_top, grad_under, is_early
    )
    later_low = later[..., :head_size].astype(bf16)
    later_norms = later[..., head_size]
    grad_kfeat = (
        grad_kfeat
        + jnp.einsum("kfd,jkd->jkf", later_low, value_head, preferred_element_type=f32)
        + later_norms[None]
    )
    grad_kfeat = jnp.where(key_mask, grad_kfeat, 0.0)
    extra = jnp.einsum("jkf,kfd->jkd", key_feat, later_low, preferred_element_type=f32)
    grad_value_ext = grad_value_ext + jnp.pad(extra, ((0, WIN), (0, 0), (0, 0)))
    key_from_feat, grad_fk = feature_back(key_ext[:length], fk_w, key_mix, grad_kfeat)
    grad_key_ext = grad_key_ext + jnp.pad(key_from_feat, ((0, WIN), (0, 0), (0, 0)))
    query_from_feat, grad_fq = feature_back(
        query, fq_w, query_mix, grad_qfeat.reshape(length, heads, 2 * head_size)
    )
    grad_queries = grad_query_s.reshape(length, heads, head_size) + query_from_feat
    grad_kv_ext = jnp.concatenate(
        [grad_key_ext.reshape(-1, kv_cols), grad_value_ext.reshape(-1, kv_cols)], 1
    )
    returned = moved(grad_kv_ext[:WIN].astype(bf16), "seq", -1).astype(f32)
    grad_kv = grad_kv_ext[WIN:] + jnp.pad(returned, ((length - WIN, 0), (0, 0)))
    grad_qkv = jnp.concatenate([grad_queries.reshape(length, q_cols), grad_kv], 1).astype(bf16)

    lora = lora_ext[WIN:]
    grad_lora = dot_nt(grad_qkv, ups).astype(bf16)
    grad_ext = jnp.concatenate([grad_qkv, grad_lora], 1)
    grad_normed_part = dot_nt(grad_ext, full)
    gain_part = jnp.sum(grad_normed_part * extended[WIN:] * scale_one, 0)
    low_part = grad_normed_part.astype(bf16)
    grad_normed = kv_sum([block(low_part, k, chunk) for k in nears])
    own_scale = block(scale_one, lane, chunk)
    unused_gain, grad_resid = norm_back(own_tokens, own_scale, gain_one, grad_normed)
    own_grad = lax.optimization_barrier((grad_middle + grad_resid).astype(bf16))
    grad_tokens = placed([g.astype(f32) for g in kv_gather(own_grad)], nears)[None]

    grad_qkv_w = dot_tn(normed, grad_qkv).astype(bf16)
    grad_w = seq_scatter([block(grad_qkv_w, i, depth) for i in order], pair)
    grad_w_query = grad_w[:, :q_cols]
    grad_w_kv = jnp.stack([grad_w[:, q_cols : q_cols + kv_cols], grad_w[:, q_cols + kv_cols :]])

    grad_up_all = dot_tn(lora[:, :lora_cols], grad_qkv)
    grad_lora_down = dot_tn(grad_lora, normed)[:lora_cols]
    fq_part = jnp.transpose(
        grad_fq.reshape(heads, count, -1, head_size), (1, 0, 2, 3)
    ).reshape(count, small_rows, head_size)
    down_part = grad_out_down.reshape(count, small_rows, rank)
    fk_part = jnp.transpose(
        grad_fk.reshape(kv_heads, count, -1, head_size), (1, 0, 2, 3)
    ).reshape(count, fk_rows, head_size)
    kv_up_part = jnp.transpose(
        jnp.stack(
            [
                grad_up_all[rank : 2 * rank, q_cols : q_cols + kv_cols],
                grad_up_all[2 * rank :, q_cols + kv_cols :],
            ]
        ).reshape(2, rank, count, kv_each),
        (2, 0, 1, 3),
    ).reshape(count, up_rows, kv_each)
    q_up_part = jnp.transpose(grad_up_all[:rank, :q_cols].reshape(rank, count, q_each), (1, 0, 2))
    vec_part = jnp.concatenate(
        [grad_lora_down, grad_out_up, gain_grad_two[None], gain_part[None]], 0
    )
    vec_count = vec_part.shape[0]
    vec_part = jnp.transpose(vec_part.reshape(vec_count, count, depth), (1, 0, 2)).reshape(
        count, -1, 64
    )
    more_rows = vec_part.shape[1]

    def lanes(a):
        return jnp.pad(a, ((0, 0), (0, 0), (0, 128 - a.shape[2])))

    small_part = jnp.concatenate(
        [
            lanes(jnp.concatenate([fq_part, down_part], 2)),
            lanes(fk_part),
            lanes(jnp.concatenate([kv_up_part, jnp.pad(q_up_part, ((0, 0), (0, rank), (0, 0)))], 2)),
            lanes(vec_part),
        ],
        1,
    ).astype(bf16)
    small_part = jnp.take(small_part, jnp.stack(order), 0)
    small_sum = seq_halves(small_part).astype(f32)
    at = small_rows
    grad_fmap_query = small_sum[:at, :head_size].reshape(query_feature_matrix.shape)
    grad_lora_down_out = small_sum[:at, head_size : head_size + rank]
    grad_fmap_key = small_sum[at : at + fk_rows, :head_size].reshape(key_feature_matrix.shape)
    at += fk_rows
    grad_lora_up_kv = small_sum[at : at + up_rows, :kv_each].reshape(2, rank, kv_each)
    grad_lora_up_query = small_sum[at : at + rank, kv_each : kv_each + q_each]
    at += up_rows
    vec_sum = kv_total(small_sum[at : at + more_rows, :64]).reshape(vec_count, depth)
    grad_lora_down = jnp.transpose(vec_sum[:lora_cols].reshape(3, rank, depth), (0, 2, 1))
    grad_lora_up_out = vec_sum[lora_cols : lora_cols + rank]
    grad_g_mlp = vec_sum[lora_cols + rank]
    grad_g_attn = vec_sum[lora_cols + rank + 1]
    return (
        output,
        grad_tokens,
        grad_g_attn,
        grad_w_query,
        grad_w_kv,
        grad_w_out,
        grad_lora_down,
        grad_lora_up_query,
        grad_lora_up_kv,
        grad_lora_down_out,
        grad_lora_up_out,
        grad_fmap_query,
        grad_fmap_key,
        grad_g_mlp,
        grad_w_gate,
        grad_w_up,
        grad_w_down,
    )


def solution(mesh):
    return jax.shard_map(
        per_device,
        mesh=mesh,
        in_specs=(
            P(None, "seq", None),
            P("seq"),
            P("seq", "kv"),
            P(None, "seq", "kv"),
            P(("kv", "seq"), None),
            P(None, "seq", None),
            P(None, ("kv", "seq")),
            P(None, None, ("kv", "seq")),
            P(("kv", "seq"), None),
            P(None, "seq"),
            P("kv", "seq", None),
            P("kv", "seq", None),
            P("seq"),
            P("seq", "kv"),
            P("seq", "kv"),
            P(("kv", "seq"), None),
            P(None, "seq", None),
        ),
        out_specs=(
            P(None, "seq", None),
            P(None, "seq", None),
            P("seq"),
            P("seq", "kv"),
            P(None, "seq", "kv"),
            P(("kv", "seq"), None),
            P(None, "seq", None),
            P(None, ("kv", "seq")),
            P(None, None, ("kv", "seq")),
            P(("kv", "seq"), None),
            P(None, "seq"),
            P("kv", "seq", None),
            P("kv", "seq", None),
            P("seq"),
            P("seq", "kv"),
            P("seq", "kv"),
            P(("kv", "seq"), None),
        ),
        check_vma=False,
    )
```

time: 2110 us -> 875 us (0.41)
  waiting for transfers between devices: 1400 us -> 289 us
  blocking collectives: 382 us -> 0 us
  starting transfers between devices: 8.17 us -> 194 us
  local copies, waits for them, and re-layouts: 39.4 us -> 134 us
    reduce_scatter x8 -> x0, waiting for transfers between devices: 719 us -> none  [the longest x1 150 us: per_device(): lax.psum_scatter(grad_gate_w.astype(jnp.bfloat16), 'seq', scatter_dimensi...]
    all_gather x6 -> x0, waiting for transfers between devices: 348 us -> none  [the longest x1 118 us: per_device(): lax.all_gather(gate_weight, 'seq', axis=0, tiled=True)]
    ppermute x2 -> x126, waiting for transfers between devices: 0.01 us -> 289 us  [the longest x116 280 us: trade(): return lax.ppermute(array, axis, [(i, i ^ mask) for i in range(count)])]
    all_gather x13 -> x0, blocking collectives: 272 us -> none  [the longest x2 40.6 us: prefix_2(): lax.all_gather(a.astype(kind), axis)]
    ppermute x2 -> x126, starting transfers between devices: 6.85 us -> 194 us  [the longest x116 144 us: trade(): return lax.ppermute(array, axis, [(i, i ^ mask) for i in range(count)])]
    psum x3 -> x0, waiting for transfers between devices: 173 us -> none  [the longest x1 88.6 us: per_device(): lax.psum(down_terms.astype(jnp.bfloat16), 'kv').astype(jnp.float32)]
    unnamed x25 -> x0, waiting for transfers between devices: 163 us -> none
    psum x2 -> x0, blocking collectives: 81.6 us -> none  [the longest x1 60.4 us: per_device(): lax.psum((jnp.dot(attended_token_rows, out_w, preferred_element_type=jnp....]
  transfers between devices with their start and end apart: 23 -> 126, of which waited for: 16 -> 40; matrix products, arithmetic and copies ran while one was open for 8% -> 41% of each run, Pallas kernels for 0% -> 0%
where the time goes in v1:
time: 875 us; the launch traced here: 858 us
  waiting for transfers between devices  289 us (33%)
  starting transfers between devices  194 us (22%)
  matrix products  170 us (19%)
  local copies, waits for them, and re-layouts  134 us (15%)
  other arithmetic  67 us (8%)
    ppermute x116, waiting for transfers between devices, trade(): return lax.ppermute(array, axis, [(i, i ^ mask) for i in range(count)])  280 us
    ppermute x116, starting transfers between devices, trade(): return lax.ppermute(array, axis, [(i, i ^ mask) for i in range(count)])  144 us
    dot_general x18, matrix products, dot_nt(): lax.dot_general(a, b, (((1,), (1,)), ((), ())), preferred_element_type=f32)  51.6 us
    ppermute x10, starting transfers between devices, moved(): return lax.ppermute(array, axis, pairs)  49.3 us
    unnamed x426, local copies, waits for them, and re-layouts  46.4 us
    dot_general x15, matrix products, dot(): return jnp.dot(a, b, preferred_element_type=f32)  34.8 us
    dot_general x8, matrix products, dot_tn(): lax.dot_general(a, b, (((0,), (0,)), ((), ())), preferred_element_type=f32)  33.9 us
    dynamic_update_slice x27, local copies, waits for them, and re-layouts, placed(): result = lax.dynamic_update_slice_in_dim(result, piece, at * rows, 0)  23.5 us
  transfers between devices with their start and end apart: 126, of which 40 were waited for; matrix products, arithmetic and copies ran while one was open for 41% of the time, Pallas kernels for 0%

profile of v1, /device:TPU:9, one launch (start us, length us, event | category | flops | bytes accessed | tf_op | source)
XLA Modules:
  0.0 858.1 jit_solution(8153041587255781375)
XLA Ops:
  63.4 35.3 %collective-permute-done.14 = bf16[64,2048]{1,0:T(8,128)(2,1)S(1)} collective-permute-done((bf16[64,2048]{1,0:T(8,128)(2,1)}, bf16[64,2048]{1,0:T(8,128)(2,1)S(1)}, u32[]{:S(2)}, u32[]{:S(2)}) %collective-permute-start.14) | collective-permute-done | bytes 262176 | tf_op jit(solution)/shard_map/ppermute | solution.py:15
  112.9 22.2 %collective-permute-done.6 = bf16[256,896]{1,0:T(8,128)(2,1)S(1)} collective-permute-done((bf16[256,896]{1,0:T(8,128)(2,1)S(1)}, bf16[256,896]{1,0:T(8,128)(2,1)S(1)}, u32[]{:S(2)}, u32[]{:S(2)}) %collective-permute-start.6) | collective-permute-done | bytes 458784 | tf_op jit(solution)/shard_map/ppermute | solution.py:15
  163.9 7.2 fusion.357
  206.9 6.5 fusion.7
  248.6 19.9 %collective-permute-done.15 = bf16[512,2048]{1,0:T(8,128)(2,1)S(1)} collective-permute-done((bf16[512,2048]{1,0:T(8,128)(2,1)}, bf16[512,2048]{1,0:T(8,128)(2,1)S(1)}, u32[]{:S(2)}, u32[]{:S(2)}) %collective-permute-start.15) | collective-permute-done | bytes 2097184 | tf_op jit(solution)/shard_map/ppermute | solution.py:15
  284.4 9.1 %collective-permute-done.18 = bf16[128,2176]{1,0:T(8,128)(2,1)S(1)} collective-permute-done((bf16[128,2176]{1,0:T(8,128)(2,1)S(1)}, bf16[128,2176]{1,0:T(8,128)(2,1)S(1)}, u32[]{:S(2)}, u32[]{:S(2)}) %collective-permute-start.18) | collective-permute-done | bytes 557088 | tf_op jit(solution)/shard_map/ppermute | solution.py:15
  310.1 12.3 %collective-permute-done.32 = bf16[128,2048]{1,0:T(8,128)(2,1)S(1)} collective-permute-done((bf16[128,2048]{1,0:T(8,128)(2,1)S(1)}, bf16[128,2048]{1,0:T(8,128)(2,1)S(1)}, u32[]{:S(2)}, u32[]{:S(2)}) %collective-permute-start.32) | collective-permute-done | bytes 524320 | tf_op jit(solution)/shard_map/ppermute | solution.py:15
  408.3 14.8 %fusion.28 = bf16[2048,1024]{1,0:T(8,128)(2,1)S(1)} fusion(bf16[2048,2048]{1,0:T(8,128)(2,1)} %constant_dynamic-update-slice_fusion.5, bf16[512,512]{1,0:T(8,128)(2,1)} %copy-done.189, bf16[512,512]{1,0:T(8,128)(2,1)} %copy-done.188, bf16[512,512]{1,0:T(8,128)(2,1)} %copy-done.187, bf16[512,512]{1,0:T(8,128)(2,1)} %copy-done.186, ...), kind=kOutput, calls=%fused_computation.38 | convolution fusion | flops 8625586176 | bytes 16777216 | tf_op jit(solution)/shard_map/dot_general | solution.py:48
  424.6 8.5 convolution_convert_fusion.9
  448.7 10.1 %collective-permute-done.121 = bf16[256,1024]{1,0:T(8,128)(2,1)S(1)} collective-permute-done((bf16[256,1024]{1,0:T(8,128)(2,1)S(1)}, bf16[256,1024]{1,0:T(8,128)(2,1)S(1)}, u32[]{:S(2)}, u32[]{:S(2)}) %collective-permute-start.121) | collective-permute-done | bytes 524320 | tf_op jit(solution)/shard_map/ppermute | solution.py:15
  460.3 9.7 %collective-permute-done.123 = bf16[256,1024]{1,0:T(8,128)(2,1)S(1)} collective-permute-done((bf16[256,1024]{1,0:T(8,128)(2,1)S(1)}, bf16[256,1024]{1,0:T(8,128)(2,1)S(1)}, u32[]{:S(2)}, u32[]{:S(2)}) %collective-permute-start.123) | collective-permute-done | bytes 524320 | tf_op jit(solution)/shard_map/ppermute | solution.py:15
  483.0 9.5 %collective-permute-done.125 = bf16[256,2048]{1,0:T(8,128)(2,1)S(1)} collective-permute-done((bf16[256,2048]{1,0:T(8,128)(2,1)S(1)}, bf16[256,2048]{1,0:T(8,128)(2,1)S(1)}, u32[]{:S(2)}, u32[]{:S(2)}) %collective-permute-start.125) | collective-permute-done | bytes 1048608 | tf_op jit(solution)/shard_map/ppermute | solution.py:15
  497.5 7.0 collective-permute-done.53
  506.3 10.1 %collective-permute-done.120 = bf16[256,1024]{1,0:T(8,128)(2,1)S(1)} collective-permute-done((bf16[256,1024]{1,0:T(8,128)(2,1)S(1)}, bf16[256,1024]{1,0:T(8,128)(2,1)S(1)}, u32[]{:S(2)}, u32[]{:S(2)}) %collective-permute-start.120) | collective-permute-done | bytes 524320 | tf_op jit(solution)/shard_map/ppermute | solution.py:15
  537.9 8.9 %collective-permute-done.124 = bf16[256,1024]{1,0:T(8,128)(2,1)S(1)} collective-permute-done((bf16[256,1024]{1,0:T(8,128)(2,1)S(1)}, bf16[256,1024]{1,0:T(8,128)(2,1)S(1)}, u32[]{:S(2)}, u32[]{:S(2)}) %collective-permute-start.124) | collective-permute-done | bytes 524320 | tf_op jit(solution)/shard_map/ppermute | solution.py:15
  547.0 15.4 %collective-permute-done.54 = bf16[128,2048]{1,0:T(8,128)(2,1)S(1)} collective-permute-done((bf16[128,2048]{1,0:T(8,128)(2,1)S(1)}, bf16[128,2048]{1,0:T(8,128)(2,1)S(1)}, u32[]{:S(2)}, u32[]{:S(2)}) %collective-permute-start.54) | collective-permute-done | bytes 524320 | tf_op jit(solution)/shard_map/ppermute | solution.py:15
  584.5 6.8 collective-permute-done.39
  693.9 6.7 fusion.150
  702.2 26.9 %collective-permute-start.96 = (bf16[64,256]{0,1:T(8,128)(2,1)S(1)}, bf16[64,256]{0,1:T(8,128)(2,1)S(1)}, u32[]{:S(2)}, u32[]{:S(2)}) collective-permute-start(bf16[64,256]{0,1:T(8,128)(2,1)S(1)} %fusion.246), channel_id=1, source_target_pairs={{4,0},{8,4},{12,8},{16,12},{20,16},{24,20},{28,24},{5,1},{9,5},{13... | collective-permute-start | bytes 98312 | tf_op jit(solution)/shard_map/ppermute | solution.py:21
  735.7 6.3 fusion.11
  759.0 6.1 collective-permute-start.104
  773.4 16.8 %collective-permute-done.105 = bf16[1,232,128]{2,1,0:T(8,128)(2,1)S(1)} collective-permute-done((bf16[1,232,128]{2,1,0:T(8,128)(2,1)S(1)}, bf16[1,232,128]{2,1,0:T(8,128)(2,1)S(1)}, u32[]{:S(2)}, u32[]{:S(2)}) %collective-permute-start.105) | collective-permute-done | bytes 59424 | tf_op jit(solution)/shard_map/ppermute | solution.py:15
  806.7 6.2 collective-permute-done.113
  828.8 14.3 %collective-permute-done.114 = bf16[256,768]{1,0:T(8,128)(2,1)S(1)} collective-permute-done((bf16[256,768]{1,0:T(8,128)(2,1)S(1)}, bf16[256,768]{1,0:T(8,128)(2,1)S(1)}, u32[]{:S(2)}, u32[]{:S(2)}) %collective-permute-start.114) | collective-permute-done | bytes 393248 | tf_op jit(solution)/shard_map/ppermute | solution.py:15
  (969 shorter events, 556.7 us)
Async XLA Ops:
  0.7 41.8 %collective-permute-start.13 = (bf16[64,2048]{1,0:T(8,128)(2,1)}, bf16[64,2048]{1,0:T(8,128)(2,1)}, u32[]{:S(2)}, u32[]{:S(2)}) collective-permute-start(bf16[64,2048]{1,0:T(8,128)(2,1)} %param.21), channel_id=1, source_target_pairs={{0,16},{4,20},{8,24},{12,28},{16,0},{20,4},{24,8},{28,12},{1,17},{... | collective-permute-start | bytes 786440 | tf_op jit(solution)/shard_map/ppermute | solution.py:15
  50.9 49.5 %collective-permute-start.23 = (bf16[256,1024]{1,0:T(8,128)(2,1)S(1)}, bf16[256,1024]{1,0:T(8,128)(2,1)S(1)}, u32[]{:S(2)}, u32[]{:S(2)}) collective-permute-start(bf16[256,1024]{1,0:T(8,128)(2,1)S(1)} %copy-done.82), channel_id=1, source_target_pairs={{0,8},{4,12},{8,0},{12,4},{16,24},{20,28},{24,16},{28,20},{1,9},{5... | collective-permute-start | bytes 1572872 | tf_op jit(solution)/shard_map/ppermute | solution.py:15
  55.3 47.1 %collective-permute-start.25 = (bf16[256,1024]{1,0:T(8,128)(2,1)S(1)}, bf16[256,1024]{1,0:T(8,128)(2,1)S(1)}, u32[]{:S(2)}, u32[]{:S(2)}) collective-permute-start(bf16[256,1024]{1,0:T(8,128)(2,1)S(1)} %copy-done.81), channel_id=1, source_target_pairs={{0,16},{4,20},{8,24},{12,28},{16,0},{20,4},{24,8},{28,12},{1,17},{... | collective-permute-start | bytes 1572872 | tf_op jit(solution)/shard_map/ppermute | solution.py:15
  58.1 46.0 %collective-permute-start.27 = (bf16[256,1024]{1,0:T(8,128)(2,1)S(1)}, bf16[256,1024]{1,0:T(8,128)(2,1)S(1)}, u32[]{:S(2)}, u32[]{:S(2)}) collective-permute-start(bf16[256,1024]{1,0:T(8,128)(2,1)S(1)} %copy-done.80), channel_id=1, source_target_pairs={{0,24},{4,28},{8,16},{12,20},{16,8},{20,12},{24,0},{28,4},{1,25},{... | collective-permute-start | bytes 1572872 | tf_op jit(solution)/shard_map/ppermute | solution.py:15
  147.3 86.8 %collective-permute-start.75 = (bf16[128,2048]{1,0:T(8,128)(2,1)}, bf16[128,2048]{1,0:T(8,128)(2,1)}, u32[]{:S(2)}, u32[]{:S(2)}) collective-permute-start(bf16[128,2048]{1,0:T(8,128)(2,1)} %collective-permute-done.73), channel_id=1, source_target_pairs={{0,2},{1,3},{2,0},{3,1},{4,6},{5,7},{6,4},{7,5},{8,10},{9,11},{10,... | collective-permute-start | bytes 1572872 | tf_op jit(solution)/shard_map/ppermute | solution.py:15
  151.6 79.2 %collective-permute-start.68 = (bf16[128,2048]{1,0:T(8,128)(2,1)}, bf16[128,2048]{1,0:T(8,128)(2,1)}, u32[]{:S(2)}, u32[]{:S(2)}) collective-permute-start(bf16[128,2048]{1,0:T(8,128)(2,1)} %collective-permute-done.67), channel_id=1, source_target_pairs={{0,1},{1,0},{2,3},{3,2},{4,5},{5,4},{6,7},{7,6},{8,9},{9,8},{10,11... | collective-permute-start | bytes 1572872 | tf_op jit(solution)/shard_map/ppermute | solution.py:15
  152.9 81.2 %collective-permute-start.82 = (bf16[128,2048]{1,0:T(8,128)(2,1)}, bf16[128,2048]{1,0:T(8,128)(2,1)}, u32[]{:S(2)}, u32[]{:S(2)}) collective-permute-start(bf16[128,2048]{1,0:T(8,128)(2,1)} %collective-permute-done.80), channel_id=1, source_target_pairs={{0,2},{1,3},{2,0},{3,1},{4,6},{5,7},{6,4},{7,5},{8,10},{9,11},{10,... | collective-permute-start | bytes 1572872 | tf_op jit(solution)/shard_map/ppermute | solution.py:15
  224.7 43.8 %collective-permute-start.15 = (bf16[512,2048]{1,0:T(8,128)(2,1)}, bf16[512,2048]{1,0:T(8,128)(2,1)S(1)}, u32[]{:S(2)}, u32[]{:S(2)}) collective-permute-start(bf16[512,2048]{1,0:T(8,128)(2,1)} %constant_dynamic-update-slice_fusion), channel_id=1, source_target_pairs={{0,4},{4,0},{8,12},{12,8},{16,20},{20,16},{24,28},{28,24},{1,5},{5... | collective-permute-start | bytes 6291464 | tf_op jit(solution)/shard_map/ppermute | solution.py:15
  225.5 52.0 %collective-permute-start.74 = (bf16[128,2048]{1,0:T(8,128)(2,1)}, bf16[128,2048]{1,0:T(8,128)(2,1)S(1)}, u32[]{:S(2)}, u32[]{:S(2)}) collective-permute-start(bf16[128,2048]{1,0:T(8,128)(2,1)} %collective-permute-done.73), channel_id=1, source_target_pairs={{0,1},{1,0},{2,3},{3,2},{4,5},{5,4},{6,7},{7,6},{8,9},{9,8},{10,11... | collective-permute-start | bytes 1572872 | tf_op jit(solution)/shard_map/ppermute | solution.py:15
  234.1 61.6 %collective-permute-start.81 = (bf16[128,2048]{1,0:T(8,128)(2,1)}, bf16[128,2048]{1,0:T(8,128)(2,1)S(1)}, u32[]{:S(2)}, u32[]{:S(2)}) collective-permute-start(bf16[128,2048]{1,0:T(8,128)(2,1)} %collective-permute-done.80), channel_id=1, source_target_pairs={{0,1},{1,0},{2,3},{3,2},{4,5},{5,4},{6,7},{7,6},{8,9},{9,8},{10,11... | collective-permute-start | bytes 1572872 | tf_op jit(solution)/shard_map/ppermute | solution.py:15
  234.1 47.6 %collective-permute-start.76 = (bf16[128,2048]{1,0:T(8,128)(2,1)}, bf16[128,2048]{1,0:T(8,128)(2,1)S(1)}, u32[]{:S(2)}, u32[]{:S(2)}) collective-permute-start(bf16[128,2048]{1,0:T(8,128)(2,1)} %collective-permute-done.75), channel_id=1, source_target_pairs={{0,1},{1,0},{2,3},{3,2},{4,5},{5,4},{6,7},{7,6},{8,9},{9,8},{10,11... | collective-permute-start | bytes 1572872 | tf_op jit(solution)/shard_map/ppermute | solution.py:15
  237.9 64.1 %collective-permute-start.83 = (bf16[128,2048]{1,0:T(8,128)(2,1)}, bf16[128,2048]{1,0:T(8,128)(2,1)S(1)}, u32[]{:S(2)}, u32[]{:S(2)}) collective-permute-start(bf16[128,2048]{1,0:T(8,128)(2,1)} %collective-permute-done.82), channel_id=1, source_target_pairs={{0,1},{1,0},{2,3},{3,2},{4,5},{5,4},{6,7},{7,6},{8,9},{9,8},{10,11... | collective-permute-start | bytes 1572872 | tf_op jit(solution)/shard_map/ppermute | solution.py:15
  350.1 43.0 %collective-permute-start.30 = (bf16[128,2048]{1,0:T(8,128)(2,1)S(1)}, bf16[128,2048]{1,0:T(8,128)(2,1)S(1)}, u32[]{:S(2)}, u32[]{:S(2)}) collective-permute-start(bf16[128,2048]{1,0:T(8,128)(2,1)S(1)} %get-tuple-element.151), channel_id=1, source_target_pairs={{0,1},{1,0},{2,3},{3,2},{4,5},{5,4},{6,7},{7,6},{8,9},{9,8},{10,11... | collective-permute-start | bytes 1572872 | tf_op jit(solution)/shard_map/ppermute | solution.py:15
  365.1 69.4 %collective-permute-start.70 = (bf16[128,2048]{1,0:T(8,128)(2,1)}, bf16[128,2048]{1,0:T(8,128)(2,1)}, u32[]{:S(2)}, u32[]{:S(2)}) collective-permute-start(bf16[128,2048]{1,0:T(8,128)(2,1)} %get-tuple-element.142), channel_id=1, source_target_pairs={{0,1},{1,0},{2,3},{3,2},{4,5},{5,4},{6,7},{7,6},{8,9},{9,8},{10,11... | collective-permute-start | bytes 1572872 | tf_op jit(solution)/shard_map/ppermute | solution.py:15
  387.0 49.7 %collective-permute-start.78 = (bf16[128,2048]{1,0:T(8,128)(2,1)}, bf16[128,2048]{1,0:T(8,128)(2,1)}, u32[]{:S(2)}, u32[]{:S(2)}) collective-permute-start(bf16[128,2048]{1,0:T(8,128)(2,1)} %get-tuple-element.145), channel_id=1, source_target_pairs={{0,1},{1,0},{2,3},{3,2},{4,5},{5,4},{6,7},{7,6},{8,9},{9,8},{10,11... | collective-permute-start | bytes 1572872 | tf_op jit(solution)/shard_map/ppermute | solution.py:15
  390.9 47.6 %collective-permute-start.37 = (bf16[128,2048]{1,0:T(8,128)(2,1)}, bf16[128,2048]{1,0:T(8,128)(2,1)}, u32[]{:S(2)}, u32[]{:S(2)}) collective-permute-start(bf16[128,2048]{1,0:T(8,128)(2,1)} %get-tuple-element.153), channel_id=1, source_target_pairs={{0,1},{1,0},{2,3},{3,2},{4,5},{5,4},{6,7},{7,6},{8,9},{9,8},{10,11... | collective-permute-start | bytes 1572872 | tf_op jit(solution)/shard_map/ppermute | solution.py:15
  393.1 47.8 %collective-permute-start.45 = (bf16[128,2048]{1,0:T(8,128)(2,1)}, bf16[128,2048]{1,0:T(8,128)(2,1)}, u32[]{:S(2)}, u32[]{:S(2)}) collective-permute-start(bf16[128,2048]{1,0:T(8,128)(2,1)} %get-tuple-element.155), channel_id=1, source_target_pairs={{0,1},{1,0},{2,3},{3,2},{4,5},{5,4},{6,7},{7,6},{8,9},{9,8},{10,11... | collective-permute-start | bytes 1572872 | tf_op jit(solution)/shard_map/ppermute | solution.py:15
  447.5 44.9 %collective-permute-start.125 = (bf16[256,2048]{1,0:T(8,128)(2,1)S(1)}, bf16[256,2048]{1,0:T(8,128)(2,1)S(1)}, u32[]{:S(2)}, u32[]{:S(2)}) collective-permute-start(bf16[256,2048]{1,0:T(8,128)(2,1)S(1)} %constant_dynamic-slice_fusion), channel_id=1, source_target_pairs={{0,4},{4,0},{8,12},{12,8},{16,20},{20,16},{24,28},{28,24},{1,5},{5... | collective-permute-start | bytes 3145736 | tf_op jit(solution)/shard_map/ppermute | solution.py:15
  473.5 48.6 %collective-permute-start.77 = (bf16[128,2048]{1,0:T(8,128)(2,1)S(1)}, bf16[128,2048]{1,0:T(8,128)(2,1)S(1)}, u32[]{:S(2)}, u32[]{:S(2)}) collective-permute-start(bf16[128,2048]{1,0:T(8,128)(2,1)S(1)} %copy-done.88), channel_id=1, source_target_pairs={{0,1},{1,0},{2,3},{3,2},{4,5},{5,4},{6,7},{7,6},{8,9},{9,8},{10,11... | collective-permute-start | bytes 1572872 | tf_op jit(solution)/shard_map/ppermute | solution.py:15
  523.8 43.9 %collective-permute-start.62 = (bf16[128,2048]{1,0:T(8,128)(2,1)S(1)}, bf16[128,2048]{1,0:T(8,128)(2,1)S(1)}, u32[]{:S(2)}, u32[]{:S(2)}) collective-permute-start(bf16[128,2048]{1,0:T(8,128)(2,1)S(1)} %copy-done.86), channel_id=1, source_target_pairs={{0,1},{1,0},{2,3},{3,2},{4,5},{5,4},{6,7},{7,6},{8,9},{9,8},{10,11... | collective-permute-start | bytes 1572872 | tf_op jit(solution)/shard_map/ppermute | solution.py:15
  618.9 60.1 %collective-permute-start.58 = (bf16[128,2048]{1,0:T(8,128)(2,1)}, bf16[128,2048]{1,0:T(8,128)(2,1)}, u32[]{:S(2)}, u32[]{:S(2)}) collective-permute-start(bf16[128,2048]{1,0:T(8,128)(2,1)} %collective-permute-done.57), channel_id=1, source_target_pairs={{0,1},{1,0},{2,3},{3,2},{4,5},{5,4},{6,7},{7,6},{8,9},{9,8},{10,11... | collective-permute-start | bytes 1572872 | tf_op jit(solution)/shard_map/ppermute | solution.py:15
  659.4 144.9 %collective-permute-start.115 = (bf16[4,64,2048]{2,1,0:T(8,128)(2,1)}, bf16[4,64,2048]{2,1,0:T(8,128)(2,1)}, u32[]{:S(2)}, u32[]{:S(2)}) collective-permute-start(bf16[4,64,2048]{2,1,0:T(8,128)(2,1)} %pad_maximum_fusion.1), channel_id=1, source_target_pairs={{0,16},{4,20},{8,24},{12,28},{16,0},{20,4},{24,8},{28,12},{1,17},{... | collective-permute-start | bytes 3145736 | tf_op jit(solution)/shard_map/ppermute | solution.py:15
  756.4 50.0 %collective-permute-start.111 = (bf16[256,768]{1,0:T(8,128)(2,1)}, bf16[256,768]{1,0:T(8,128)(2,1)}, u32[]{:S(2)}, u32[]{:S(2)}) collective-permute-start(bf16[256,768]{1,0:T(8,128)(2,1)} %get-tuple-element.116), channel_id=1, source_target_pairs={{0,4},{4,0},{8,12},{12,8},{16,20},{20,16},{24,28},{28,24},{1,5},{5... | collective-permute-start | bytes 1179656 | tf_op jit(solution)/shard_map/ppermute | solution.py:15
  768.3 55.5 %collective-permute-start.108 = (bf16[256,768]{1,0:T(8,128)(2,1)}, bf16[256,768]{1,0:T(8,128)(2,1)}, u32[]{:S(2)}, u32[]{:S(2)}) collective-permute-start(bf16[256,768]{1,0:T(8,128)(2,1)} %get-tuple-element.114), channel_id=1, source_target_pairs={{0,4},{4,0},{8,12},{12,8},{16,20},{20,16},{24,28},{28,24},{1,5},{5... | collective-permute-start | bytes 1179656 | tf_op jit(solution)/shard_map/ppermute | solution.py:15
  (298 other events, 5191.2 us)

commit v2 on v1

v2 whole, which is shorter than its diff:
```python
import functools

import jax
import jax.numpy as jnp
from jax import lax
from jax.experimental import pallas as pl
from jax.experimental.pallas import tpu as pltpu
from jax.sharding import Mesh, PartitionSpec as P

WIN = 64
RING = 4
SEQ = ("ring", "pair")
STEP = 128
SMALL = 80
LANES = 128
epsilon = 1e-05
bf16 = jnp.bfloat16
f32 = jnp.float32
shape = jax.ShapeDtypeStruct


def trade(array, axis, mask):
    count = lax.axis_size(axis)
    return lax.ppermute(array, axis, [(i, i ^ mask) for i in range(count)])


def moved(array, axis, by):
    count = lax.axis_size(axis)
    pairs = [(i, i + by) for i in range(count) if 0 <= i + by < count]
    return lax.ppermute(array, axis, pairs)


def after(value, *earlier):
    return lax.optimization_barrier((value,) + earlier)[0]


def dot(a, b):
    return jnp.dot(a, b, preferred_element_type=f32)


def dot_nt(a, b):
    return lax.dot_general(a, b, (((1,), (1,)), ((), ())), preferred_element_type=f32)


def dot_tn(a, b):
    return lax.dot_general(a, b, (((0,), (0,)), ((), ())), preferred_element_type=f32)


def add_low(a, b):
    return (a.astype(f32) + b.astype(f32)).astype(bf16)


def block(array, at, rows, axis=0):
    return lax.dynamic_slice_in_dim(array, at * rows, rows, axis)


def own_call(body, outs, inputs, scalars=0, scratch=(), flops=0, room=8, deps=(), hbm=0):
    count, deps = len(inputs), list(deps)

    def run(*refs):
        body(*refs[:count], *refs[count + len(deps) :])

    vmem = pl.BlockSpec(memory_space=pltpu.VMEM)
    smem = pl.BlockSpec(memory_space=pltpu.SMEM)
    size = sum(a.size * a.dtype.itemsize for a in list(inputs)[: count - hbm] + list(outs))
    return pl.pallas_call(
        run,
        out_shape=tuple(outs),
        in_specs=[smem] * scalars
        + [vmem] * (count - scalars - hbm)
        + [pl.BlockSpec(memory_space=pl.ANY)] * (hbm + len(deps)),
        out_specs=tuple(vmem for _ in outs),
        scratch_shapes=list(scratch),
        compiler_params=pltpu.CompilerParams(vmem_limit_bytes=size + room * 2**20),
        cost_estimate=pl.CostEstimate(flops=flops, bytes_accessed=0, transcendentals=0),
    )(*inputs, *deps)


def placed(pieces, rows, order, extra=None, outs=(), more=(), deps=()):
    count = len(pieces)

    def body(order_ref, *refs):
        refs = refs[: count + len(more)] + refs[count + len(more) + len(deps) :]
        out, sems = refs[count + len(more)], refs[-1]
        copies = []
        i = 0
        for piece in refs[:count]:
            for inner in range(0, piece.shape[0], rows):
                at = pl.multiple_of(order_ref[i] * rows, rows)
                copies.append(
                    pltpu.make_async_copy(piece.at[pl.ds(inner, rows)], out.at[pl.ds(at, rows)], sems.at[i])
                )
                copies[-1].start()
                i += 1
        for copy in copies:
            copy.wait()
        if extra is not None:
            extra(out, *refs[count : count + len(more)], *refs[count + len(more) + 1 : -1])

    vmem = pl.BlockSpec(memory_space=pltpu.VMEM)
    total = sum(p.shape[0] for p in pieces)
    result = pl.pallas_call(
        body,
        out_shape=(shape((total, pieces[0].shape[1]), pieces[0].dtype),) + tuple(outs),
        in_specs=[pl.BlockSpec(memory_space=pltpu.SMEM)]
        + [pl.BlockSpec(memory_space=pl.ANY)] * count
        + [vmem] * len(more)
        + [pl.BlockSpec(memory_space=pl.ANY)] * len(deps),
        out_specs=(vmem,) * (1 + len(outs)),
        scratch_shapes=[pltpu.SemaphoreType.DMA((total // rows,))],
        compiler_params=pltpu.CompilerParams(vmem_limit_bytes=16 * 2**20),
        cost_estimate=pl.CostEstimate(flops=0, bytes_accessed=0, transcendentals=0),
    )(jnp.stack(order).astype(jnp.int32), *pieces, *more, *deps)
    return result if outs else result[0]


def rows_placed(order_ref, *refs):
    out = refs[-1]
    each = STEP
    at = 0
    for ref in refs[:-1]:
        for inner in range(0, ref.shape[0], each):
            to = pl.multiple_of(order_ref[at] * each, each)
            out[pl.ds(to, each)] = ref[inner : inner + each].astype(out.dtype)
            at += 1


def pack_weights(*refs):
    q_hbm, kv_hbm = refs[:2]
    number = (len(refs) - 4) // 2
    out_ref, held, sems = refs[2 + number], refs[3 + number : -1], refs[-1]
    depth, q_cols = q_hbm.shape
    kv_cols = kv_hbm.shape[2]
    moves = [(q_hbm, out_ref.at[:, :q_cols])]
    for c in range(2):
        moves.append((kv_hbm.at[c], out_ref.at[:, pl.ds(q_cols + c * kv_cols, kv_cols)]))
    moves += list(zip(refs[2 : 2 + number], held))
    copies = [pltpu.make_async_copy(a, b, sems.at[i]) for i, (a, b) in enumerate(moves)]
    for copy in copies:
        copy.start()
    for copy in copies:
        copy.wait()
    down_ref, fq_ref, outd_ref, fk_ref, kvup_ref, qup_ref, gain_ref, outu_ref = held
    lora = down_ref.shape[0] * down_ref.shape[1]
    rank = down_ref.shape[1]
    size = fq_ref.shape[1]

    def wide(value, rows, cols):
        value = value.astype(f32)
        if value.shape[1] < cols:
            value = jnp.concatenate([value, jnp.zeros((value.shape[0], cols - value.shape[1]), f32)], 1)
        if value.shape[0] < rows:
            value = jnp.concatenate([value, jnp.zeros((rows - value.shape[0], cols), f32)], 0)
        return value

    downs = [wide(down_ref[c], rank, depth) for c in range(down_ref.shape[0])]
    gap = jnp.zeros((size, depth), f32)
    outd = wide(outd_ref[...], rank, depth)
    rest = jnp.zeros((LANES - lora - size - rank, depth), f32)
    tall = jnp.concatenate(downs + [gap, outd, rest], 0)
    groups = [
        wide(fq_ref[...], fq_ref.shape[0], SMALL),
        wide(fk_ref[...], 16, SMALL),
        wide(jnp.concatenate([kvup_ref[...].astype(f32), wide(qup_ref[...], 2 * rank, qup_ref.shape[1])], 1), 16, SMALL),
    ]
    vec = jnp.concatenate(
        [gain_ref[...].astype(f32), outu_ref[...].astype(f32)], 0
    )
    for at in range(0, depth, 64):
        groups.append(wide(vec[:, at : at + 64], 16, SMALL))
    small = wide(jnp.concatenate(groups, 0), depth, SMALL)
    small = jnp.concatenate(
        [jnp.zeros((depth, lora), f32), small, jnp.zeros((depth, LANES - lora - SMALL), f32)], 1
    )
    out_ref[:, q_cols + 2 * kv_cols :] = (tall.T + small).astype(bf16)


def unpack_weights(full_ref, fq_ref, fk_ref, ups_ref, outd_ref, vec_ref, *, count):
    depth = full_ref.shape[0] // count
    all_cols = full_ref.shape[1] - LANES
    heads, size = fq_ref.shape[0], fq_ref.shape[2]
    kv_heads = fk_ref.shape[0]
    rank = vec_ref.shape[0] - 8
    each = size // count
    lora = 3 * rank
    q_cols = heads * size
    kv_cols = kv_heads * size
    q_each, kv_each = q_cols // count, kv_cols // count
    fq_rows = heads * each
    ups_ref[...] = jnp.zeros_like(ups_ref)
    outd_ref[...] = jnp.zeros_like(outd_ref)
    vec_ref[...] = jnp.zeros_like(vec_ref)
    for s in range(count):
        part = full_ref[s * depth : (s + 1) * depth, all_cols:].astype(f32)
        small = part[:, lora : lora + SMALL]
        for h in range(heads):
            fq_ref[h, s * each : (s + 1) * each] = small[h * each : (h + 1) * each, :size]
        outd_ref[s * fq_rows : (s + 1) * fq_rows, :rank] = small[:fq_rows, size : size + rank]
        at = fq_rows
        for h in range(kv_heads):
            fk_ref[h, s * each : (s + 1) * each] = small[at + h * each : at + (h + 1) * each, :size]
        at += 16
        ups_ref[:rank, s * q_each : (s + 1) * q_each] = small[at : at + rank, kv_each : kv_each + q_each]
        for c in range(2):
            to = q_cols + c * kv_cols + s * kv_each
            ups_ref[(c + 1) * rank : (c + 2) * rank, to : to + kv_each] = small[
                at + c * rank : at + (c + 1) * rank, :kv_each
            ]
        at += 16
        for q in range(depth // 64):
            to = s * depth + q * 64
            vec_ref[:, to : to + 64] = small[at : at + 16, :64]
            at += 16


def cut_units(at_ref, gate_ref, up_ref, *outs):
    units = outs[0].shape[1] // 2
    for i, out in enumerate(outs):
        at = pl.multiple_of(at_ref[i] * units, units)
        out[:, :units] = gate_ref[:, pl.ds(at, units)]
        out[:, units:] = up_ref[:, pl.ds(at, units)]


def place_units(at_ref, *refs):
    gate_ref, up_ref = refs[-2:]
    units = refs[0].shape[1] // 2
    for i, ref in enumerate(refs[:-2]):
        at = pl.multiple_of(at_ref[i] * units, units)
        gate_ref[:, pl.ds(at, units)] = ref[:, :units].astype(f32)
        up_ref[:, pl.ds(at, units)] = ref[:, units:].astype(f32)


def softmax_pair(mixing):
    up = jnp.exp(mixing - jnp.max(mixing, -1, keepdims=True))
    down = jnp.exp(jnp.min(mixing, -1, keepdims=True) - mixing)
    up = up / jnp.sum(up, -1, keepdims=True)
    down = down / jnp.sum(down, -1, keepdims=True)
    return jnp.concatenate([up, down], -1).astype(bf16)


def softmax_pair_back(feat, grad):
    size = feat.shape[1] // 2
    feat = feat.astype(f32)
    term = feat * grad.astype(bf16).astype(f32)
    is_up = lax.broadcasted_iota(jnp.int32, term.shape, 1) < size
    up_sum = jnp.sum(jnp.where(is_up, term, 0.0), -1, keepdims=True)
    down_sum = jnp.sum(jnp.where(is_up, 0.0, term), -1, keepdims=True)
    term = term - feat * jnp.where(is_up, up_sum, down_sum)
    return (term[:, :size] - term[:, size:]).astype(bf16)


def with_ones(values, ones):
    rows, size = values.shape
    column = lax.broadcasted_iota(jnp.int32, (rows, size), 1)
    return jnp.concatenate([values, jnp.where(column < ones, 1.0, 0.0).astype(values.dtype)], 1)


def split_column(wide, size):
    column = lax.broadcasted_iota(jnp.int32, wide.shape, 1)
    total = wide[:, size : size + 1]
    high = total.astype(bf16).astype(f32)
    wide = jnp.where(column == size, high, wide)
    return jnp.where(column == size + 1, total - high, wide).astype(bf16)


def inverse_rms(values):
    return lax.rsqrt(jnp.mean(values * values, -1, keepdims=True) + epsilon)


def project(
    place_ref, halo_ref, tokens_ref, full_ref, vec_ref, ups_ref, fk_ref,
    normed_ref, lora_ref, query_ref, kv_ref, feat_ref, total_ref, *, size
):
    length = tokens_ref.shape[0]
    all_cols = ups_ref.shape[1]
    q_cols = query_ref.shape[1]
    gain = vec_ref[0:1]
    ups = ups_ref[...].astype(bf16)
    step = 192
    for at in range(0, length + WIN, step):
        if at == 0:
            rows = jnp.concatenate([halo_ref[...], tokens_ref[: step - WIN]], 0).astype(f32)
        else:
            rows = tokens_ref[at - WIN : at - WIN + step].astype(f32)
        normed = (rows * inverse_rms(rows) * gain).astype(bf16)
        wide = dot(normed, full_ref[...])
        lora = wide[:, all_cols:].astype(bf16)
        qkv = (wide[:, :all_cols] + dot(lora, ups)).astype(bf16)
        kv_ref[at : at + step] = qkv[:, q_cols:]
        skip = WIN if at == 0 else 0
        to = slice(at - WIN + skip, at - WIN + step)
        normed_ref[to] = normed[skip:]
        lora_ref[to] = lora[skip:]
        query_ref[to] = qkv[skip:, :q_cols]
    heads = fk_ref.shape[0]
    hidden = jnp.where(place_ref[0] == 0, WIN, 0)
    valid = lax.broadcasted_iota(jnp.int32, (length, 2 * size), 0) >= hidden
    for k in range(heads):
        keys = kv_ref[:length, k * size : (k + 1) * size]
        values = kv_ref[:length, (heads + k) * size : (heads + k + 1) * size]
        feat = softmax_pair(dot(keys, fk_ref[k].astype(bf16)))
        feat = jnp.where(valid, feat.astype(f32), 0.0).astype(bf16)
        feat_ref[:, k * 2 * size : (k + 1) * 2 * size] = feat
        total_ref[k] = dot_tn(feat, with_ones(values, 1))


def window_mask(step):
    row = lax.broadcasted_iota(jnp.int32, (step, step + WIN), 0)
    col = lax.broadcasted_iota(jnp.int32, (step, step + WIN), 1)
    return (col > row) & (col <= row + WIN), col


def early_mask(rows, cols):
    row = lax.broadcasted_iota(jnp.int32, (rows, cols), 0)
    col = lax.broadcasted_iota(jnp.int32, (rows, cols), 1)
    return col <= row + (cols - rows)


def local_attention(place_ref, q_ref, kv_ref, fq_ref, kfeat_ref, *outs, size):
    kv_heads = kfeat_ref.shape[1] // (2 * size)
    group = fq_ref.shape[0] // kv_heads
    length = kfeat_ref.shape[0]
    step = STEP
    hidden = jnp.where(place_ref[0] == 0, WIN, 0)
    in_window, col = window_mask(step)
    for k in range(kv_heads):
        acc_ref, feat_ref = outs[k], outs[kv_heads + k]
        keys = kv_ref[:, k * size : (k + 1) * size]
        values = with_ones(kv_ref[:, (kv_heads + k) * size : (kv_heads + k + 1) * size], 1)
        kfeat = kfeat_ref[:, k * 2 * size : (k + 1) * 2 * size]
        for g in range(group):
            h = k * group + g
            query = q_ref[:, h * size : (h + 1) * size]
            feat = softmax_pair(dot(query, fq_ref[h].astype(bf16)))
            feat_ref[:, g * 2 * size : (g + 1) * 2 * size] = feat
            query = (query.astype(f32) * size ** (-0.5)).astype(bf16)
            for at in range(0, length, step):
                end = at + step
                mask = in_window & (col >= hidden) if at == 0 else in_window
                weight = jnp.where(mask, jnp.exp(dot_nt(query[at:end], keys[at : end + WIN])), 0.0)
                linear = dot_nt(feat[at:end], kfeat[:end])
                linear = jnp.where(early_mask(step, end), linear, 0.0)
                acc = dot(weight.astype(bf16), values[at : end + WIN])
                acc = acc + dot(linear.astype(bf16), values[:end])
                acc_ref[at:end, g * 2 * size : (g + 1) * 2 * size] = acc


def finish_attention(
    lane_ref, *refs, size, kv_heads
):
    accs, feats = refs[:kv_heads], refs[kv_heads : 2 * kv_heads]
    state_ref, out_w_ref, down_ref = refs[2 * kv_heads : 2 * kv_heads + 3]
    total_ref, out_ref, keep_ref, send_ref = refs[2 * kv_heads + 3 :]
    group = accs[0].shape[1] // (2 * size)
    for k in range(kv_heads):
        state = split_column(state_ref[k], size)
        for g in range(group):
            cols = slice(g * 2 * size, (g + 1) * 2 * size)
            h = k * group + g
            acc = accs[k][:, cols] + dot(feats[k][:, cols], state)
            total_ref[:, h * 2 * size : (h + 1) * 2 * size] = acc
            under = acc[:, size : size + 1] + acc[:, size + 1 : size + 2]
            out_ref[:, h * size : (h + 1) * size] = (acc[:, :size] / under).astype(bf16)
    chunk = keep_ref.shape[0] // 2
    for ref, masks in ((send_ref, (1, 3)), (keep_ref, (0, 2))):
        rows = [out_ref[pl.ds(pl.multiple_of(jnp.bitwise_xor(lane_ref[0], m) * chunk, chunk), chunk)] for m in masks]
        rows = jnp.concatenate(rows, 0)
        width = out_w_ref.shape[1]
        ref[:, :width] = dot(rows, out_w_ref[...]).astype(bf16)
        ref[:, width:] = dot(rows, down_ref[...].astype(bf16)).astype(bf16)


def residual_norm(near_ref, got_ref, tokens_ref, vec_ref, middle_ref, normed_ref, lora_ref):
    width = tokens_ref.shape[1]
    branch = near_ref[...].astype(f32) + got_ref[...].astype(f32)
    rank = vec_ref.shape[0] - 8
    lora = branch[:, width:].astype(bf16)
    lora_ref[...] = lora
    ups = vec_ref[2 : 2 + rank].astype(bf16)
    middle = tokens_ref[...].astype(f32) + branch[:, :width] + dot(lora[:, :rank], ups)
    middle_ref[...] = middle
    normed_ref[...] = (middle * inverse_rms(middle) * vec_ref[1:2]).astype(bf16)


def residual_norm_back(
    near_ref, one_ref, two_ref, three_ref, middle_ref, vec_ref, dy_ref, lora_ref,
    grad_ref, branch_ref, gain_ref, up_ref
):
    grad = near_ref[...].astype(f32) + one_ref[...].astype(f32)
    grad = grad + (two_ref[...].astype(f32) + three_ref[...].astype(f32))
    middle = middle_ref[...]
    scale = inverse_rms(middle)
    rank = vec_ref.shape[0] - 8
    gain_ref[...] = jnp.broadcast_to(jnp.sum(grad * middle * scale, 0, keepdims=True), gain_ref.shape)
    scaled = grad * vec_ref[1:2]
    mean = jnp.mean(scaled * middle, -1, keepdims=True)
    total = dy_ref[...].astype(f32) + scale * scaled - middle * (scale * scale * scale * mean)
    grad_ref[...] = total
    low = total.astype(bf16)
    branch_ref[...] = low
    up_ref[...] = dot_tn(lora_ref[...], low)[:rank]


def attended_back(
    lane_ref, own_ref, side_ref, cross_ref, far_ref, out_w_ref, down_ref, vec_ref, total_ref, *refs, size, kv_heads
):
    feats = refs[:kv_heads]
    tops = refs[kv_heads : 2 * kv_heads]
    state_ref, rows_ref, grad_ref = refs[2 * kv_heads :]
    width = own_ref.shape[1]
    rank = vec_ref.shape[0] - 8
    chunk = own_ref.shape[0]
    ups = vec_ref[2 : 2 + rank].astype(bf16)
    for pieces, masks in (((own_ref, side_ref), (0, 2)), ((cross_ref, far_ref), (1, 3))):
        rows = jnp.concatenate([r[...] for r in pieces], 0)
        lora = dot_nt(rows, ups).astype(bf16)
        lora = jnp.concatenate([lora.astype(f32), jnp.zeros((2 * chunk, LANES - rank), f32)], 1).astype(bf16)
        wide = jnp.concatenate([rows, lora], 1)
        grad = dot_nt(rows, out_w_ref[...]) + dot_nt(lora, down_ref[...].astype(bf16))
        for i, m in enumerate(masks):
            to = pl.ds(pl.multiple_of(jnp.bitwise_xor(lane_ref[0], m) * chunk, chunk), chunk)
            rows_ref[to] = wide[i * chunk : (i + 1) * chunk]
            grad_ref[to] = grad[i * chunk : (i + 1) * chunk]
    group = feats[0].shape[1] // (2 * size)
    for k in range(kv_heads):
        state = None
        for g in range(group):
            h = k * group + g
            cols = slice(g * 2 * size, (g + 1) * 2 * size)
            total = total_ref[:, h * 2 * size : (h + 1) * 2 * size]
            under = total[:, size : size + 1] + total[:, size + 1 : size + 2]
            grad = grad_ref[:, h * size : (h + 1) * size] / under
            grad_under = -jnp.sum(grad * total[:, :size], -1, keepdims=True) / under
            wide = jnp.concatenate([grad, jnp.broadcast_to(grad_under, grad.shape)], 1)
            column = lax.broadcasted_iota(jnp.int32, wide.shape, 1)
            wide = split_column(jnp.where(column > size, 0.0, wide), size)
            tops[k][:, cols] = wide
            term = dot_tn(feats[k][:, cols], wide)
            state = term if state is None else state + term
        state_ref[k] = state


def local_back(
    place_ref, q_ref, kv_ref, fq_ref, kfeat_ref, feat_ref, top_ref, state_ref,
    gq_ref, gk_ref, gv_ref, gkfeat_ref, gfq_ref, *, size, k
):
    kv_heads = kfeat_ref.shape[1] // (2 * size)
    group = fq_ref.shape[0] // kv_heads
    length = kfeat_ref.shape[0]
    step = STEP
    hidden = jnp.where(place_ref[0] == 0, WIN, 0)
    in_window, col = window_mask(step)
    gk_ref[...] = jnp.zeros_like(gk_ref)
    gv_ref[...] = jnp.zeros_like(gv_ref)
    gkfeat_ref[...] = jnp.zeros_like(gkfeat_ref)
    keys = kv_ref[:, k * size : (k + 1) * size]
    values = with_ones(kv_ref[:, (kv_heads + k) * size : (kv_heads + k + 1) * size], 2)
    kfeat = kfeat_ref[:, k * 2 * size : (k + 1) * 2 * size]
    state = state_ref[k]
    column = lax.broadcasted_iota(jnp.int32, state.shape, 1)
    norm = state[:, size : size + 1]
    state = jnp.where((column == size) | (column == size + 1), norm, state).astype(bf16)
    for g in range(group):
        h = k * group + g
        matrix = fq_ref[h].astype(bf16)
        query = q_ref[:, h * size : (h + 1) * size]
        scaled = (query.astype(f32) * size ** (-0.5)).astype(bf16)
        cols = slice(g * 2 * size, (g + 1) * 2 * size)
        gfq = None
        for at in range(0, length, step):
            end = at + step
            feat = feat_ref[at:end, cols]
            top = top_ref[at:end, cols]
            mask = in_window & (col >= hidden) if at == 0 else in_window
            near = keys[at : end + WIN]
            weight = jnp.where(mask, jnp.exp(dot_nt(scaled[at:end], near)), 0.0)
            grad = (dot_nt(top, values[at : end + WIN]) * weight).astype(bf16)
            gq = dot(grad, near) * size ** (-0.5)
            gk_ref[at : end + WIN] += dot_tn(grad, scaled[at:end])
            gv_ref[at : end + WIN] += dot_tn(weight.astype(bf16), top)
            early = early_mask(step, end)
            linear = jnp.where(early, dot_nt(feat, kfeat[:end]), 0.0).astype(bf16)
            grad = jnp.where(early, dot_nt(top, values[:end]), 0.0).astype(bf16)
            gfeat = dot(grad, kfeat[:end]) + dot_nt(top, state)
            gkfeat_ref[:end] += dot_tn(grad, feat)
            gv_ref[:end] += dot_tn(linear, top)
            mix = softmax_pair_back(feat, gfeat)
            gq_ref[at:end, g * size : (g + 1) * size] = (gq + dot_nt(mix, matrix)).astype(bf16)
            term = dot_tn(query[at:end], mix)
            gfq = term if gfq is None else gfq + term
        gfq_ref[g] = gfq


def key_back(kv_ref, fk_ref, kfeat_ref, later_ref, *refs, size):
    heads = fk_ref.shape[0]
    gks, gvs, gkfeats = refs[:heads], refs[heads : 2 * heads], refs[2 * heads : 3 * heads]
    gkv_ref, halo_ref, gfk_ref = refs[3 * heads :]
    length = kfeat_ref.shape[0]
    for k in range(heads):
        keys = kv_ref[:length, k * size : (k + 1) * size]
        values = with_ones(kv_ref[:length, (heads + k) * size : (heads + k + 1) * size], 2)
        cols = slice(k * 2 * size, (k + 1) * 2 * size)
        later = later_ref[k]
        column = lax.broadcasted_iota(jnp.int32, later.shape, 1)
        norm = later[:, size : size + 1] + later[:, size + 1 : size + 2]
        later = split_column(jnp.where(column == size, norm, later), size)
        kfeat = kfeat_ref[:, cols]
        mix = softmax_pair_back(kfeat, gkfeats[k][...] + dot_nt(values, later))
        gk, gv = slice(k * size, (k + 1) * size), slice((heads + k) * size, (heads + k + 1) * size)
        gkv_ref[:, gk] = gks[k][...]
        gkv_ref[:length, gk] += dot_nt(mix, fk_ref[k].astype(bf16))
        gkv_ref[:, gv] = gvs[k][:, :size]
        gkv_ref[:length, gv] += dot(kfeat, later)[:, :size]
        gfk_ref[k] = dot_tn(keys, mix)
    halo_ref[...] = gkv_ref[:WIN].astype(bf16)


def project_back(
    lane_ref, *refs, kv_heads
):
    gqs = refs[:kv_heads]
    gkv_ref, back_ref, ups_ref, full_ref, tokens_ref, normed_ref, lora_ref = refs[kv_heads : kv_heads + 7]
    gqkv_ref, keep_ref, send_ref, gain_ref, down_ref, up_ref, ext_ref = refs[kv_heads + 7 :]
    length = tokens_ref.shape[0]
    each = gqs[0].shape[1]
    q_cols = each * kv_heads
    all_cols = ups_ref.shape[1]
    for k in range(kv_heads):
        ext_ref[:, k * each : (k + 1) * each] = gqs[k][...]
    ext_ref[: length - WIN, q_cols:all_cols] = gkv_ref[WIN:length].astype(bf16)
    ext_ref[length - WIN :, q_cols:all_cols] = (gkv_ref[length:] + back_ref[...].astype(f32)).astype(bf16)
    gqkv_ref[...] = ext_ref[:, :all_cols]
    ext_ref[:, all_cols:] = dot_nt(ext_ref[:, :all_cols], ups_ref[...].astype(bf16)).astype(bf16)
    down_ref[...] = dot_tn(ext_ref[:, all_cols:], normed_ref[...])[: down_ref.shape[0]]
    up_ref[...] = dot_tn(lora_ref[...], ext_ref[:, :all_cols])[: up_ref.shape[0]]
    chunk = keep_ref.shape[0] // 2
    width = keep_ref.shape[1]
    gain_ref[...] = jnp.zeros_like(gain_ref)
    for ref, masks in ((send_ref, (1, 3)), (keep_ref, (0, 2))):
        for i, m in enumerate(masks):
            at = pl.ds(pl.multiple_of(jnp.bitwise_xor(lane_ref[0], m) * chunk, chunk), chunk)
            rows = tokens_ref[at].astype(f32)
            scale = inverse_rms(rows)
            grad = dot_nt(ext_ref[at], full_ref[...])
            ref[i * chunk : (i + 1) * chunk] = grad.astype(bf16)
            gain_ref[...] += jnp.broadcast_to(
                jnp.sum(grad * rows * scale, 0, keepdims=True), gain_ref.shape
            )


def norm_back(near_ref, got_ref, tokens_ref, vec_ref, middle_ref, out_ref):
    grad = near_ref[...].astype(f32) + got_ref[...].astype(f32)
    values = tokens_ref[...].astype(f32)
    scale = inverse_rms(values)
    scaled = grad * vec_ref[0:1]
    mean = jnp.mean(scaled * values, -1, keepdims=True)
    total = middle_ref[...] + scale * scaled - values * (scale * scale * scale * mean)
    out_ref[...] = total.astype(bf16)


def units_kernel(*refs):
    gu_ref, down_ref, keep_ref, send_ref, hkeep_ref, hsend_ref, ggu_ref = refs[8:]
    half = keep_ref.shape[0]
    units = down_ref.shape[0]
    width = down_ref.shape[1]
    step = 256
    normed = jnp.concatenate([r[...] for r in refs[:4]], 0)
    grad_out = jnp.concatenate([r[...] for r in refs[4:8]], 0)
    for at in range(0, units, step):
        one = slice(at, at + step)
        two = slice(units + at, units + at + step)
        gate = dot(normed, gu_ref[:, one])
        up = dot(normed, gu_ref[:, two])
        grad = dot_nt(grad_out, down_ref[one])
        sigma = 1.0 / (1.0 + jnp.exp(-gate))
        active = gate * sigma
        hidden = (active * up).astype(bf16)
        hkeep_ref[:, one] = hidden[:half]
        hsend_ref[:, one] = hidden[half:]
        ggu_ref[:, one] = (grad * up * sigma * (1.0 + gate * (1.0 - sigma))).astype(bf16)
        ggu_ref[:, two] = (grad * active).astype(bf16)
    for at in range(0, width, 512):
        cols = slice(at, at + 512)
        grad = dot_nt(ggu_ref[...], gu_ref[cols]).astype(bf16)
        keep_ref[:, cols] = grad[:half]
        send_ref[:, cols] = grad[half:]


def blocks_of_product(place_ref, *refs, lefts, rights, groups, picks):
    left, right = refs[:lefts], refs[lefts : lefts + rights]
    out = refs[-1]
    rows = out.shape[0] // len(picks)

    def joined(pieces):
        return jnp.concatenate(pieces, 0) if len(pieces) > 1 else pieces[0]

    for i, pick in enumerate(picks):
        at = pl.multiple_of(jnp.bitwise_xor(place_ref[0], pick) * rows, rows)
        total = None
        for d in range(groups):
            own = slice(d * lefts // groups, (d + 1) * lefts // groups)
            part = joined([r[:, pl.ds(at, rows)] for r in left[own]])
            own = slice(d * rights // groups, (d + 1) * rights // groups)
            term = dot_tn(part, joined([r[...] for r in right[own]]))
            total = term if total is None else total + term
        out[i * rows : (i + 1) * rows] = total.astype(bf16)


def out_blocks(place_ref, left_ref, right_ref, keep_ref, send_ref, sum_ref, *, pair):
    sum_ref[...] = dot_tn(left_ref[...], right_ref[...])
    count = RING * pair
    rows = sum_ref.shape[0] // count
    for i in range(count):
        at = pl.multiple_of(jnp.bitwise_xor(place_ref[0], i) * rows, rows)
        d, beta = i // pair, i % pair
        part = sum_ref[pl.ds(at, rows)].astype(bf16)
        d = (0, 2, 1, 3)[d]
        if beta == 0:
            keep_ref[d * rows : (d + 1) * rows] = part
        else:
            to = (beta - 1) * RING + d
            send_ref[to * rows : (to + 1) * rows] = part


def pack_small(place_ref, gfk_ref, up_ref, down_ref, outu_ref, two_ref, one_ref, *refs, kv_heads, group):
    gfqs, out_ref = refs[:kv_heads], refs[-1]
    count = out_ref.shape[0]
    size = gfk_ref.shape[2]
    each = size // count
    rank = up_ref.shape[0] // 3
    q_cols = kv_heads * group * size
    kv_cols = kv_heads * size
    q_each, kv_each = q_cols // count, kv_cols // count
    vec_cols = down_ref.shape[1] // count
    vec_rows = 48

    def wide(value, rows):
        if value.shape[1] < LANES:
            value = jnp.concatenate([value, jnp.zeros((value.shape[0], LANES - value.shape[1]), f32)], 1)
        if value.shape[0] < rows:
            value = jnp.concatenate([value, jnp.zeros((rows - value.shape[0], LANES), f32)], 0)
        return value

    for s in range(count):
        own = slice(s * each, (s + 1) * each)
        fq = jnp.concatenate([gfqs[k][g, own] for k in range(kv_heads) for g in range(group)], 0)
        fk = jnp.concatenate([gfk_ref[k, own] for k in range(kv_heads)], 0)
        kv = [
            up_ref[(c + 1) * rank : (c + 2) * rank, q_cols + c * kv_cols + s * kv_each : q_cols + c * kv_cols + (s + 1) * kv_each]
            for c in range(2)
        ]
        q = up_ref[:rank, s * q_each : (s + 1) * q_each]
        groups = [wide(fq, fq.shape[0]), wide(fk, 16), wide(jnp.concatenate(kv, 0), 16), wide(q, 16)]
        for at in range(s * vec_cols, (s + 1) * vec_cols, min(LANES, vec_cols)):
            cols = slice(at, at + min(LANES, vec_cols))
            vec = [down_ref[:, cols], outu_ref[:, cols], two_ref[:1, cols], one_ref[:1, cols]]
            groups.append(wide(jnp.concatenate(vec, 0), vec_rows))
        away = jnp.bitwise_xor(place_ref[0], s)
        to, bit = 0, 1
        while bit < count:
            to = to + jnp.where((away & bit) != 0, count // (2 * bit), 0)
            bit *= 2
        out_ref[pl.ds(to, 1)] = jnp.concatenate(groups, 0).astype(bf16)[None]


def per_device(
    tokens,
    attention_norm_gain,
    query_weight,
    key_value_weight,
    output_weight,
    adapter_down_matrices,
    adapter_query_up,
    adapter_key_value_up,
    adapter_output_down,
    adapter_output_up,
    query_feature_matrix,
    key_feature_matrix,
    feedforward_norm_gain,
    gate_weight,
    up_weight,
    down_weight,
    cotangent,
):
    count = lax.axis_size(SEQ)
    pair = count // RING
    place = lax.axis_index(SEQ)
    along, beside = place // pair, place % pair
    lane = lax.axis_index("kv")
    unused, length, width = tokens.shape
    depth, q_cols = query_weight.shape
    kv_cols = key_value_weight.shape[2]
    heads, head_size = query_feature_matrix.shape[0], query_feature_matrix.shape[2]
    kv_heads = key_feature_matrix.shape[0]
    group = heads // kv_heads
    rank = adapter_query_up.shape[0]
    all_cols = q_cols + 2 * kv_cols
    wide_size = 2 * head_size
    chunk = length // lax.axis_size("kv")
    rows_out = output_weight.shape[0]
    units_each = down_weight.shape[0]
    units = gate_weight.shape[1] // RING
    here = place.astype(jnp.int32)[None]
    lane_here = lane.astype(jnp.int32)[None]
    order = [place ^ i for i in range(count)]
    nears = [lane ^ k for k in (0, 2, 1, 3)]
    rings = [d * pair for d in range(RING)]
    x = tokens[0]
    dy = cotangent[0]

    def across(array, *gates):
        result = [array]
        bit = 1
        while bit < pair:
            result = result + [trade(after(a, *gates), SEQ, bit) for a in result]
            bit *= 2
        return result

    def across_sum(parts, *gates):
        bit = pair // 2
        while bit:
            parts = [
                add_low(parts[i], after(trade(parts[i + bit], SEQ, bit), *gates)) for i in range(bit)
            ]
            bit //= 2
        return parts[0]

    parameters = [
        jnp.swapaxes(adapter_down_matrices, 1, 2),
        query_feature_matrix.reshape(-1, head_size),
        adapter_output_down.T,
        key_feature_matrix.reshape(-1, head_size),
        adapter_key_value_up.reshape(2 * rank, -1),
        adapter_query_up,
        jnp.stack([attention_norm_gain, feedforward_norm_gain]),
        adapter_output_up,
    ]
    packed = pl.pallas_call(
        pack_weights,
        out_shape=shape((depth, all_cols + LANES), bf16),
        in_specs=[pl.BlockSpec(memory_space=pltpu.HBM)] * (2 + len(parameters)),
        out_specs=pl.BlockSpec(memory_space=pltpu.VMEM),
        scratch_shapes=[pltpu.VMEM(p.shape, bf16) for p in parameters]
        + [pltpu.SemaphoreType.DMA((3 + len(parameters),))],
        compiler_params=pltpu.CompilerParams(vmem_limit_bytes=12 * 2**20),
    )(query_weight, key_value_weight, *parameters)
    got = [packed, trade(packed, SEQ, rings[1]), trade(packed, SEQ, rings[2])]
    halo = moved(x[length - WIN :], SEQ, 1)
    pieces = [across(packed)]

    cuts = own_call(
        cut_units,
        [shape((depth, 2 * units), bf16)] * RING,
        [jnp.stack([along ^ d for d in range(RING)]).astype(jnp.int32), gate_weight, up_weight],
        1,
    )
    own_gu = across(cuts[0], got[2], pieces[0][-1], halo)
    pieces.append(across(got[1]))
    pieces.append(across(got[2]))
    got.append(trade(got[2], SEQ, rings[1]))
    pieces.append(across(got[3]))
    last_piece = pieces[3][-1]
    out_got = [output_weight] + [trade(after(output_weight, pieces[1][-1], pieces[0][-1], halo), SEQ, m) for m in rings[1:3]]
    gu_got = [cuts[0], None, None, None]
    gu_got[2] = trade(after(cuts[2], *out_got[1:]), SEQ, rings[2])
    out_got.append(trade(out_got[2], SEQ, rings[1]))
    gu_got[1] = trade(after(cuts[1], out_got[3]), SEQ, rings[1])
    out_first = across(jnp.concatenate(out_got[:2], 0), last_piece)

    own_x = block(x, lane, chunk)
    own_dy = block(dy, lane, chunk)
    dy_blocks = [[block(dy, k, chunk) for k in nears]]
    full, fq_w, fk_w, ups, out_down, vecs = placed(
        [pieces[d][b] for d in range(RING) for b in range(pair)],
        depth,
        order,
        functools.partial(unpack_weights, count=count),
        [
            shape((heads, head_size, head_size), f32),
            shape((kv_heads, head_size, head_size), f32),
            shape((LANES, all_cols), f32),
            shape((q_cols, LANES), f32),
            shape((8 + rank, width), f32),
        ],
        deps=[own_x, own_gu[-1]] + dy_blocks[0],
    )

    normed, lora, query, kv_ext, key_feat, totals = own_call(
        functools.partial(project, size=head_size),
        [
            shape((length, width), bf16),
            shape((length, LANES), bf16),
            shape((length, q_cols), bf16),
            shape((length + WIN, 2 * kv_cols), bf16),
            shape((length, kv_heads * wide_size), bf16),
            shape((kv_heads, wide_size, wide_size), f32),
        ],
        [here, halo, x, full, vecs, ups, fk_w],
        1,
    )
    def running(total, sign, between, beside=True):
        result = jnp.zeros_like(total)
        results, steps = [], []
        bit = 1
        while bit < count:
            other = trade(total, SEQ, bit)
            if len(results) < len(between):
                results.append(between[len(results)](*(steps[-1:] if beside else [other])))
                if beside:
                    other = after(other, results[-1][0])
            steps.append(other)
            mine = (place & bit) != 0 if sign > 0 else (place & bit) == 0
            result = result + jnp.where(mine, other, 0.0)
            total = total + other
            bit *= 2
        return result, results, steps

    states, unused, steps = running(totals, 1, [])
    local = own_call(
        functools.partial(local_attention, size=head_size),
        [shape((length, group * wide_size), f32)] * kv_heads
        + [shape((length, group * wide_size), bf16)] * kv_heads,
        [here, query, kv_ext, fq_w, key_feat],
        1,
        deps=[steps[1], gu_got[1], gu_got[2]],
    )
    accs, feats = list(local[:kv_heads]), list(local[kv_heads:])
    out_second = across(jnp.concatenate(out_got[2:], 0), steps[0])
    gu_got[3] = trade(after(cuts[3], states), SEQ, rings[3])
    dy_got = [None, trade(after(own_dy, states), SEQ, rings[1])]
    out_w = placed(
        out_first + out_second,
        rows_out,
        [order[rings[d] + b] for b in range(pair) for d in (0, 1)]
        + [order[rings[d] + b] for b in range(pair) for d in (2, 3)],
    )
    gu_mid = across(jnp.concatenate([gu_got[1], gu_got[2]], 0))
    tops, attended, keep, send = own_call(
        functools.partial(finish_attention, size=head_size, kv_heads=kv_heads),
        [
            shape((length, heads * wide_size), f32),
            shape((length, q_cols), bf16),
            shape((2 * chunk, width + LANES), bf16),
            shape((2 * chunk, width + LANES), bf16),
        ],
        [lane_here] + accs + feats + [states, out_w, out_down],
        1,
        deps=[],
    )
    downs = across(down_weight, gu_mid[-1])

    def kv_sums(keep, send, *gates):
        other = after(trade(send, "kv", 1), *gates)
        near = add_low(keep[:chunk], other[:chunk])
        side = add_low(keep[chunk:], other[chunk:])
        return near, trade(side, "kv", 2)

    def kv_all(own, *gates):
        side = trade(own, "kv", 2)
        return own, side, trade(own, "kv", 1), trade(after(side, *gates), "kv", 1)

    near, other = kv_sums(keep, send)
    middle, normed_two, lora_out = own_call(
        residual_norm,
        [shape((chunk, width), f32), shape((chunk, width), bf16), shape((chunk, LANES), bf16)],
        [near, other, own_x, vecs],
        deps=[gu_got[3]],
    )

    n_got = [normed_two, None, None, None]
    n_got[2] = trade(normed_two, SEQ, rings[2])
    n_got[1] = trade(normed_two, SEQ, rings[1])
    gu_last = across(gu_got[3])
    n_first = kv_all(normed_two, gu_mid[-1], downs[-1], gu_last[-1])
    n_got[3] = trade(n_got[2], SEQ, rings[1])
    dy_got.append(trade(after(own_dy, n_got[1]), SEQ, rings[2]))
    dy_got.append(trade(after(dy_got[2], n_got[3]), SEQ, rings[1]))
    dy_blocks.append(kv_all(after(dy_got[1], normed_two)))
    gu_w = placed(
        [after(g, normed_two) for g in own_gu + gu_mid + gu_last],
        depth,
        [order[b] for b in range(pair)]
        + [order[rings[d] + b] for b in range(pair) for d in (1, 2)]
        + [order[rings[3] + b] for b in range(pair)],
    )
    down_w = placed([after(w, normed_two) for w in downs], units_each, [beside ^ b for b in range(pair)])
    n_blocks = []
    keeps, hiddens, ggus = [], [], []
    sums = [None] * RING
    halves = [None] * RING
    for d in range(RING):
        n_blocks.append(n_first if d == 0 else kv_all(n_got[d]))
        if d == 0:
            ready = []
        elif d == 1:
            ready = [n_got[3], dy_got[2], kv_all(n_got[2])[1]]
        else:
            ready = [halves[d - 2][0], halves[d - 2][1]]
        if d == 2:
            ready.append(kv_all(n_got[3])[1])
        if d > 1:
            dy_blocks.append(kv_all(dy_got[d]))
        keep, send, hkeep, hsend, ggu = own_call(
            units_kernel,
            [shape((2 * chunk, width), bf16)] * 2
            + [shape((2 * chunk, units), bf16)] * 2
            + [shape((4 * chunk, 2 * units), bf16)],
            list(n_blocks[d]) + list(dy_blocks[d]) + [gu_w, down_w],
            deps=ready + keeps[-1:],
        )
        keeps.append(keep)
        other = trade(send, "kv", 1)
        halves[d] = (add_low(keep[:chunk], other[:chunk]), add_low(keep[chunk:], other[chunk:]))
        hiddens.append((hkeep, hsend))
        ggus.append(ggu)
    def product(left, right, picks, rows, groups=RING, at=here, deps=()):
        if rows % LANES == 0:
            return own_call(
                functools.partial(
                    blocks_of_product, lefts=len(left), rights=len(right), groups=groups, picks=picks
                ),
                [shape((rows * len(picks), right[0].shape[1]), bf16)],
                [at] + left + right,
                1,
                deps=deps,
            )[0]
        result = dot_tn(jnp.concatenate(left, 0), jnp.concatenate(right, 0)).astype(bf16)
        return jnp.concatenate([block(result, at[0] ^ i, rows) for i in picks], 0)

    n_all = [p for n in n_blocks for p in n]
    picks = [[m + b for m in rings] for b in range(pair)]
    gu_parts = [None] * pair
    for b in range(1, pair):
        gu_parts[b] = [product(n_all, ggus, p, depth, deps=halves[3]) for p in (picks[b][2:], picks[b][:2])]
    firsts = [p for part in gu_parts[1:] for p in part]
    sums = [None] * RING
    for d in (0, 3, 2, 1):
        side = halves[d][1]
        sums[d] = add_low(after(halves[d][0], *firsts) if d == 3 else halves[d][0], trade(side, "kv", 2))
    rest = [trade(sums[d], SEQ, rings[d]) for d in (1, 2, 3)]
    gu_parts[0] = [product(n_all, ggus, p, depth, deps=[sums[3]]) for p in (picks[0][2:], picks[0][:2])]
    far_cols = across_sum([p[0] for p in gu_parts])
    hidden_all = [p for h in hiddens for p in h]
    dy_all = [p for b in dy_blocks for p in b]
    beside_here = beside.astype(jnp.int32)[None]
    down_parts = [None] * pair
    for b in reversed(range(pair)):
        down_parts[b] = product(
            hidden_all, dy_all, [b], units_each, RING, beside_here, [sums[3]]
        )
    grad_middle, grad_branch, gain_two, out_up_part = own_call(
        residual_norm_back,
        [
            shape((chunk, width), f32),
            shape((chunk, width), bf16),
            shape((8, width), f32),
            shape((rank, width), f32),
        ],
        [sums[0]] + rest + [middle, vecs, own_dy, lora_out],
        deps=gu_parts[0] + down_parts + [far_cols],
    )

    all_branch = kv_all(grad_branch)

    hkeep = jnp.concatenate([h[0] for h in hiddens], 0)
    hsend = jnp.concatenate([h[1] for h in hiddens], 0)
    down_send = dot(after(hsend, grad_branch), down_w).astype(bf16)
    down_keep = dot(after(hkeep, grad_branch), down_w).astype(bf16)
    near_cols = across_sum([p[1] for p in gu_parts])
    down_other = trade(down_send, "kv", 1)
    gate_parts = [near_cols[:depth], None, None, None]
    gate_parts[2] = trade(far_cols[:depth], SEQ, rings[2])
    gate_parts[3] = trade(after(far_cols[depth:], all_branch[1]), SEQ, rings[3])
    results = own_call(
        functools.partial(attended_back, size=head_size, kv_heads=kv_heads),
        [shape((length, group * wide_size), bf16)] * kv_heads
        + [shape((kv_heads, wide_size, wide_size), f32), shape((length, width + LANES), bf16)],
        [lane_here] + list(all_branch) + [out_w, out_down, vecs, tops] + feats,
        1,
        [pltpu.VMEM((length, q_cols), f32)],
        deps=[],
    )
    grad_tops, grad_state, branch_rows = results[:kv_heads], results[kv_heads], results[kv_heads + 1]
    other = down_other.reshape(RING, 2, chunk, width)
    down_keep = down_keep.reshape(RING, 2, chunk, width)
    near = add_low(down_keep[:, 0], other[:, 0])
    side = add_low(down_keep[:, 1], other[:, 1])
    high = trade(after(side[2:], all_branch[1]), "kv", 2)
    down_sum = across_sum(down_parts)
    out_keep, out_send = own_call(
        functools.partial(out_blocks, pair=pair),
        [
            shape((RING * rows_out, width + LANES), bf16),
            shape(((pair - 1) * RING * rows_out, width + LANES), bf16),
        ],
        [here, attended, branch_rows],
        1,
        [pltpu.VMEM((q_cols, width + LANES), f32)],
    )
    out_parts = [out_keep] + [
        out_send[b * RING * rows_out : (b + 1) * RING * rows_out] for b in range(pair - 1)
    ]

    def attend_back(k, *step):
        return own_call(
            functools.partial(local_back, size=head_size, k=k),
            [
                shape((length, group * head_size), bf16),
                shape((length + WIN, head_size), f32),
                shape((length + WIN, wide_size), f32),
                shape((length, wide_size), f32),
                shape((group, head_size, head_size), f32),
            ],
            [here, query, kv_ext, fq_w, key_feat, feats[k], grad_tops[k], states],
            1,
            deps=list(step) + ([high, gate_parts[3]] if k else [side, out_send, down_sum, gate_parts[2]]),
        )

    later, local, steps = running(grad_state, -1, [functools.partial(attend_back, k) for k in range(kv_heads)])
    gate_parts[1] = trade(near_cols[depth:], SEQ, rings[1])
    low = trade(after(side[:2], high), "kv", 2)
    high = add_low(near[2:], high)
    low = add_low(near[:2], low)
    out_sum = across_sum([out_keep] + [after(p, steps[0]) for p in out_parts[1:]], local[0][0])
    mixed = trade(jnp.concatenate([high[1], low[1]], 0), SEQ, rings[1])
    out_half = 2 * rows_out
    out_other = trade(out_sum[out_half:], SEQ, rings[1])
    grad_kv, halo_back, grad_fk = own_call(
        functools.partial(key_back, size=head_size),
        [
            shape((length + WIN, 2 * kv_cols), f32),
            shape((WIN, 2 * kv_cols), bf16),
            shape((kv_heads, head_size, head_size), f32),
        ],
        [kv_ext, fk_w, key_feat, later] + [l[1] for l in local] + [l[2] for l in local] + [l[3] for l in local],
    )
    returned = moved(halo_back, SEQ, -1)

    gqkv, grad_keep, grad_send, gain_one, lora_down, up_all, ext = own_call(
        functools.partial(project_back, kv_heads=kv_heads),
        [
            shape((length, all_cols), bf16),
            shape((2 * chunk, width), bf16),
            shape((2 * chunk, width), bf16),
            shape((8, width), f32),
            shape((3 * rank, width), f32),
            shape((3 * rank, all_cols), f32),
            shape((length, all_cols + LANES), bf16),
        ],
        [lane_here] + [l[0] for l in local] + [grad_kv, returned, ups, full, x, normed, lora],
        1,
    )
    near, other = kv_sums(grad_keep, grad_send)
    qkv_parts = [None] * pair
    for b in reversed(range(pair)):
        qkv_parts[b] = [product([normed], [gqkv], p, depth, 1, deps=[near]) for p in (picks[b][2:], picks[b][:2])]

    qkv_high = across_sum([p[0] for p in qkv_parts])
    qkv_low = across_sum([p[1] for p in qkv_parts])
    (own_grad,) = own_call(
        norm_back, [shape((chunk, width), bf16)], [near, other, own_x, vecs, grad_middle],
        deps=[qkv_high],
    )
    all_grad = kv_all(own_grad)

    vec_cols = width // count
    fq_rows = heads * head_size // count
    fk_rows = kv_heads * head_size // count
    small_rows = fq_rows + 48 + 48 * max(1, vec_cols // LANES)
    (small,) = own_call(
        functools.partial(pack_small, kv_heads=kv_heads, group=group),
        [shape((count, small_rows, LANES), bf16)],
        [here, grad_fk, up_all, lora_down, out_up_part, gain_two, gain_one] + [l[4] for l in local],
        1,
        deps=[own_grad],
    )
    half, bit = count // 2, 1
    while half:
        small = add_low(small[:half], trade(small[half:], SEQ, bit))
        half, bit = half // 2, 2 * bit
    qkv_far = add_low(qkv_high[:depth], trade(qkv_high[depth:], SEQ, rings[1]))
    qkv_near = add_low(qkv_low[:depth], trade(qkv_low[depth:], SEQ, rings[1]))
    grad_w = qkv_near.astype(f32) + trade(qkv_far, SEQ, rings[2]).astype(f32)
    grad_w_query = grad_w[:, :q_cols]
    grad_w_kv = jnp.stack([grad_w[:, q_cols : q_cols + kv_cols], grad_w[:, q_cols + kv_cols :]])

    (grad_tokens,) = own_call(
        rows_placed, [shape((length, width), f32)], [jnp.stack(nears).astype(jnp.int32), *all_grad], 1
    )

    mixed = after(mixed, own_grad)
    high = add_low(high[0], mixed[:chunk])
    low = add_low(low[0], mixed[chunk:])
    ffn_out = add_low(low, trade(high, SEQ, rings[2])).astype(f32)
    own_out = (middle + ffn_out).astype(bf16)
    all_out = kv_all(own_out)
    (output,) = own_call(
        rows_placed, [shape((length, width), bf16)], [jnp.stack(nears).astype(jnp.int32), *all_out], 1
    )
    out_sum = add_low(after(out_sum[:out_half], own_grad), out_other)
    out_sum = add_low(out_sum[:rows_out], trade(out_sum[rows_out:], SEQ, rings[2])).astype(f32)
    grad_w_gate, grad_w_up = own_call(
        place_units,
        [shape(gate_weight.shape, f32)] * 2,
        [jnp.stack([along ^ d for d in range(RING)]).astype(jnp.int32)]
        + gate_parts,
        1,
        deps=[own_grad],
    )

    small = small[0]
    at = fq_rows
    grad_fmap_query = small[:at, :head_size].astype(f32).reshape(query_feature_matrix.shape)
    grad_fmap_key = small[at : at + fk_rows, :head_size].astype(f32).reshape(key_feature_matrix.shape)
    at += 16
    kv_each, q_each = kv_cols // count, q_cols // count
    grad_lora_up_kv = small[at : at + 2 * rank, :kv_each].astype(f32).reshape(2, rank, kv_each)
    at += 16
    grad_lora_up_query = small[at : at + rank, :q_each].astype(f32)
    at += 16
    total = small[at:]
    for mask in (1, 2):
        total = lax.optimization_barrier(total)
        total = add_low(total, trade(total, "kv", mask))
    total = lax.optimization_barrier(total).astype(f32)
    each = min(LANES, vec_cols)
    total = jnp.concatenate(
        [total[i * 48 : (i + 1) * 48, :each] for i in range(vec_cols // each)], 1
    )
    grad_lora_down = jnp.transpose(total[: 3 * rank].reshape(3, rank, depth), (0, 2, 1))
    grad_lora_up_out = total[3 * rank : 4 * rank]
    grad_g_mlp = total[4 * rank]
    grad_g_attn = total[4 * rank + 1]
    return (
        output[None],
        grad_tokens[None],
        grad_g_attn,
        grad_w_query,
        grad_w_kv,
        out_sum[:, :width],
        grad_lora_down,
        grad_lora_up_query,
        grad_lora_up_kv,
        out_sum[:, width : width + rank],
        grad_lora_up_out,
        grad_fmap_query,
        grad_fmap_key,
        grad_g_mlp,
        grad_w_gate,
        grad_w_up,
        down_sum.astype(f32),
    )


def solution(mesh):
    devices = mesh.devices
    count, kv = devices.shape
    mesh = Mesh(devices.reshape(RING, count // RING, kv), SEQ + ("kv",))
    return jax.shard_map(
        per_device,
        mesh=mesh,
        in_specs=(
            P(None, SEQ, None),
            P(SEQ),
            P(SEQ, "kv"),
            P(None, SEQ, "kv"),
            P(("kv",) + SEQ, None),
            P(None, SEQ, None),
            P(None, ("kv",) + SEQ),
            P(None, None, ("kv",) + SEQ),
            P(("kv",) + SEQ, None),
            P(None, SEQ),
            P("kv", SEQ, None),
            P("kv", SEQ, None),
            P(SEQ),
            P(SEQ, "kv"),
            P(SEQ, "kv"),
            P(("kv",) + SEQ, None),
            P(None, SEQ, None),
        ),
        out_specs=(
            P(None, SEQ, None),
            P(None, SEQ, None),
            P(SEQ),
            P(SEQ, "kv"),
            P(None, SEQ, "kv"),
            P(("kv",) + SEQ, None),
            P(None, SEQ, None),
            P(None, ("kv",) + SEQ),
            P(None, None, ("kv",) + SEQ),
            P(("kv",) + SEQ, None),
            P(None, SEQ),
            P("kv", SEQ, None),
            P("kv", SEQ, None),
            P(SEQ),
            P(SEQ, "kv"),
            P(SEQ, "kv"),
            P(("kv",) + SEQ, None),
        ),
        check_vma=False,
    )
```

time: 875 us -> 640 us (0.73); the launches traced: 858 us -> 634 us
  matrix products: 170 us -> 5.08 us
  Pallas kernels: 0 us -> 138 us
  local copies, waits for them, and re-layouts: 134 us -> 54.3 us
  starting transfers between devices: 194 us -> 115 us
  other arithmetic: 67 us -> 26 us
    pallas_call x0 -> x36, Pallas kernels: none -> 138 us  [the longest x31 130 us: own_call(): pl.pallas_call(run, out_shape=tuple(outs), in_specs=[smem] * scalars + [v...]
    dot_general x47 -> x0, matrix products: 125 us -> none  [the longest x18 51.6 us: dot_nt(): lax.dot_general(a, b, (((1,), (1,)), ((), ())), preferred_element_type=f32)]
    ppermute x10 -> x2, starting transfers between devices: 49.3 us -> 5.41 us  [moved(): return lax.ppermute(array, axis, pairs)]
    ppermute x116 -> x100, starting transfers between devices: 144 us -> 110 us  [trade(): return lax.ppermute(array, axis, [(i, i ^ mask) for i in range(count)])]
    dot_general x15 -> x2, matrix products: 34.8 us -> 5.08 us  [dot(): return jnp.dot(a, b, preferred_element_type=f32)]
    dynamic_update_slice x27 -> x0, local copies, waits for them, and re-layouts: 23.5 us -> none  [placed(): result = lax.dynamic_update_slice_in_dim(result, piece, at * rows, 0)]
    slice x40 -> x15, local copies, waits for them, and re-layouts: 22.3 us -> 6.67 us  [the longest x1 1.67 us: per_device(): halo = moved(x[length - WIN:], SEQ, 1)]
    ppermute x116 -> x100, waiting for transfers between devices: 280 us -> 291 us  [trade(): return lax.ppermute(array, axis, [(i, i ^ mask) for i in range(count)])]
  transfers between devices with their start and end apart: 126 -> 102, of which waited for: 40 -> 38; matrix products, arithmetic and copies ran while one was open for 41% -> 8% of each run, Pallas kernels for 0% -> 20%
where the time goes in v2:
time: 640 us; the launch traced here: 634 us
  waiting for transfers between devices  292 us (46%)
  Pallas kernels  138 us (22%)
  starting transfers between devices  115 us (18%)
  local copies, waits for them, and re-layouts  54.3 us (8%)
  other arithmetic  26 us (4%)
    ppermute x100, waiting for transfers between devices, trade(): return lax.ppermute(array, axis, [(i, i ^ mask) for i in range(count)])  291 us
    pallas_call x31, Pallas kernels, own_call(): pl.pallas_call(run, out_shape=tuple(outs), in_specs=[smem] * scalars + [v...  130 us
    ppermute x100, starting transfers between devices, trade(): return lax.ppermute(array, axis, [(i, i ^ mask) for i in range(count)])  110 us
    unnamed x254, local copies, waits for them, and re-layouts  37.5 us
    convert_element_type x25, other arithmetic, add_low(): return (a.astype(f32) + b.astype(f32)).astype(bf16)  14.3 us
  transfers between devices with their start and end apart: 102, of which 38 were waited for; matrix products, arithmetic and copies ran while one was open for 8% of the time, Pallas kernels for 20%

profile of v2, /device:TPU:9, one launch (start us, length us, event | category | flops | bytes accessed | tf_op | source)
XLA Modules:
  0.0 633.8 jit_solution(2657923829813500883)
XLA Ops:
  16.7 14.8 %collective-permute-done.2.refs_2_ = bf16[256,896]{1,0:T(8,128)(2,1)S(1)} collective-permute-done((bf16[256,896]{1,0:T(8,128)(2,1)S(1)}, bf16[256,896]{1,0:T(8,128)(2,1)S(1)}, u32[]{:S(2)}, u32[]{:S(2)}) %collective-permute-start.2) | collective-permute-done | bytes 458784 | tf_op jit(solution)/shard_map/ppermute | solution.py:24
  38.8 9.7 %collective-permute-done.3.refs_3_ = bf16[256,896]{1,0:T(8,128)(2,1)} collective-permute-done((bf16[256,896]{1,0:T(8,128)(2,1)S(1)}, bf16[256,896]{1,0:T(8,128)(2,1)}, u32[]{:S(2)}, u32[]{:S(2)}) %collective-permute-start.3) | collective-permute-done | bytes 458784 | tf_op jit(solution)/shard_map/ppermute | solution.py:24
  66.2 20.8 %collective-permute-done.7.refs_7_ = bf16[256,896]{1,0:T(8,128)(2,1)S(1)} collective-permute-done((bf16[256,896]{1,0:T(8,128)(2,1)}, bf16[256,896]{1,0:T(8,128)(2,1)S(1)}, u32[]{:S(2)}, u32[]{:S(2)}) %collective-permute-start.7) | collective-permute-done | bytes 458784 | tf_op jit(solution)/shard_map/ppermute | solution.py:24
  106.1 9.3 %collective-permute-done.10.refs_5_ = f32[2,128,128]{2,1,0:T(8,128)S(1)} collective-permute-done((f32[2,128,128]{2,1,0:T(8,128)S(1)}, f32[2,128,128]{2,1,0:T(8,128)S(1)}, u32[]{:S(2)}, u32[]{:S(2)}) %collective-permute-start.10) | collective-permute-done | bytes 131104 | tf_op jit(solution)/shard_map/ppermute | solution.py:24
  122.2 10.7 %shard_map.300 = (f32[512,512]{1,0:T(8,128)S(1)}, f32[512,512]{1,0:T(8,128)S(1)}, bf16[512,512]{1,0:T(8,128)(2,1)S(1)}, bf16[512,512]{1,0:T(8,128)(2,1)S(1)}) custom-call(s32[1]{0:T(128)} %bitcast.4.refs_0_, bf16[512,512]{1,0:T(8,128)(2,1)S(1)} %get-tuple-element.134.refs_1_, bf16[576,256]{1,0:T(8,128)(2,1)S(1)} %get-tuple-element.135.refs_2_.refs_0_, ...), custom_call_target="tpu_custom_call" | custom-call | tf_op jit(solution)/shard_map/pallas_call | solution.py:66
  151.6 18.6 %collective-permute-done.24.refs_3_ = bf16[512,1024]{1,0:T(8,128)(2,1)S(1)} collective-permute-done((bf16[512,1024]{1,0:T(8,128)(2,1)S(1)}, bf16[512,1024]{1,0:T(8,128)(2,1)S(1)}, u32[]{:S(2)}, u32[]{:S(2)}) %collective-permute-start.24) | collective-permute-done | bytes 1048608 | tf_op jit(solution)/shard_map/ppermute | solution.py:24
  188.7 16.3 %collective-permute-done.26.refs_5_ = bf16[256,1024]{1,0:T(8,128)(2,1)S(1)} collective-permute-done((bf16[256,1024]{1,0:T(8,128)(2,1)S(1)}, bf16[256,1024]{1,0:T(8,128)(2,1)S(1)}, u32[]{:S(2)}, u32[]{:S(2)}) %collective-permute-start.26) | collective-permute-done | bytes 524320 | tf_op jit(solution)/shard_map/ppermute | solution.py:24
  225.9 7.3 %shard_map.306 = (bf16[256,2048]{1,0:T(8,128)(2,1)S(1)}, bf16[256,2048]{1,0:T(8,128)(2,1)S(1)}, bf16[256,512]{1,0:T(8,128)(2,1)S(1)}, bf16[256,512]{1,0:T(8,128)(2,1)S(1)}, bf16[512,1024]{1,0:T(8,128)(2,1)S(1)}) custom-call(bf16[128,2048]{1,0:T(8,128)(2,1)S(1)} %copy-done.5, bf16[128,2048]{1,0:T(8,128)(2,1)} %collective-permute-done.22.refs_1_.refs_2_, ...), custom_call_target="tpu_custom_call" | custom-call | tf_op jit(solution)/shard_map/pallas_call | solution.py:66
  239.2 7.5 %shard_map.307 = (bf16[256,2048]{1,0:T(8,128)(2,1)S(1)}, bf16[256,2048]{1,0:T(8,128)(2,1)S(1)}, bf16[256,512]{1,0:T(8,128)(2,1)S(1)}, bf16[256,512]{1,0:T(8,128)(2,1)S(1)}, bf16[512,1024]{1,0:T(8,128)(2,1)S(1)}) custom-call(bf16[128,2048]{1,0:T(8,128)(2,1)S(1)} %copy-done.7, bf16[128,2048]{1,0:T(8,128)(2,1)S(1)} %copy-done.9, ...), custom_call_target="tpu_custom_call" | custom-call | tf_op jit(solution)/shard_map/pallas_call | solution.py:66
  252.4 10.9 %collective-permute-done.49.refs_4_.refs_21_ = bf16[128,2048]{1,0:T(8,128)(2,1)S(1)} collective-permute-done((bf16[128,2048]{1,0:T(8,128)(2,1)}, bf16[128,2048]{1,0:T(8,128)(2,1)S(1)}, u32[]{:S(2)}, u32[]{:S(2)}) %collective-permute-start.49) | collective-permute-done | bytes 524320 | tf_op jit(solution)/shard_map/ppermute | solution.py:24
  266.9 10.6 %collective-permute-done.50.refs_5_.refs_22_ = bf16[128,2048]{1,0:T(8,128)(2,1)S(1)} collective-permute-done((bf16[128,2048]{1,0:T(8,128)(2,1)S(1)}, bf16[128,2048]{1,0:T(8,128)(2,1)S(1)}, u32[]{:S(2)}, u32[]{:S(2)}) %collective-permute-start.50) | collective-permute-done | bytes 524320 | tf_op jit(solution)/shard_map/ppermute | solution.py:24
  279.8 9.0 %collective-permute-done.54 = bf16[128,2048]{1,0:T(8,128)(2,1)S(1)} collective-permute-done((bf16[128,2048]{1,0:T(8,128)(2,1)S(1)}, bf16[128,2048]{1,0:T(8,128)(2,1)S(1)}, u32[]{:S(2)}, u32[]{:S(2)}) %collective-permute-start.54) | collective-permute-done | bytes 524320 | tf_op jit(solution)/shard_map/ppermute | solution.py:24
  324.3 7.1 %collective-permute-done.61 = bf16[128,2048]{1,0:T(8,128)(2,1)S(1)} collective-permute-done((bf16[128,2048]{1,0:T(8,128)(2,1)S(1)}, bf16[128,2048]{1,0:T(8,128)(2,1)S(1)}, u32[]{:S(2)}, u32[]{:S(2)}) %collective-permute-start.61) | collective-permute-done | bytes 524320 | tf_op jit(solution)/shard_map/ppermute | solution.py:24
  349.6 7.8 %collective-permute-done.59.refs_2_ = bf16[128,2048]{1,0:T(8,128)(2,1)S(1)} collective-permute-done((bf16[128,2048]{1,0:T(8,128)(2,1)S(1)}, bf16[128,2048]{1,0:T(8,128)(2,1)S(1)}, u32[]{:S(2)}, u32[]{:S(2)}) %collective-permute-start.59) | collective-permute-done | bytes 524320 | tf_op jit(solution)/shard_map/ppermute | solution.py:24
  357.4 13.1 %collective-permute-done.62.refs_3_ = bf16[128,2048]{1,0:T(8,128)(2,1)S(1)} collective-permute-done((bf16[128,2048]{1,0:T(8,128)(2,1)S(1)}, bf16[128,2048]{1,0:T(8,128)(2,1)S(1)}, u32[]{:S(2)}, u32[]{:S(2)}) %collective-permute-start.62) | collective-permute-done | bytes 524320 | tf_op jit(solution)/shard_map/ppermute | solution.py:24
  379.2 10.9 %collective-permute-done.65.refs_2_ = bf16[128,2048]{1,0:T(8,128)(2,1)S(1)} collective-permute-done((bf16[128,2048]{1,0:T(8,128)(2,1)S(1)}, bf16[128,2048]{1,0:T(8,128)(2,1)S(1)}, u32[]{:S(2)}, u32[]{:S(2)}) %collective-permute-start.65) | collective-permute-done | bytes 524320 | tf_op jit(solution)/shard_map/ppermute | solution.py:24
  422.9 12.3 %shard_map.319 = (bf16[512,256]{1,0:T(8,128)(2,1)S(1)}, f32[576,64]{1,0:T(8,128)S(1)}, f32[576,128]{1,0:T(8,128)S(1)}, f32[512,128]{1,0:T(8,128)S(1)}, f32[4,64,64]{2,1,0:T(8,128)S(1)}) custom-call(s32[1]{0:T(128)} %bitcast.4.refs_0_, bf16[512,512]{1,0:T(8,128)(2,1)S(1)} %copy-done.24, bf16[576,256]{1,0:T(8,128)(2,1)S(1)} %get-tuple-element.135.refs_2_.refs_0_, ...), custom_call_target="tpu_custom_call" | custom-call | tf_op jit(solution)/shard_map/pallas_call | solution.py:66
  446.8 16.1 %collective-permute-done.74.refs_10_.refs_4_ = bf16[256,1024]{1,0:T(8,128)(2,1)} collective-permute-done((bf16[256,1024]{1,0:T(8,128)(2,1)}, bf16[256,1024]{1,0:T(8,128)(2,1)}, u32[]{:S(2)}, u32[]{:S(2)}) %collective-permute-start.74) | collective-permute-done | bytes 524320 | tf_op jit(solution)/shard_map/ppermute | solution.py:24
  463.0 12.5 %shard_map.320 = (bf16[512,256]{1,0:T(8,128)(2,1)S(1)}, f32[576,64]{1,0:T(8,128)S(1)}, f32[576,128]{1,0:T(8,128)S(1)}, f32[512,128]{1,0:T(8,128)S(1)}, f32[4,64,64]{2,1,0:T(8,128)S(1)}) custom-call(s32[1]{0:T(128)} %bitcast.4.refs_0_, bf16[512,512]{1,0:T(8,128)(2,1)S(1)} %copy-done.25, bf16[576,256]{1,0:T(8,128)(2,1)S(1)} %get-tuple-element.135.refs_2_.refs_0_, ...), custom_call_target="tpu_custom_call" | custom-call | tf_op jit(solution)/shard_map/pallas_call | solution.py:66
  509.8 11.1 %collective-permute-done.80 = bf16[512,768]{1,0:T(8,128)(2,1)S(1)} collective-permute-done((bf16[512,768]{1,0:T(8,128)(2,1)S(1)}, bf16[512,768]{1,0:T(8,128)(2,1)S(1)}, u32[]{:S(2)}, u32[]{:S(2)}) %collective-permute-start.80) | collective-permute-done | bytes 786464 | tf_op jit(solution)/shard_map/ppermute | solution.py:24
  528.5 9.3 %collective-permute-done.93 = bf16[512,768]{1,0:T(8,128)(2,1)S(1)} collective-permute-done((bf16[512,768]{1,0:T(8,128)(2,1)S(1)}, bf16[512,768]{1,0:T(8,128)(2,1)S(1)}, u32[]{:S(2)}, u32[]{:S(2)}) %collective-permute-start.93) | collective-permute-done | bytes 786464 | tf_op jit(solution)/shard_map/ppermute | solution.py:24
  547.7 11.8 %collective-permute-done.89 = bf16[2,208,128]{2,1,0:T(8,128)(2,1)S(1)} collective-permute-done((bf16[2,208,128]{2,1,0:T(8,128)(2,1)S(1)}, bf16[2,208,128]{2,1,0:T(8,128)(2,1)S(1)}, u32[]{:S(2)}, u32[]{:S(2)}) %collective-permute-start.89) | collective-permute-done | bytes 106528 | tf_op jit(solution)/shard_map/ppermute | solution.py:24
  583.8 26.3 %collective-permute-done.81 = bf16[128,2048]{1,0:T(8,128)(2,1)S(1)} collective-permute-done((bf16[128,2048]{1,0:T(8,128)(2,1)}, bf16[128,2048]{1,0:T(8,128)(2,1)S(1)}, u32[]{:S(2)}, u32[]{:S(2)}) %collective-permute-start.81) | collective-permute-done | bytes 524320 | tf_op jit(solution)/shard_map/ppermute | solution.py:24
  616.0 8.0 %collective-permute-done.82.refs_2_ = bf16[128,2048]{1,0:T(8,128)(2,1)S(1)} collective-permute-done((bf16[128,2048]{1,0:T(8,128)(2,1)S(1)}, bf16[128,2048]{1,0:T(8,128)(2,1)S(1)}, u32[]{:S(2)}, u32[]{:S(2)}) %collective-permute-start.82) | collective-permute-done | bytes 524320 | tf_op jit(solution)/shard_map/ppermute | solution.py:24
  (550 shorter events, 339.2 us)
Async XLA Ops:
  55.2 32.1 %collective-permute-start.8 = (bf16[256,1024]{1,0:T(8,128)(2,1)}, bf16[256,1024]{1,0:T(8,128)(2,1)S(1)}, u32[]{:S(2)}, u32[]{:S(2)}) collective-permute-start(bf16[256,1024]{1,0:T(8,128)(2,1)} %get-tuple-element.159.refs_0_), channel_id=1, source_target_pairs={{0,4},{4,0},{8,12},{12,8},{16,20},{20,16},{24,28},{28,24},{1,5},{5... | collective-permute-start | bytes 1572872 | tf_op jit(solution)/shard_map/ppermute | solution.py:24
  62.1 59.2 %collective-permute-start.15 = (bf16[256,1024]{1,0:T(8,128)(2,1)}, bf16[256,1024]{1,0:T(8,128)(2,1)}, u32[]{:S(2)}, u32[]{:S(2)}) collective-permute-start(bf16[256,1024]{1,0:T(8,128)(2,1)} %copy-done.117), channel_id=1, source_target_pairs={{0,16},{4,20},{8,24},{12,28},{16,0},{20,4},{24,8},{28,12},{1,17},{... | collective-permute-start | bytes 1572872 | tf_op jit(solution)/shard_map/ppermute | solution.py:24
  62.1 39.7 %collective-permute-start.12 = (bf16[64,2048]{1,0:T(8,128)(2,1)}, bf16[64,2048]{1,0:T(8,128)(2,1)S(1)}, u32[]{:S(2)}, u32[]{:S(2)}) collective-permute-start(bf16[64,2048]{1,0:T(8,128)(2,1)} %collective-permute-done.11), channel_id=1, source_target_pairs={{0,8},{4,12},{8,0},{12,4},{16,24},{20,28},{24,16},{28,20},{1,9},{5... | collective-permute-start | bytes 786440 | tf_op jit(solution)/shard_map/ppermute | solution.py:24
  87.0 46.0 %collective-permute-start.17 = (bf16[128,2048]{1,0:T(8,128)(2,1)}, bf16[128,2048]{1,0:T(8,128)(2,1)}, u32[]{:S(2)}, u32[]{:S(2)}) collective-permute-start(bf16[128,2048]{1,0:T(8,128)(2,1)} %constant_dynamic-update-slice_fusion.refs_0_), channel_id=1, source_target_pairs={{0,4},{4,0},{8,12},{12,8},{16,20},{20,16},{24,28},{28,24},{1,5},{5... | collective-permute-start | bytes 1572872 | tf_op jit(solution)/shard_map/ppermute | solution.py:24
  170.2 37.7 %collective-permute-start.25 = (bf16[256,2048]{1,0:T(8,128)(2,1)S(1)}, bf16[256,2048]{1,0:T(8,128)(2,1)S(1)}, u32[]{:S(2)}, u32[]{:S(2)}) collective-permute-start(bf16[256,2048]{1,0:T(8,128)(2,1)S(1)} %copy-done.66), channel_id=1, source_target_pairs={{0,4},{4,0},{8,12},{12,8},{16,20},{20,16},{24,28},{28,24},{1,5},{5... | collective-permute-start | bytes 3145736 | tf_op jit(solution)/shard_map/ppermute | solution.py:24
  177.8 31.8 %collective-permute-start.22 = (bf16[128,2048]{1,0:T(8,128)(2,1)S(1)}, bf16[128,2048]{1,0:T(8,128)(2,1)}, u32[]{:S(2)}, u32[]{:S(2)}) collective-permute-start(bf16[128,2048]{1,0:T(8,128)(2,1)S(1)} %get-tuple-element.156.refs_0_.refs_1_), channel_id=1, source_target_pairs={{0,2},{1,3},{2,0},{3,1},{4,6},{5,7},{6,4},{7,5},{8,10},{9,11},{10,... | collective-permute-start | bytes 1572872 | tf_op jit(solution)/shard_map/ppermute | solution.py:24
  310.3 39.3 %collective-permute-start.56 = (bf16[128,2048]{1,0:T(8,128)(2,1)S(1)}, bf16[128,2048]{1,0:T(8,128)(2,1)S(1)}, u32[]{:S(2)}, u32[]{:S(2)}) collective-permute-start(bf16[128,2048]{1,0:T(8,128)(2,1)S(1)} %get-tuple-element.275), channel_id=1, source_target_pairs={{0,8},{4,12},{8,0},{12,4},{16,24},{20,28},{24,16},{28,20},{1,9},{5... | collective-permute-start | bytes 1572872 | tf_op jit(solution)/shard_map/ppermute | solution.py:24
  317.2 32.0 %collective-permute-start.63 = (bf16[512,1024]{1,0:T(8,128)(2,1)S(1)}, bf16[512,1024]{1,0:T(8,128)(2,1)S(1)}, u32[]{:S(2)}, u32[]{:S(2)}) collective-permute-start(bf16[512,1024]{1,0:T(8,128)(2,1)S(1)} %shard_map.310), channel_id=1, source_target_pairs={{0,4},{4,0},{8,12},{12,8},{16,20},{20,16},{24,28},{28,24},{1,5},{5... | collective-permute-start | bytes 3145736 | tf_op jit(solution)/shard_map/ppermute | solution.py:24
  324.2 33.2 %collective-permute-start.59 = (bf16[128,2048]{1,0:T(8,128)(2,1)S(1)}, bf16[128,2048]{1,0:T(8,128)(2,1)S(1)}, u32[]{:S(2)}, u32[]{:S(2)}) collective-permute-start(bf16[128,2048]{1,0:T(8,128)(2,1)S(1)} %add_convert_fusion.18), channel_id=1, source_target_pairs={{0,16},{4,20},{8,24},{12,28},{16,0},{20,4},{24,8},{28,12},{1,17},{... | collective-permute-start | bytes 1572872 | tf_op jit(solution)/shard_map/ppermute | solution.py:24
  331.5 38.9 %collective-permute-start.62 = (bf16[128,2048]{1,0:T(8,128)(2,1)S(1)}, bf16[128,2048]{1,0:T(8,128)(2,1)S(1)}, u32[]{:S(2)}, u32[]{:S(2)}) collective-permute-start(bf16[128,2048]{1,0:T(8,128)(2,1)S(1)} %add_convert_fusion.15.refs_21_.refs_25_), channel_id=1, source_target_pairs={{0,24},{4,28},{8,16},{12,20},{16,8},{20,12},{24,0},{28,4},{1,25},{... | collective-permute-start | bytes 1572872 | tf_op jit(solution)/shard_map/ppermute | solution.py:24
  374.9 32.7 %collective-permute-start.64 = (bf16[1024,2048]{1,0:T(8,128)(2,1)S(1)}, bf16[1024,2048]{1,0:T(8,128)(2,1)S(1)}, u32[]{:S(2)}, u32[]{:S(2)}) collective-permute-start(bf16[1024,2048]{1,0:T(8,128)(2,1)S(1)} %convolution_convert_fusion), channel_id=1, source_target_pairs={{0,1},{1,0},{2,3},{3,2},{4,5},{5,4},{6,7},{7,6},{8,9},{9,8},{10,11... | collective-permute-start | bytes 12582920 | tf_op jit(solution)/shard_map/ppermute | solution.py:24
  377.0 62.7 %collective-permute-start.100 = (bf16[512,1024]{1,0:T(8,128)(2,1)}, bf16[512,1024]{1,0:T(8,128)(2,1)}, u32[]{:S(2)}, u32[]{:S(2)}) collective-permute-start(bf16[512,1024]{1,0:T(8,128)(2,1)} %shard_map.311), channel_id=1, source_target_pairs={{0,4},{4,0},{8,12},{12,8},{16,20},{20,16},{24,28},{28,24},{1,5},{5... | collective-permute-start | bytes 3145736 | tf_op jit(solution)/shard_map/ppermute | solution.py:24
  407.3 31.4 %collective-permute-start.73 = (f32[2,128,128]{2,1,0:T(8,128)S(1)}, f32[2,128,128]{2,1,0:T(8,128)S(1)}, u32[]{:S(2)}, u32[]{:S(2)}) collective-permute-start(f32[2,128,128]{2,1,0:T(8,128)S(1)} %get-tuple-element.205), channel_id=1, source_target_pairs={{0,4},{4,0},{8,12},{12,8},{16,20},{20,16},{24,28},{28,24},{1,5},{5... | collective-permute-start | bytes 393224 | tf_op jit(solution)/shard_map/ppermute | solution.py:24
  411.9 51.1 %collective-permute-start.66 = (bf16[2,128,2048]{2,1,0:T(8,128)(2,1)}, bf16[2,128,2048]{2,1,0:T(8,128)(2,1)}, u32[]{:S(2)}, u32[]{:S(2)}) collective-permute-start(bf16[2,128,2048]{2,1,0:T(8,128)(2,1)} %get-tuple-element.196), channel_id=1, source_target_pairs={{0,2},{1,3},{2,0},{3,1},{4,6},{5,7},{6,4},{7,5},{8,10},{9,11},{10,... | collective-permute-start | bytes 3145736 | tf_op jit(solution)/shard_map/ppermute | solution.py:24
  439.4 38.2 %collective-permute-start.97 = (bf16[256,2176]{1,0:T(8,128)(2,1)}, bf16[256,2176]{1,0:T(8,128)(2,1)}, u32[]{:S(2)}, u32[]{:S(2)}) collective-permute-start(bf16[256,2176]{1,0:T(8,128)(2,1)} %get-tuple-element.234.refs_9_), channel_id=1, source_target_pairs={{0,4},{4,0},{8,12},{12,8},{16,20},{20,16},{24,28},{28,24},{1,5},{5... | collective-permute-start | bytes 3342344 | tf_op jit(solution)/shard_map/ppermute | solution.py:24
  440.8 34.7 %collective-permute-start.75 = (f32[2,128,128]{2,1,0:T(8,128)S(1)}, f32[2,128,128]{2,1,0:T(8,128)S(1)}, u32[]{:S(2)}, u32[]{:S(2)}) collective-permute-start(f32[2,128,128]{2,1,0:T(8,128)S(1)} %add.198), channel_id=1, source_target_pairs={{0,8},{4,12},{8,0},{12,4},{16,24},{20,28},{24,16},{28,20},{1,9},{5... | collective-permute-start | bytes 393224 | tf_op jit(solution)/shard_map/ppermute | solution.py:24
  475.8 64.5 %collective-permute-start.101 = (bf16[256,1024]{1,0:T(8,128)(2,1)S(1)}, bf16[256,1024]{1,0:T(8,128)(2,1)S(1)}, u32[]{:S(2)}, u32[]{:S(2)}) collective-permute-start(bf16[256,1024]{1,0:T(8,128)(2,1)S(1)} %get-tuple-element.297), channel_id=1, source_target_pairs={{0,8},{4,12},{8,0},{12,4},{16,24},{20,28},{24,16},{28,20},{1,9},{5... | collective-permute-start | bytes 1572872 | tf_op jit(solution)/shard_map/ppermute | solution.py:24
  506.4 38.8 %collective-permute-start.68 = (bf16[256,2048]{1,0:T(8,128)(2,1)S(1)}, bf16[256,2048]{1,0:T(8,128)(2,1)S(1)}, u32[]{:S(2)}, u32[]{:S(2)}) collective-permute-start(bf16[256,2048]{1,0:T(8,128)(2,1)S(1)} %pad_maximum_fusion.2), channel_id=1, source_target_pairs={{0,8},{4,12},{8,0},{12,4},{16,24},{20,28},{24,16},{28,20},{1,9},{5... | collective-permute-start | bytes 3145736 | tf_op jit(solution)/shard_map/ppermute | solution.py:24
  524.2 104.5 %collective-permute-start.86 = (bf16[128,2048]{1,0:T(8,128)(2,1)S(1)}, bf16[128,2048]{1,0:T(8,128)(2,1)S(1)}, u32[]{:S(2)}, u32[]{:S(2)}) collective-permute-start(bf16[128,2048]{1,0:T(8,128)(2,1)S(1)} %shard_map.325.refs_1_.refs_9_.refs_5_), channel_id=1, source_target_pairs={{0,1},{1,0},{2,3},{3,2},{4,5},{5,4},{6,7},{7,6},{8,9},{9,8},{10,11... | collective-permute-start | bytes 1572872 | tf_op jit(solution)/shard_map/ppermute | solution.py:24
  526.9 87.8 %collective-permute-start.85 = (bf16[128,2048]{1,0:T(8,128)(2,1)S(1)}, bf16[128,2048]{1,0:T(8,128)(2,1)S(1)}, u32[]{:S(2)}, u32[]{:S(2)}) collective-permute-start(bf16[128,2048]{1,0:T(8,128)(2,1)S(1)} %shard_map.325.refs_1_.refs_9_.refs_5_), channel_id=1, source_target_pairs={{0,2},{1,3},{2,0},{3,1},{4,6},{5,7},{6,4},{7,5},{8,10},{9,11},{10,... | collective-permute-start | bytes 1572872 | tf_op jit(solution)/shard_map/ppermute | solution.py:24
  545.2 33.5 %collective-permute-start.95 = (bf16[256,768]{1,0:T(8,128)(2,1)}, bf16[256,768]{1,0:T(8,128)(2,1)}, u32[]{:S(2)}, u32[]{:S(2)}) collective-permute-start(bf16[256,768]{1,0:T(8,128)(2,1)} %slice.348), channel_id=1, source_target_pairs={{0,8},{4,12},{8,0},{12,4},{16,24},{20,28},{24,16},{28,20},{1,9},{5... | collective-permute-start | bytes 1179656 | tf_op jit(solution)/shard_map/ppermute | solution.py:24
  559.5 66.5 %collective-permute-start.94 = (bf16[256,768]{1,0:T(8,128)(2,1)}, bf16[256,768]{1,0:T(8,128)(2,1)}, u32[]{:S(2)}, u32[]{:S(2)}) collective-permute-start(bf16[256,768]{1,0:T(8,128)(2,1)} %slice.346), channel_id=1, source_target_pairs={{0,8},{4,12},{8,0},{12,4},{16,24},{20,28},{24,16},{28,20},{1,9},{5... | collective-permute-start | bytes 1179656 | tf_op jit(solution)/shard_map/ppermute | solution.py:24
  578.7 31.4 %collective-permute-start.81 = (bf16[128,2048]{1,0:T(8,128)(2,1)}, bf16[128,2048]{1,0:T(8,128)(2,1)S(1)}, u32[]{:S(2)}, u32[]{:S(2)}) collective-permute-start(bf16[128,2048]{1,0:T(8,128)(2,1)} %fusion.2), channel_id=1, source_target_pairs={{0,16},{4,20},{8,24},{12,28},{16,0},{20,4},{24,8},{28,12},{1,17},{... | collective-permute-start | bytes 1572872 | tf_op jit(solution)/shard_map/ppermute | solution.py:24
  581.5 44.5 %collective-permute-start.96 = (bf16[256,768]{1,0:T(8,128)(2,1)S(1)}, bf16[256,768]{1,0:T(8,128)(2,1)S(1)}, u32[]{:S(2)}, u32[]{:S(2)}) collective-permute-start(bf16[256,768]{1,0:T(8,128)(2,1)S(1)} %add_convert_fusion.27), channel_id=1, source_target_pairs={{0,16},{4,20},{8,24},{12,28},{16,0},{20,4},{24,8},{28,12},{1,17},{... | collective-permute-start | bytes 1179656 | tf_op jit(solution)/shard_map/ppermute | solution.py:24
  (203 other events, 2563.9 us)

commit v3 on v2

--- a/solution.py
+++ b/solution.py
@@ -864,7 +864,7 @@
         residual_norm,
         [shape((chunk, width), f32), shape((chunk, width), bf16), shape((chunk, LANES), bf16)],
         [near, other, own_x, vecs],
-        deps=[gu_got[3]],
+        deps=[gu_mid[-1]],
     )
 
     n_got = [normed_two, None, None, None]
@@ -970,7 +970,7 @@
     down_other = trade(down_send, "kv", 1)
     gate_parts = [near_cols[:depth], None, None, None]
     gate_parts[2] = trade(far_cols[:depth], SEQ, rings[2])
-    gate_parts[3] = trade(after(far_cols[depth:], all_branch[1]), SEQ, rings[3])
+    gate_parts[3] = trade(far_cols[depth:], SEQ, rings[3])
     results = own_call(
         functools.partial(attended_back, size=head_size, kv_heads=kv_heads),
         [shape((length, group * wide_size), bf16)] * kv_heads
@@ -1013,12 +1013,13 @@
             ],
             [here, query, kv_ext, fq_w, key_feat, feats[k], grad_tops[k], states],
             1,
-            deps=list(step) + ([high, gate_parts[3]] if k else [side, out_send, down_sum, gate_parts[2]]),
+            deps=list(step) + ([high] if k else [side, out_send, down_sum]),
         )
 
     later, local, steps = running(grad_state, -1, [functools.partial(attend_back, k) for k in range(kv_heads)])
     gate_parts[1] = trade(near_cols[depth:], SEQ, rings[1])
     low = trade(after(side[:2], high), "kv", 2)
+    low_first = low
     high = add_low(near[2:], high)
     low = add_low(near[:2], low)
     out_sum = across_sum([out_keep] + [after(p, steps[0]) for p in out_parts[1:]], local[0][0])
@@ -1033,6 +1034,7 @@
             shape((kv_heads, head_size, head_size), f32),
         ],
         [kv_ext, fk_w, key_feat, later] + [l[1] for l in local] + [l[2] for l in local] + [l[3] for l in local],
+        deps=[low_first],
     )
     returned = moved(halo_back, SEQ, -1)
 
@@ -1105,7 +1107,7 @@
         [jnp.stack([along ^ d for d in range(RING)]).astype(jnp.int32)]
         + gate_parts,
         1,
-        deps=[own_grad],
+        deps=[qkv_low],
     )
 
     small = small[0]

time: 640 us -> 606 us (0.947)
  waiting for transfers between devices: 292 us -> 260 us
    ppermute x100, waiting for transfers between devices: 291 us -> 257 us  [trade(): return lax.ppermute(array, axis, [(i, i ^ mask) for i in range(count)])]
  transfers between devices with their start and end apart: 102 -> 102, of which waited for: 38 -> 37; matrix products, arithmetic and copies ran while one was open for 8% -> 8% of each run, Pallas kernels for 20% -> 22%
where the time goes in v3:
time: 606 us; the launch traced here: 598 us
  waiting for transfers between devices  260 us (43%)
  Pallas kernels  138 us (23%)
  starting transfers between devices  109 us (18%)
  local copies, waits for them, and re-layouts  56.8 us (9%)
  other arithmetic  25.7 us (4%)
    ppermute x100, waiting for transfers between devices, trade(): return lax.ppermute(array, axis, [(i, i ^ mask) for i in range(count)])  257 us
    pallas_call x31, Pallas kernels, own_call(): pl.pallas_call(run, out_shape=tuple(outs), in_specs=[smem] * scalars + [v...  130 us
    ppermute x100, starting transfers between devices, trade(): return lax.ppermute(array, axis, [(i, i ^ mask) for i in range(count)])  104 us
    unnamed x254, local copies, waits for them, and re-layouts  39.9 us
    convert_element_type x25, other arithmetic, add_low(): return (a.astype(f32) + b.astype(f32)).astype(bf16)  13.5 us
  transfers between devices with their start and end apart: 102, of which 37 were waited for; matrix products, arithmetic and copies ran while one was open for 8% of the time, Pallas kernels for 22%

profile of v3, /device:TPU:9, one launch (start us, length us, event | category | flops | bytes accessed | tf_op | source)
XLA Modules:
  0.0 597.9 jit_solution(12404523307242764709)
XLA Ops:
  16.7 14.8 %collective-permute-done.2.refs_2_ = bf16[256,896]{1,0:T(8,128)(2,1)S(1)} collective-permute-done((bf16[256,896]{1,0:T(8,128)(2,1)S(1)}, bf16[256,896]{1,0:T(8,128)(2,1)S(1)}, u32[]{:S(2)}, u32[]{:S(2)}) %collective-permute-start.2) | collective-permute-done | bytes 458784 | tf_op jit(solution)/shard_map/ppermute | solution.py:24
  38.1 10.4 %collective-permute-done.3.refs_3_ = bf16[256,896]{1,0:T(8,128)(2,1)} collective-permute-done((bf16[256,896]{1,0:T(8,128)(2,1)S(1)}, bf16[256,896]{1,0:T(8,128)(2,1)}, u32[]{:S(2)}, u32[]{:S(2)}) %collective-permute-start.3) | collective-permute-done | bytes 458784 | tf_op jit(solution)/shard_map/ppermute | solution.py:24
  67.1 19.9 %collective-permute-done.7.refs_7_ = bf16[256,896]{1,0:T(8,128)(2,1)S(1)} collective-permute-done((bf16[256,896]{1,0:T(8,128)(2,1)}, bf16[256,896]{1,0:T(8,128)(2,1)S(1)}, u32[]{:S(2)}, u32[]{:S(2)}) %collective-permute-start.7) | collective-permute-done | bytes 458784 | tf_op jit(solution)/shard_map/ppermute | solution.py:24
  107.2 9.3 %collective-permute-done.10.refs_5_ = f32[2,128,128]{2,1,0:T(8,128)S(1)} collective-permute-done((f32[2,128,128]{2,1,0:T(8,128)S(1)}, f32[2,128,128]{2,1,0:T(8,128)S(1)}, u32[]{:S(2)}, u32[]{:S(2)}) %collective-permute-start.10) | collective-permute-done | bytes 131104 | tf_op jit(solution)/shard_map/ppermute | solution.py:24
  124.4 10.8 %shard_map.300 = (f32[512,512]{1,0:T(8,128)S(1)}, f32[512,512]{1,0:T(8,128)S(1)}, bf16[512,512]{1,0:T(8,128)(2,1)S(1)}, bf16[512,512]{1,0:T(8,128)(2,1)S(1)}) custom-call(s32[1]{0:T(128)} %bitcast.4.refs_0_, bf16[512,512]{1,0:T(8,128)(2,1)S(1)} %get-tuple-element.133.refs_1_, bf16[576,256]{1,0:T(8,128)(2,1)S(1)} %get-tuple-element.134.refs_2_.refs_0_, ...), custom_call_target="tpu_custom_call" | custom-call | tf_op jit(solution)/shard_map/pallas_call | solution.py:66
  152.8 19.4 %collective-permute-done.21.refs_4_.refs_3_ = bf16[512,1024]{1,0:T(8,128)(2,1)S(1)} collective-permute-done((bf16[512,1024]{1,0:T(8,128)(2,1)S(1)}, bf16[512,1024]{1,0:T(8,128)(2,1)S(1)}, u32[]{:S(2)}, u32[]{:S(2)}) %collective-permute-start.21) | collective-permute-done | bytes 1048608 | tf_op jit(solution)/shard_map/ppermute | solution.py:24
  179.2 7.1 %collective-permute-done.33.refs_5_.refs_14_ = bf16[128,2048]{1,0:T(8,128)(2,1)} collective-permute-done((bf16[128,2048]{1,0:T(8,128)(2,1)}, bf16[128,2048]{1,0:T(8,128)(2,1)}, u32[]{:S(2)}, u32[]{:S(2)}) %collective-permute-start.33) | collective-permute-done | bytes 524320 | tf_op jit(solution)/shard_map/ppermute | solution.py:24
  190.5 16.4 %collective-permute-done.26.refs_5_ = bf16[256,1024]{1,0:T(8,128)(2,1)S(1)} collective-permute-done((bf16[256,1024]{1,0:T(8,128)(2,1)S(1)}, bf16[256,1024]{1,0:T(8,128)(2,1)S(1)}, u32[]{:S(2)}, u32[]{:S(2)}) %collective-permute-start.26) | collective-permute-done | bytes 524320 | tf_op jit(solution)/shard_map/ppermute | solution.py:24
  227.4 7.3 %shard_map.306 = (bf16[256,2048]{1,0:T(8,128)(2,1)S(1)}, bf16[256,2048]{1,0:T(8,128)(2,1)S(1)}, bf16[256,512]{1,0:T(8,128)(2,1)S(1)}, bf16[256,512]{1,0:T(8,128)(2,1)S(1)}, bf16[512,1024]{1,0:T(8,128)(2,1)S(1)}) custom-call(bf16[128,2048]{1,0:T(8,128)(2,1)S(1)} %copy-done.5, bf16[128,2048]{1,0:T(8,128)(2,1)} %collective-permute-done.22.refs_1_.refs_2_, ...), custom_call_target="tpu_custom_call" | custom-call | tf_op jit(solution)/shard_map/pallas_call | solution.py:66
  240.0 7.5 %shard_map.307 = (bf16[256,2048]{1,0:T(8,128)(2,1)S(1)}, bf16[256,2048]{1,0:T(8,128)(2,1)S(1)}, bf16[256,512]{1,0:T(8,128)(2,1)S(1)}, bf16[256,512]{1,0:T(8,128)(2,1)S(1)}, bf16[512,1024]{1,0:T(8,128)(2,1)S(1)}) custom-call(bf16[128,2048]{1,0:T(8,128)(2,1)S(1)} %copy-done.7, bf16[128,2048]{1,0:T(8,128)(2,1)S(1)} %copy-done.9, ...), custom_call_target="tpu_custom_call" | custom-call | tf_op jit(solution)/shard_map/pallas_call | solution.py:66
  253.2 10.2 %collective-permute-done.49.refs_4_.refs_21_ = bf16[128,2048]{1,0:T(8,128)(2,1)S(1)} collective-permute-done((bf16[128,2048]{1,0:T(8,128)(2,1)}, bf16[128,2048]{1,0:T(8,128)(2,1)S(1)}, u32[]{:S(2)}, u32[]{:S(2)}) %collective-permute-start.49) | collective-permute-done | bytes 524320 | tf_op jit(solution)/shard_map/ppermute | solution.py:24
  267.7 10.2 %collective-permute-done.50.refs_5_.refs_22_ = bf16[128,2048]{1,0:T(8,128)(2,1)S(1)} collective-permute-done((bf16[128,2048]{1,0:T(8,128)(2,1)S(1)}, bf16[128,2048]{1,0:T(8,128)(2,1)S(1)}, u32[]{:S(2)}, u32[]{:S(2)}) %collective-permute-start.50) | collective-permute-done | bytes 524320 | tf_op jit(solution)/shard_map/ppermute | solution.py:24
  280.9 8.2 %collective-permute-done.54 = bf16[128,2048]{1,0:T(8,128)(2,1)S(1)} collective-permute-done((bf16[128,2048]{1,0:T(8,128)(2,1)S(1)}, bf16[128,2048]{1,0:T(8,128)(2,1)S(1)}, u32[]{:S(2)}, u32[]{:S(2)}) %collective-permute-start.54) | collective-permute-done | bytes 524320 | tf_op jit(solution)/shard_map/ppermute | solution.py:24
  290.4 7.1 %shard_map.308 = (bf16[256,2048]{1,0:T(8,128)(2,1)S(1)}, bf16[256,2048]{1,0:T(8,128)(2,1)S(1)}, bf16[256,512]{1,0:T(8,128)(2,1)S(1)}, bf16[256,512]{1,0:T(8,128)(2,1)S(1)}, bf16[512,1024]{1,0:T(8,128)(2,1)S(1)}) custom-call(bf16[128,2048]{1,0:T(8,128)(2,1)} %collective-permute-done.36.refs_0_.refs_9_, ...), custom_call_target="tpu_custom_call" | custom-call | tf_op jit(solution)/shard_map/pallas_call | solution.py:66
  324.5 7.1 %collective-permute-done.61 = bf16[128,2048]{1,0:T(8,128)(2,1)S(1)} collective-permute-done((bf16[128,2048]{1,0:T(8,128)(2,1)S(1)}, bf16[128,2048]{1,0:T(8,128)(2,1)S(1)}, u32[]{:S(2)}, u32[]{:S(2)}) %collective-permute-start.61) | collective-permute-done | bytes 524320 | tf_op jit(solution)/shard_map/ppermute | solution.py:24
  350.4 7.0 %collective-permute-done.59.refs_2_ = bf16[128,2048]{1,0:T(8,128)(2,1)S(1)} collective-permute-done((bf16[128,2048]{1,0:T(8,128)(2,1)S(1)}, bf16[128,2048]{1,0:T(8,128)(2,1)S(1)}, u32[]{:S(2)}, u32[]{:S(2)}) %collective-permute-start.59) | collective-permute-done | bytes 524320 | tf_op jit(solution)/shard_map/ppermute | solution.py:24
  357.4 12.9 %collective-permute-done.62.refs_3_ = bf16[128,2048]{1,0:T(8,128)(2,1)S(1)} collective-permute-done((bf16[128,2048]{1,0:T(8,128)(2,1)S(1)}, bf16[128,2048]{1,0:T(8,128)(2,1)S(1)}, u32[]{:S(2)}, u32[]{:S(2)}) %collective-permute-start.62) | collective-permute-done | bytes 524320 | tf_op jit(solution)/shard_map/ppermute | solution.py:24
  379.9 11.3 %collective-permute-done.65.refs_2_ = bf16[128,2048]{1,0:T(8,128)(2,1)S(1)} collective-permute-done((bf16[128,2048]{1,0:T(8,128)(2,1)S(1)}, bf16[128,2048]{1,0:T(8,128)(2,1)S(1)}, u32[]{:S(2)}, u32[]{:S(2)}) %collective-permute-start.65) | collective-permute-done | bytes 524320 | tf_op jit(solution)/shard_map/ppermute | solution.py:24
  418.9 12.3 %shard_map.319 = (bf16[512,256]{1,0:T(8,128)(2,1)S(1)}, f32[576,64]{1,0:T(8,128)S(1)}, f32[576,128]{1,0:T(8,128)S(1)}, f32[512,128]{1,0:T(8,128)S(1)}, f32[4,64,64]{2,1,0:T(8,128)S(1)}) custom-call(s32[1]{0:T(128)} %bitcast.4.refs_0_, bf16[512,512]{1,0:T(8,128)(2,1)S(1)} %copy-done.26, bf16[576,256]{1,0:T(8,128)(2,1)S(1)} %get-tuple-element.134.refs_2_.refs_0_, ...), custom_call_target="tpu_custom_call" | custom-call | tf_op jit(solution)/shard_map/pallas_call | solution.py:66
  440.2 12.5 %shard_map.320 = (bf16[512,256]{1,0:T(8,128)(2,1)S(1)}, f32[576,64]{1,0:T(8,128)S(1)}, f32[576,128]{1,0:T(8,128)S(1)}, f32[512,128]{1,0:T(8,128)S(1)}, f32[4,64,64]{2,1,0:T(8,128)S(1)}) custom-call(s32[1]{0:T(128)} %bitcast.4.refs_0_, bf16[512,512]{1,0:T(8,128)(2,1)S(1)} %copy-done.27, bf16[576,256]{1,0:T(8,128)(2,1)S(1)} %get-tuple-element.134.refs_2_.refs_0_, ...), custom_call_target="tpu_custom_call" | custom-call | tf_op jit(solution)/shard_map/pallas_call | solution.py:66
  486.4 14.2 %collective-permute-done.78 = bf16[512,768]{1,0:T(8,128)(2,1)S(1)} collective-permute-done((bf16[512,768]{1,0:T(8,128)(2,1)S(1)}, bf16[512,768]{1,0:T(8,128)(2,1)S(1)}, u32[]{:S(2)}, u32[]{:S(2)}) %collective-permute-start.78) | collective-permute-done | bytes 786464 | tf_op jit(solution)/shard_map/ppermute | solution.py:24
  512.3 8.7 %collective-permute-done.91 = bf16[512,768]{1,0:T(8,128)(2,1)S(1)} collective-permute-done((bf16[512,768]{1,0:T(8,128)(2,1)S(1)}, bf16[512,768]{1,0:T(8,128)(2,1)S(1)}, u32[]{:S(2)}, u32[]{:S(2)}) %collective-permute-start.91) | collective-permute-done | bytes 786464 | tf_op jit(solution)/shard_map/ppermute | solution.py:24
  543.5 17.5 %collective-permute-done.88 = bf16[1,208,128]{2,1,0:T(8,128)(2,1)S(1)} collective-permute-done((bf16[1,208,128]{2,1,0:T(8,128)(2,1)S(1)}, bf16[1,208,128]{2,1,0:T(8,128)(2,1)S(1)}, u32[]{:S(2)}, u32[]{:S(2)}) %collective-permute-start.88) | collective-permute-done | bytes 53280 | tf_op jit(solution)/shard_map/ppermute | solution.py:24
  578.9 8.4 %collective-permute-done.80.refs_2_ = bf16[128,2048]{1,0:T(8,128)(2,1)S(1)} collective-permute-done((bf16[128,2048]{1,0:T(8,128)(2,1)S(1)}, bf16[128,2048]{1,0:T(8,128)(2,1)S(1)}, u32[]{:S(2)}, u32[]{:S(2)}) %collective-permute-start.80) | collective-permute-done | bytes 524320 | tf_op jit(solution)/shard_map/ppermute | solution.py:24
  (550 shorter events, 324.8 us)
Async XLA Ops:
  55.2 32.1 %collective-permute-start.8 = (bf16[256,1024]{1,0:T(8,128)(2,1)}, bf16[256,1024]{1,0:T(8,128)(2,1)S(1)}, u32[]{:S(2)}, u32[]{:S(2)}) collective-permute-start(bf16[256,1024]{1,0:T(8,128)(2,1)} %get-tuple-element.158.refs_0_), channel_id=1, source_target_pairs={{0,4},{4,0},{8,12},{12,8},{16,20},{20,16},{24,28},{28,24},{1,5},{5... | collective-permute-start | bytes 1572872 | tf_op jit(solution)/shard_map/ppermute | solution.py:24
  57.0 30.4 %collective-permute-start.5 = (bf16[256,896]{1,0:T(8,128)(2,1)}, bf16[256,896]{1,0:T(8,128)(2,1)S(1)}, u32[]{:S(2)}, u32[]{:S(2)}) collective-permute-start(bf16[256,896]{1,0:T(8,128)(2,1)} %collective-permute-done.4.refs_4_), channel_id=1, source_target_pairs={{0,4},{4,0},{8,12},{12,8},{16,20},{20,16},{24,28},{28,24},{1,5},{5... | collective-permute-start | bytes 1376264 | tf_op jit(solution)/shard_map/ppermute | solution.py:24
  62.1 60.4 %collective-permute-start.15 = (bf16[256,1024]{1,0:T(8,128)(2,1)}, bf16[256,1024]{1,0:T(8,128)(2,1)}, u32[]{:S(2)}, u32[]{:S(2)}) collective-permute-start(bf16[256,1024]{1,0:T(8,128)(2,1)} %copy-done.118), channel_id=1, source_target_pairs={{0,16},{4,20},{8,24},{12,28},{16,0},{20,4},{24,8},{28,12},{1,17},{... | collective-permute-start | bytes 1572872 | tf_op jit(solution)/shard_map/ppermute | solution.py:24
  62.1 40.9 %collective-permute-start.12 = (bf16[64,2048]{1,0:T(8,128)(2,1)}, bf16[64,2048]{1,0:T(8,128)(2,1)S(1)}, u32[]{:S(2)}, u32[]{:S(2)}) collective-permute-start(bf16[64,2048]{1,0:T(8,128)(2,1)} %collective-permute-done.11), channel_id=1, source_target_pairs={{0,8},{4,12},{8,0},{12,4},{16,24},{20,28},{24,16},{28,20},{1,9},{5... | collective-permute-start | bytes 786440 | tf_op jit(solution)/shard_map/ppermute | solution.py:24
  87.0 48.1 %collective-permute-start.17 = (bf16[128,2048]{1,0:T(8,128)(2,1)}, bf16[128,2048]{1,0:T(8,128)(2,1)}, u32[]{:S(2)}, u32[]{:S(2)}) collective-permute-start(bf16[128,2048]{1,0:T(8,128)(2,1)} %constant_dynamic-update-slice_fusion.refs_0_), channel_id=1, source_target_pairs={{0,4},{4,0},{8,12},{12,8},{16,20},{20,16},{24,28},{28,24},{1,5},{5... | collective-permute-start | bytes 1572872 | tf_op jit(solution)/shard_map/ppermute | solution.py:24
  105.6 29.6 %collective-permute-start.18 = (bf16[128,2048]{1,0:T(8,128)(2,1)}, bf16[128,2048]{1,0:T(8,128)(2,1)}, u32[]{:S(2)}, u32[]{:S(2)}) collective-permute-start(bf16[128,2048]{1,0:T(8,128)(2,1)} %constant_dynamic-update-slice_fusion.2.refs_2_), channel_id=1, source_target_pairs={{0,4},{4,0},{8,12},{12,8},{16,20},{20,16},{24,28},{28,24},{1,5},{5... | collective-permute-start | bytes 1572872 | tf_op jit(solution)/shard_map/ppermute | solution.py:24
  172.2 37.6 %collective-permute-start.24 = (bf16[256,2048]{1,0:T(8,128)(2,1)S(1)}, bf16[256,2048]{1,0:T(8,128)(2,1)S(1)}, u32[]{:S(2)}, u32[]{:S(2)}) collective-permute-start(bf16[256,2048]{1,0:T(8,128)(2,1)S(1)} %copy-done.66), channel_id=1, source_target_pairs={{0,4},{4,0},{8,12},{12,8},{16,20},{20,16},{24,28},{28,24},{1,5},{5... | collective-permute-start | bytes 3145736 | tf_op jit(solution)/shard_map/ppermute | solution.py:24
  176.9 30.0 %collective-permute-start.26 = (bf16[256,1024]{1,0:T(8,128)(2,1)S(1)}, bf16[256,1024]{1,0:T(8,128)(2,1)S(1)}, u32[]{:S(2)}, u32[]{:S(2)}) collective-permute-start(bf16[256,1024]{1,0:T(8,128)(2,1)S(1)} %collective-permute-done.25.refs_4_), channel_id=1, source_target_pairs={{0,4},{4,0},{8,12},{12,8},{16,20},{20,16},{24,28},{28,24},{1,5},{5... | collective-permute-start | bytes 1572872 | tf_op jit(solution)/shard_map/ppermute | solution.py:24
  179.0 32.7 %collective-permute-start.22 = (bf16[128,2048]{1,0:T(8,128)(2,1)S(1)}, bf16[128,2048]{1,0:T(8,128)(2,1)}, u32[]{:S(2)}, u32[]{:S(2)}) collective-permute-start(bf16[128,2048]{1,0:T(8,128)(2,1)S(1)} %get-tuple-element.153.refs_0_.refs_1_), channel_id=1, source_target_pairs={{0,2},{1,3},{2,0},{3,1},{4,6},{5,7},{6,4},{7,5},{8,10},{9,11},{10,... | collective-permute-start | bytes 1572872 | tf_op jit(solution)/shard_map/ppermute | solution.py:24
  234.7 29.4 %collective-permute-start.45 = (bf16[256,2048]{1,0:T(8,128)(2,1)S(1)}, bf16[256,2048]{1,0:T(8,128)(2,1)S(1)}, u32[]{:S(2)}, u32[]{:S(2)}) collective-permute-start(bf16[256,2048]{1,0:T(8,128)(2,1)S(1)} %get-tuple-element.172), channel_id=1, source_target_pairs={{0,1},{1,0},{2,3},{3,2},{4,5},{5,4},{6,7},{7,6},{8,9},{9,8},{10,11... | collective-permute-start | bytes 3145736 | tf_op jit(solution)/shard_map/ppermute | solution.py:24
  311.4 39.0 %collective-permute-start.56 = (bf16[128,2048]{1,0:T(8,128)(2,1)S(1)}, bf16[128,2048]{1,0:T(8,128)(2,1)S(1)}, u32[]{:S(2)}, u32[]{:S(2)}) collective-permute-start(bf16[128,2048]{1,0:T(8,128)(2,1)S(1)} %get-tuple-element.273), channel_id=1, source_target_pairs={{0,8},{4,12},{8,0},{12,4},{16,24},{20,28},{24,16},{28,20},{1,9},{5... | collective-permute-start | bytes 1572872 | tf_op jit(solution)/shard_map/ppermute | solution.py:24
  317.3 32.7 %collective-permute-start.63 = (bf16[512,1024]{1,0:T(8,128)(2,1)S(1)}, bf16[512,1024]{1,0:T(8,128)(2,1)S(1)}, u32[]{:S(2)}, u32[]{:S(2)}) collective-permute-start(bf16[512,1024]{1,0:T(8,128)(2,1)S(1)} %shard_map.310), channel_id=1, source_target_pairs={{0,4},{4,0},{8,12},{12,8},{16,20},{20,16},{24,28},{28,24},{1,5},{5... | collective-permute-start | bytes 3145736 | tf_op jit(solution)/shard_map/ppermute | solution.py:24
  324.2 33.2 %collective-permute-start.59 = (bf16[128,2048]{1,0:T(8,128)(2,1)S(1)}, bf16[128,2048]{1,0:T(8,128)(2,1)S(1)}, u32[]{:S(2)}, u32[]{:S(2)}) collective-permute-start(bf16[128,2048]{1,0:T(8,128)(2,1)S(1)} %add_convert_fusion.18), channel_id=1, source_target_pairs={{0,16},{4,20},{8,24},{12,28},{16,0},{20,4},{24,8},{28,12},{1,17},{... | collective-permute-start | bytes 1572872 | tf_op jit(solution)/shard_map/ppermute | solution.py:24
  331.7 38.6 %collective-permute-start.62 = (bf16[128,2048]{1,0:T(8,128)(2,1)S(1)}, bf16[128,2048]{1,0:T(8,128)(2,1)S(1)}, u32[]{:S(2)}, u32[]{:S(2)}) collective-permute-start(bf16[128,2048]{1,0:T(8,128)(2,1)S(1)} %add_convert_fusion.15.refs_21_.refs_25_), channel_id=1, source_target_pairs={{0,24},{4,28},{8,16},{12,20},{16,8},{20,12},{24,0},{28,4},{1,25},{... | collective-permute-start | bytes 1572872 | tf_op jit(solution)/shard_map/ppermute | solution.py:24
  376.0 33.0 %collective-permute-start.64 = (bf16[1024,2048]{1,0:T(8,128)(2,1)S(1)}, bf16[1024,2048]{1,0:T(8,128)(2,1)S(1)}, u32[]{:S(2)}, u32[]{:S(2)}) collective-permute-start(bf16[1024,2048]{1,0:T(8,128)(2,1)S(1)} %convolution_convert_fusion), channel_id=1, source_target_pairs={{0,1},{1,0},{2,3},{3,2},{4,5},{5,4},{6,7},{7,6},{8,9},{9,8},{10,11... | collective-permute-start | bytes 12582920 | tf_op jit(solution)/shard_map/ppermute | solution.py:24
  392.4 44.3 %collective-permute-start.98 = (bf16[512,1024]{1,0:T(8,128)(2,1)}, bf16[512,1024]{1,0:T(8,128)(2,1)}, u32[]{:S(2)}, u32[]{:S(2)}) collective-permute-start(bf16[512,1024]{1,0:T(8,128)(2,1)} %shard_map.311), channel_id=1, source_target_pairs={{0,4},{4,0},{8,12},{12,8},{16,20},{20,16},{24,28},{28,24},{1,5},{5... | collective-permute-start | bytes 3145736 | tf_op jit(solution)/shard_map/ppermute | solution.py:24
  436.1 91.6 %collective-permute-start.101 = (bf16[256,1024]{1,0:T(8,128)(2,1)S(1)}, bf16[256,1024]{1,0:T(8,128)(2,1)S(1)}, u32[]{:S(2)}, u32[]{:S(2)}) collective-permute-start(bf16[256,1024]{1,0:T(8,128)(2,1)S(1)} %get-tuple-element.295), channel_id=1, source_target_pairs={{0,24},{4,28},{8,16},{12,20},{16,8},{20,12},{24,0},{28,4},{1,25},{... | collective-permute-start | bytes 1572872 | tf_op jit(solution)/shard_map/ppermute | solution.py:24
  465.8 37.8 %collective-permute-start.96 = (bf16[128,2176]{1,0:T(8,128)(2,1)S(1)}, bf16[128,2176]{1,0:T(8,128)(2,1)S(1)}, u32[]{:S(2)}, u32[]{:S(2)}) collective-permute-start(bf16[128,2176]{1,0:T(8,128)(2,1)S(1)} %get-tuple-element.294), channel_id=1, source_target_pairs={{0,8},{4,12},{8,0},{12,4},{16,24},{20,28},{24,16},{28,20},{1,9},{5... | collective-permute-start | bytes 1671176 | tf_op jit(solution)/shard_map/ppermute | solution.py:24
  500.6 30.1 %collective-permute-start.100 = (bf16[256,1024]{1,0:T(8,128)(2,1)S(1)}, bf16[256,1024]{1,0:T(8,128)(2,1)S(1)}, u32[]{:S(2)}, u32[]{:S(2)}) collective-permute-start(bf16[256,1024]{1,0:T(8,128)(2,1)S(1)} %get-tuple-element.296), channel_id=1, source_target_pairs={{0,16},{4,20},{8,24},{12,28},{16,0},{20,4},{24,8},{28,12},{1,17},{... | collective-permute-start | bytes 1572872 | tf_op jit(solution)/shard_map/ppermute | solution.py:24
  501.6 32.1 %collective-permute-start.99 = (bf16[256,1024]{1,0:T(8,128)(2,1)S(1)}, bf16[256,1024]{1,0:T(8,128)(2,1)S(1)}, u32[]{:S(2)}, u32[]{:S(2)}) collective-permute-start(bf16[256,1024]{1,0:T(8,128)(2,1)S(1)} %get-tuple-element.297), channel_id=1, source_target_pairs={{0,8},{4,12},{8,0},{12,4},{16,24},{20,28},{24,16},{28,20},{1,9},{5... | collective-permute-start | bytes 1572872 | tf_op jit(solution)/shard_map/ppermute | solution.py:24
  527.7 63.8 %collective-permute-start.84 = (bf16[128,2048]{1,0:T(8,128)(2,1)S(1)}, bf16[128,2048]{1,0:T(8,128)(2,1)}, u32[]{:S(2)}, u32[]{:S(2)}) collective-permute-start(bf16[128,2048]{1,0:T(8,128)(2,1)S(1)} %shard_map.325.refs_1_.refs_9_), channel_id=1, source_target_pairs={{0,1},{1,0},{2,3},{3,2},{4,5},{5,4},{6,7},{7,6},{8,9},{9,8},{10,11... | collective-permute-start | bytes 1572872 | tf_op jit(solution)/shard_map/ppermute | solution.py:24
  530.6 46.5 %collective-permute-start.83 = (bf16[128,2048]{1,0:T(8,128)(2,1)S(1)}, bf16[128,2048]{1,0:T(8,128)(2,1)}, u32[]{:S(2)}, u32[]{:S(2)}) collective-permute-start(bf16[128,2048]{1,0:T(8,128)(2,1)S(1)} %shard_map.325.refs_1_.refs_9_), channel_id=1, source_target_pairs={{0,2},{1,3},{2,0},{3,1},{4,6},{5,7},{6,4},{7,5},{8,10},{9,11},{10,... | collective-permute-start | bytes 1572872 | tf_op jit(solution)/shard_map/ppermute | solution.py:24
  533.7 36.9 %collective-permute-start.93 = (bf16[256,768]{1,0:T(8,128)(2,1)}, bf16[256,768]{1,0:T(8,128)(2,1)}, u32[]{:S(2)}, u32[]{:S(2)}) collective-permute-start(bf16[256,768]{1,0:T(8,128)(2,1)} %slice.346), channel_id=1, source_target_pairs={{0,8},{4,12},{8,0},{12,4},{16,24},{20,28},{24,16},{28,20},{1,9},{5... | collective-permute-start | bytes 1179656 | tf_op jit(solution)/shard_map/ppermute | solution.py:24
  538.8 34.9 %collective-permute-start.79 = (bf16[128,2048]{1,0:T(8,128)(2,1)}, bf16[128,2048]{1,0:T(8,128)(2,1)}, u32[]{:S(2)}, u32[]{:S(2)}) collective-permute-start(bf16[128,2048]{1,0:T(8,128)(2,1)} %fusion.2), channel_id=1, source_target_pairs={{0,16},{4,20},{8,24},{12,28},{16,0},{20,4},{24,8},{28,12},{1,17},{... | collective-permute-start | bytes 1572872 | tf_op jit(solution)/shard_map/ppermute | solution.py:24
  (203 other events, 2370.4 us)
